TPU v7x, 512 devices: a whole 4x4x16 slice. The times are simulated.
512 devices in a mesh: dp: 128 (over z, x, core), mp: 4 (over y).
Axes of the slice: x: 4, y: 4, z: 16, core: 2. Of those that a mesh axis runs over, the one named last changes fastest.
Arguments:
- old_factors: float32 [128, 1, 1024, 1024], P('dp', None, 'mp'), as said below
- gradients: bfloat16 [128, 56, 32, 1024], P('dp', None, 'mp'), may hold values from -2.5 to 2.5
- old_slots: int32 [128, 1], replicated, may hold values from -1 to 71, as said below
- new_slots: int32 [128, 1], replicated, may hold values from -1 to 71, as said below
Outputs:
- inverses: bfloat16 [128, 1, 1024, 1024], P('dp', None, 'mp')
- preconditioned: bfloat16 [56, 32, 1024], P(None, 'mp')
Inputs may be any that keep to these rules, and one draw needn't show every extreme that they name: `old_slots`: every block number 0 to 71 stands in exactly one slot and all other slots hold -1; some owner has all 1 slots filled. `new_slots`: every block number 0 to 71 stands in exactly one slot and all other slots hold -1; some owner has all 1 slots filled. `old_factors`: every slot holds a symmetric positive definite matrix.
All inputs are finite; a program needn't handle non-finite values.
Results may differ from a plain program's by a relative error of at most 0.0057.
Values may be sent and summed in bfloat16 or wider, within the bound.
No kernel may reach another device: no remote copies, remote signals or barrier semaphores. Data moves between devices by JAX's collectives and lax.ppermute only.
A program may use at most 64 MiB of HBM per device.

v0:
```python
import jax
import jax.numpy as jnp
from jax import lax
from jax.sharding import PartitionSpec as P

D = 8192
FF = 28672


damping_base = 2.0


def times_plain(left, right):
    return jnp.einsum(
        "sij,sjk->sik",
        left,
        right,
        precision=lax.Precision.HIGHEST,
        preferred_element_type=jnp.float32,
    )


def times_right_t(left, right):
    return jnp.einsum(
        "sij,skj->sik",
        left,
        right,
        precision=lax.Precision.HIGHEST,
        preferred_element_type=jnp.float32,
    )


def times_left_t(left, right):
    return jnp.einsum(
        "sji,sjk->sik",
        left,
        right,
        precision=lax.Precision.HIGHEST,
        preferred_element_type=jnp.float32,
    )


def blocked_inverse(damped):
    width = damped.shape[-1]
    panel_size = min(256, width)
    panel_count = width // panel_size
    eye_panel = jnp.broadcast_to(
        jnp.eye(panel_size, dtype=jnp.float32), damped.shape[:-2] + (panel_size, panel_size)
    )
    lower = {}
    diag_inv = {}
    for col_block in range(panel_count):
        for row_block in range(col_block, panel_count):
            update = damped[
                :,
                row_block * panel_size : (row_block + 1) * panel_size,
                col_block * panel_size : (col_block + 1) * panel_size,
            ]
            for inner in range(col_block):
                update = update - times_right_t(lower[row_block, inner], lower[col_block, inner])
            if row_block == col_block:
                factor = jnp.linalg.cholesky(update)
                lower[col_block, col_block] = factor
                diag_inv[col_block] = lax.linalg.triangular_solve(
                    factor, eye_panel, left_side=True, lower=True
                )
            else:
                lower[row_block, col_block] = times_right_t(update, diag_inv[col_block])
    inverse_lower = {}
    for col_block in range(panel_count):
        inverse_lower[col_block, col_block] = diag_inv[col_block]
        for row_block in range(col_block + 1, panel_count):
            total = times_plain(lower[row_block, col_block], inverse_lower[col_block, col_block])
            for inner in range(col_block + 1, row_block):
                total = total + times_plain(
                    lower[row_block, inner], inverse_lower[inner, col_block]
                )
            inverse_lower[row_block, col_block] = -times_plain(diag_inv[row_block], total)
    upper_part = {}
    for first in range(panel_count):
        for second in range(first, panel_count):
            total = times_left_t(inverse_lower[second, first], inverse_lower[second, second])
            for inner in range(second + 1, panel_count):
                total = total + times_left_t(
                    inverse_lower[inner, first], inverse_lower[inner, second]
                )
            upper_part[first, second] = total
    row_pieces = []
    for first in range(panel_count):
        column_pieces = []
        for second in range(panel_count):
            if second >= first:
                column_pieces.append(upper_part[first, second])
            else:
                column_pieces.append(jnp.swapaxes(upper_part[second, first], 1, 2))
        row_pieces.append(jnp.concatenate(column_pieces, axis=2))
    return jnp.concatenate(row_pieces, axis=1)


def invert_slots(matrices, shift_values, is_valid):
    width = matrices.shape[-1]
    identity = jnp.eye(width, dtype=jnp.float32)
    damped = jnp.where(
        is_valid[:, None, None], matrices + shift_values[:, None, None] * identity, identity
    )
    inverse = blocked_inverse(damped)
    return jnp.where(is_valid[:, None, None], inverse, 0.0).astype(jnp.bfloat16)


def slot_positions(slot_ids, wanted):
    slot_range = jnp.arange(slot_ids.shape[0], dtype=jnp.int32)
    found = jnp.sum(jnp.where(slot_ids[None, :] == wanted[:, None], slot_range[None, :], 0), axis=1)
    return jnp.minimum(found, slot_ids.shape[0] - 1).astype(jnp.int32)


def damping_for(own_ids, trace_ratio, layer_ids, layer_blocks, a_span):
    own_valid = own_ids >= 0
    own_block = jnp.maximum(own_ids, 0)
    own_input = own_block % layer_blocks < a_span
    own_ratio = jnp.sum(
        jnp.where(
            (own_block // layer_blocks)[:, None] == layer_ids[None, :], trace_ratio[None, :], 0.0
        ),
        axis=1,
    )
    own_ratio = jnp.where(own_valid, own_ratio, 1.0)
    return (jnp.where(own_input, damping_base * own_ratio, damping_base / own_ratio), own_valid)


def local(old_factors, gradients, old_slots, new_slots):
    mp_index = lax.axis_index("mp")
    dp_index = lax.axis_index("dp")
    dp_count = lax.axis_size("dp")
    slot_count = old_factors.shape[1]
    band = old_factors.shape[2]
    block_width = old_factors.shape[3]
    strip_width = block_width // dp_count
    tile_count = gradients.shape[1]
    row_count = gradients.shape[2]
    a_span = FF // block_width
    layer_blocks = a_span + D // block_width
    layers = tile_count // a_span
    slot_total = dp_count * slot_count
    old_flat = old_slots.reshape(slot_total)
    new_flat = new_slots.reshape(slot_total)
    strips = old_factors[0]
    own_old = lax.dynamic_slice_in_dim(old_flat, dp_index * slot_count, slot_count)
    own_new = lax.dynamic_slice_in_dim(new_flat, dp_index * slot_count, slot_count)
    squares = lax.dynamic_slice_in_dim(strips, mp_index * band, band, 2)
    diag_sums = jnp.trace(squares, axis1=1, axis2=2)
    layer_ids = jnp.arange(layers, dtype=jnp.int32)
    old_input = jnp.maximum(own_old, 0) % layer_blocks < a_span
    layer_hit = ((own_old // layer_blocks)[:, None] == layer_ids[None, :]) & (own_old >= 0)[:, None]
    input_terms = jnp.sum(
        jnp.where(layer_hit & old_input[:, None], diag_sums[:, None], 0.0), axis=0
    )
    output_terms = jnp.sum(
        jnp.where(layer_hit & ~old_input[:, None], diag_sums[:, None], 0.0), axis=0
    )
    trace_totals = lax.psum(jnp.stack([input_terms, output_terms], axis=0), ("dp", "mp"))
    trace_ratio = jnp.sqrt(trace_totals[0] / FF / (trace_totals[1] / D))
    new_valid = new_flat >= 0
    source = slot_positions(old_flat, new_flat)
    spread = lax.all_to_all(strips, "dp", split_axis=2, concat_axis=0, tiled=True)
    outgoing = jnp.where(
        new_valid[:, None, None], jnp.take(spread, source, axis=0), jnp.zeros((), jnp.float32)
    )
    outgoing = outgoing.reshape(dp_count, slot_count, band, strip_width)
    arrived = lax.all_to_all(outgoing, "dp", split_axis=0, concat_axis=3, tiled=True)[0]
    whole = lax.all_gather(arrived, "mp", axis=1, tiled=True)
    shift_values, own_valid = damping_for(own_new, trace_ratio, layer_ids, layer_blocks, a_span)
    full_half = invert_slots(whole, shift_values, own_valid)
    inverse_band = lax.dynamic_slice_in_dim(full_half, mp_index * band, band, 1)
    summed = lax.psum_scatter(
        gradients[0].astype(jnp.float32), "dp", scatter_dimension=2, tiled=True
    ).astype(jnp.bfloat16)
    plan_valid = new_flat >= 0
    plan_block = jnp.maximum(new_flat, 0)
    plan_input = plan_valid & (plan_block % layer_blocks < a_span)
    tile_of = jnp.minimum(
        plan_block // layer_blocks * a_span + plan_block % layer_blocks, tile_count - 1
    )
    tile_send = jnp.where(
        plan_input[:, None, None], jnp.take(summed, tile_of, axis=0), jnp.zeros((), jnp.bfloat16)
    )
    tile_send = tile_send.reshape(dp_count, slot_count, row_count, strip_width)
    owned_tiles = lax.all_to_all(tile_send, "dp", split_axis=0, concat_axis=3, tiled=True)[0]
    result = jnp.einsum(
        "srk,skj->srj", owned_tiles, full_half, preferred_element_type=jnp.float32
    ).astype(jnp.bfloat16)
    tile_range = jnp.arange(tile_count, dtype=jnp.int32)
    tile_block = tile_range // a_span * layer_blocks + tile_range % a_span
    placed = slot_positions(new_flat, tile_block)
    gathered = lax.all_gather(result, "dp", axis=0, tiled=True)
    precond = jnp.take(gathered, placed, axis=0)
    return (inverse_band[None], precond)


def solution(mesh):
    in_specs = (P("dp", None, "mp", None), P("dp", None, "mp", None), P(), P())
    out_specs = (P("dp", None, "mp", None), P(None, "mp", None))
    return jax.shard_map(local, mesh=mesh, in_specs=in_specs, out_specs=out_specs, check_vma=False)
```

profile of v0, /device:TPU:1, one launch (start us, length us, event | category | flops | bytes accessed | tf_op | source)
XLA Modules:
  0.0 853.5 jit_solution(9655227339929867047)
XLA Ops:
  8.0 3.6 copy.138
  11.6 20.4 %all-to-all-start = ((f32[1,256,1024]{1,0,2:T(1,128)}), f32[1,256,1024]{1,0,2:T(1,128)S(1)}, u32[]{:S(2)}, u32[]{:S(2)}) async-start(f32[1,256,1024]{1,0,2:T(1,128)} %bitcast.3), calls=%async_computation | async-start | bytes 2097152 | tf_op jit(solution)/shard_map/all_to_all | solution.py:164
  32.3 51.6 %all-to-all-done = f32[1,256,1024]{1,0,2:T(1,128)S(1)} async-done(((f32[1,256,1024]{1,0,2:T(1,128)}), f32[1,256,1024]{1,0,2:T(1,128)S(1)}, u32[]{:S(2)}, u32[]{:S(2)}) %all-to-all-start) | async-done | bytes 1048608 | tf_op jit(solution)/shard_map/all_to_all | solution.py:164
  84.7 1.3 fusion.48
  86.0 10.2 %all-to-all-start.1 = ((f32[128,1,256,8]{2,3,1,0:T(8,128)}), f32[128,1,256,8]{2,3,1,0:T(8,128)S(1)}, u32[]{:S(2)}, u32[]{:S(2)}) async-start(f32[128,1,256,8]{2,3,1,0:T(8,128)} %fusion.48), calls=%async_computation.1 | async-start | bytes 2097152 | tf_op jit(solution)/shard_map/all_to_all | solution.py:169
  96.3 3.2 copy.169
  99.5 2.2 bitcast_convert_fusion
  101.7 46.3 %all-to-all-done.1 = f32[128,1,256,8]{2,3,1,0:T(8,128)S(1)} async-done(((f32[128,1,256,8]{2,3,1,0:T(8,128)}), f32[128,1,256,8]{2,3,1,0:T(8,128)S(1)}, u32[]{:S(2)}, u32[]{:S(2)}) %all-to-all-start.1) | async-done | bytes 1048608 | tf_op jit(solution)/shard_map/all_to_all | solution.py:169
  153.1 1.6 fusion.58
  155.3 106.2 %psum.7 = f32[2,2]{1,0:T(2,128)S(1)} all-reduce(f32[2,2]{1,0:T(2,128)S(1)} %pad_maximum_fusion.2), channel_id=1, replica_groups=mesh['dp'=128,'mp'=4] {'dp','mp'}, use_global_device_ids=true, to_apply=%region_2.3 | all-reduce | flops 4 | bytes 32 | tf_op jit(solution)/shard_map/psum | solution.py:160
  266.1 90.3 %reduce-scatter.2.cloned.1.call-done = f32[56,8,8]{0,1,2:T(8,128)} async-done(((f32[56,8,1024]{0,1,2:T(8,128)}), f32[56,8,8]{0,1,2:T(8,128)}) %reduce-scatter.2.cloned.1.call-update) | async-done | bytes 14352 | tf_op jit(solution)/shard_map/reduce_scatter | solution.py:174
  359.0 24.0 %all-to-all-start.2 = ((bf16[128,1,8,8]{3,2,1,0:T(8,128)(2,1)}), bf16[128,1,8,8]{3,2,1,0:T(8,128)(2,1)S(1)}, u32[]{:S(2)}, u32[]{:S(2)}) async-start(bf16[128,1,8,8]{3,2,1,0:T(8,128)(2,1)} %fusion.53), calls=%async_computation.3 | async-start | bytes 524288 | tf_op jit(solution)/shard_map/all_to_all | solution.py:187
  383.2 20.2 %all-to-all-done.2 = bf16[128,1,8,8]{3,2,1,0:T(8,128)(2,1)S(1)} async-done(((bf16[128,1,8,8]{3,2,1,0:T(8,128)(2,1)}), bf16[128,1,8,8]{3,2,1,0:T(8,128)(2,1)S(1)}, u32[]{:S(2)}, u32[]{:S(2)}) %all-to-all-start.2) | async-done | bytes 16416 | tf_op jit(solution)/shard_map/all_to_all | solution.py:187
  403.8 2.7 convert_select_fusion
  406.5 1.9 copy-done
  409.6 11.7 %custom-call.25 = f32[1,128,128]{2,1,0:T(8,128)S(1)} custom-call(f32[1,128,128]{2,1,0:T(8,128)S(1)} %cholesky.339), custom_call_target="Cholesky" | custom-call | tf_op jit(solution)/shard_map/jit(cholesky)/cholesky | solution.py:62
  421.4 9.8 %custom-call.26 = f32[1,1,128,128]{2,3,1,0:T(8,128)S(1)} custom-call(f32[1,1,128,128]{3,2,1,0:T(8,128)S(1)} %get-tuple-element.95), custom_call_target="InvertDiagBlocksLowerTriangular" | custom-call | tf_op jit(solution)/shard_map/jit(cholesky)/cholesky | solution.py:62
  431.7 11.7 %custom-call.27 = f32[1,128,128]{2,1,0:T(8,128)S(1)} custom-call(f32[1,128,128]{2,1,0:T(8,128)S(1)} %fusion.28), custom_call_target="Cholesky" | custom-call | tf_op jit(solution)/shard_map/jit(cholesky)/cholesky | solution.py:62
  446.1 4.0 while.8
  446.7 1.4 bitcast_dynamic-update-slice_fusion.12
  448.7 1.4 bitcast_dynamic-update-slice_fusion.12
  450.1 20.1 %custom-call.28 = f32[1,2,128,128]{2,3,1,0:T(8,128)S(1)} custom-call(f32[1,2,128,128]{3,2,1,0:T(8,128)S(1)} %bitcast.561), custom_call_target="InvertDiagBlocksLowerTriangular" | custom-call | tf_op jit(solution)/shard_map/triangular_solve/custom-call.0 | solution.py:64
  471.2 1.5 fusion.49
  472.7 1.5 fusion.51
  474.3 1.5 fusion.50
  475.8 1.4 fusion.7
  477.2 1.4 fusion.16
  478.8 11.7 %custom-call.29 = f32[1,128,128]{2,1,0:T(8,128)S(1)} custom-call(f32[1,128,128]{2,1,0:T(8,128)S(1)} %cholesky.342), custom_call_target="Cholesky" | custom-call | tf_op jit(solution)/shard_map/jit(cholesky)/cholesky | solution.py:62
  490.5 9.8 %custom-call.30 = f32[1,1,128,128]{2,3,1,0:T(8,128)S(1)} custom-call(f32[1,1,128,128]{3,2,1,0:T(8,128)S(1)} %get-tuple-element.91), custom_call_target="InvertDiagBlocksLowerTriangular" | custom-call | tf_op jit(solution)/shard_map/jit(cholesky)/cholesky | solution.py:62
  500.8 11.9 %custom-call.31 = f32[1,128,128]{2,1,0:T(8,128)S(1)} custom-call(f32[1,128,128]{2,1,0:T(8,128)S(1)} %fusion.29), custom_call_target="Cholesky" | custom-call | tf_op jit(solution)/shard_map/jit(cholesky)/cholesky | solution.py:62
  515.4 4.0 while.9
  516.0 1.4 bitcast_dynamic-update-slice_fusion.13
  518.0 1.4 bitcast_dynamic-update-slice_fusion.13
  519.4 19.7 %custom-call.32 = f32[1,2,128,128]{2,3,1,0:T(8,128)S(1)} custom-call(f32[1,2,128,128]{3,2,1,0:T(8,128)S(1)} %bitcast.562), custom_call_target="InvertDiagBlocksLowerTriangular" | custom-call | tf_op jit(solution)/shard_map/triangular_solve/custom-call.0 | solution.py:64
  540.0 1.4 fusion.11
  543.4 1.4 fusion.19
  544.8 1.4 fusion.9
  546.3 11.7 %custom-call.33 = f32[1,128,128]{2,1,0:T(8,128)S(1)} custom-call(f32[1,128,128]{2,1,0:T(8,128)S(1)} %cholesky.345), custom_call_target="Cholesky" | custom-call | tf_op jit(solution)/shard_map/jit(cholesky)/cholesky | solution.py:62
  558.1 9.8 %custom-call.34 = f32[1,1,128,128]{2,3,1,0:T(8,128)S(1)} custom-call(f32[1,1,128,128]{3,2,1,0:T(8,128)S(1)} %get-tuple-element.87), custom_call_target="InvertDiagBlocksLowerTriangular" | custom-call | tf_op jit(solution)/shard_map/jit(cholesky)/cholesky | solution.py:62
  568.4 12.1 %custom-call.35 = f32[1,128,128]{2,1,0:T(8,128)S(1)} custom-call(f32[1,128,128]{2,1,0:T(8,128)S(1)} %fusion.30), custom_call_target="Cholesky" | custom-call | tf_op jit(solution)/shard_map/jit(cholesky)/cholesky | solution.py:62
  583.2 4.0 while.10
  583.8 1.4 bitcast_dynamic-update-slice_fusion.14
  585.8 1.4 bitcast_dynamic-update-slice_fusion.14
  587.2 19.7 %custom-call.36 = f32[1,2,128,128]{2,3,1,0:T(8,128)S(1)} custom-call(f32[1,2,128,128]{3,2,1,0:T(8,128)S(1)} %bitcast.563), custom_call_target="InvertDiagBlocksLowerTriangular" | custom-call | tf_op jit(solution)/shard_map/triangular_solve/custom-call.0 | solution.py:64
  609.6 1.3 fusion.83
  614.9 1.3 fusion.88
  616.2 1.3 fusion.97
  617.6 1.4 fusion.14
  619.2 11.7 %custom-call.37 = f32[1,128,128]{2,1,0:T(8,128)S(1)} custom-call(f32[1,128,128]{2,1,0:T(8,128)S(1)} %cholesky.348), custom_call_target="Cholesky" | custom-call | tf_op jit(solution)/shard_map/jit(cholesky)/cholesky | solution.py:62
  630.9 10.0 %custom-call.38 = f32[1,1,128,128]{2,3,1,0:T(8,128)S(1)} custom-call(f32[1,1,128,128]{3,2,1,0:T(8,128)S(1)} %get-tuple-element.83), custom_call_target="InvertDiagBlocksLowerTriangular" | custom-call | tf_op jit(solution)/shard_map/jit(cholesky)/cholesky | solution.py:62
  641.4 11.7 %custom-call.39 = f32[1,128,128]{2,1,0:T(8,128)S(1)} custom-call(f32[1,128,128]{2,1,0:T(8,128)S(1)} %fusion.31), custom_call_target="Cholesky" | custom-call | tf_op jit(solution)/shard_map/jit(cholesky)/cholesky | solution.py:62
  655.8 5.4 while.11
  657.1 1.3 bitcast_dynamic-update-slice_fusion.15
  659.8 1.3 bitcast_dynamic-update-slice_fusion.15
  661.2 19.7 %custom-call.40 = f32[1,2,128,128]{2,3,1,0:T(8,128)S(1)} custom-call(f32[1,2,128,128]{3,2,1,0:T(8,128)S(1)} %bitcast.560), custom_call_target="InvertDiagBlocksLowerTriangular" | custom-call | tf_op jit(solution)/shard_map/triangular_solve/custom-call.0 | solution.py:64
  686.3 1.3 convolution_add_fusion.6
  689.6 1.3 fusion.91
  695.6 1.5 convolution_add_fusion.3
  697.8 1.7 convolution_add_fusion.7
  700.5 1.5 convolution_add_fusion.13
  704.6 3.0 maximum_bitcast_fusion.1
  707.7 1.3 fusion.32
  710.2 132.2 %all-gather.6.cloned.1.call-done = bf16[1024,1024]{1,0:T(8,128)(2,1)} async-done(((bf16[8,1024]{1,0:T(8,128)(2,1)}), bf16[1024,1024]{1,0:T(8,128)(2,1)}) %all-gather.6.cloned.1.call-update) | async-done | bytes 2097168 | tf_op jit(solution)/shard_map/all_gather | solution.py:194
  842.4 2.2 gather_fusion.2
  (183 shorter events, 52.3 us)
Async XLA Ops:
  8.0 24.0 %copy-start.9 = (s32[128,1]{0,1:T(1,128)S(1)}, s32[128,1]{0,1:T(1,128)}, u32[]{:S(2)}) copy-start(s32[128,1]{0,1:T(1,128)} %param.9) | copy-start | bytes 1540
  8.0 24.0 %copy-start.10 = (s32[128,1]{0,1:T(1,128)S(1)}, s32[128,1]{0,1:T(1,128)}, u32[]{:S(2)}) copy-start(s32[128,1]{0,1:T(1,128)} %param.10) | copy-start | bytes 1540
  11.6 72.2 %all-to-all-start = ((f32[1,256,1024]{1,0,2:T(1,128)}), f32[1,256,1024]{1,0,2:T(1,128)S(1)}, u32[]{:S(2)}, u32[]{:S(2)}) async-start(f32[1,256,1024]{1,0,2:T(1,128)} %bitcast.3), calls=%async_computation | async-start | bytes 2097152 | tf_op jit(solution)/shard_map/all_to_all | solution.py:164
  86.0 62.1 %all-to-all-start.1 = ((f32[128,1,256,8]{2,3,1,0:T(8,128)}), f32[128,1,256,8]{2,3,1,0:T(8,128)S(1)}, u32[]{:S(2)}, u32[]{:S(2)}) async-start(f32[128,1,256,8]{2,3,1,0:T(8,128)} %fusion.48), calls=%async_computation.1 | async-start | bytes 2097152 | tf_op jit(solution)/shard_map/all_to_all | solution.py:169
  96.2 260.1 %reduce-scatter.2.cloned.1.call-start = ((), (), s32[]{:S(2)}) async-start(), calls=%async_computation.5 | async-start | bytes 4227072 | tf_op jit(solution)/shard_map/reduce_scatter | solution.py:174
  101.7 302.1 %all-gather.4.cloned.1.call-start = ((), (), s32[]{:S(2)}) async-start(), calls=%async_computation.4 | async-start | bytes 5242880 | tf_op jit(solution)/shard_map/all_gather | solution.py:170
  148.1 1.1 copy-start.1
  359.0 44.5 %all-to-all-start.2 = ((bf16[128,1,8,8]{3,2,1,0:T(8,128)(2,1)}), bf16[128,1,8,8]{3,2,1,0:T(8,128)(2,1)S(1)}, u32[]{:S(2)}, u32[]{:S(2)}) async-start(bf16[128,1,8,8]{3,2,1,0:T(8,128)(2,1)} %fusion.53), calls=%async_computation.3 | async-start | bytes 524288 | tf_op jit(solution)/shard_map/all_to_all | solution.py:187
  383.0 459.4 %all-gather.6.cloned.1.call-start = ((), (), s32[]{:S(2)}) async-start(), calls=%async_computation.6 | async-start | bytes 2113536 | tf_op jit(solution)/shard_map/all_gather | solution.py:194
  406.5 1.9 copy-start
  587.2 20.6 %copy-start.12 = (s32[2,2]{1,0:T(2,128)}, s32[2,2]{1,0:T(2,128)S(1)}, u32[]{:S(2)}) copy-start(s32[2,2]{1,0:T(2,128)S(1)} %get-tuple-element.309) | copy-start | bytes 52
  619.0 65.1 %copy-start.3 = (f32[256,256]{0,1:T(8,128)S(1)}, f32[256,256]{0,1:T(8,128)}, u32[]{:S(2)}) copy-start(f32[256,256]{0,1:T(8,128)} %fusion.83) | copy-start | bytes 786436
  683.4 7.5 copy-start.5
  685.7 6.6 copy-start.4
  700.3 4.3 copy-start.2
  702.0 2.6 copy-start.6
  702.6 2.0 copy-start.7
  704.3 3.4 copy-start.8
  707.6 1.3 copy-start.11
Sparse Core Ops, SparseCore 0:
  101.8 254.5 reduce-scatter.1
  709.1 133.2 all-gather.5
Sparse Core Ops, SparseCore 1:
  149.3 51.6 all-gather.3
where the time goes:
time: 862 us; the launch traced here: 853 us
  waiting for transfers between devices  341 us (40%)
  other arithmetic  236 us (27%)
  blocking collectives  106 us (12%)
  starting transfers between devices  54.9 us (6%)
  matrix products  51.2 us (6%)
  local copies, waits for them, and re-layouts  35.1 us (4%)
  between operations  28.8 us (3%)
    another operation x28, other arithmetic, blocked_inverse(): factor = jnp.linalg.cholesky(update)  139 us
    all_gather x1, waiting for transfers between devices, local(): gathered = lax.all_gather(result, 'dp', axis=0, tiled=True)  132 us
    psum x1, blocking collectives, local(): lax.psum(jnp.stack([input_terms, output_terms], axis=0), ('dp', 'mp'))  106 us
    reduce_scatter x1, waiting for transfers between devices, local(): lax.psum_scatter(gradients[0].astype(jnp.float32), 'dp', scatter_dimensio...  90.3 us
    another operation x9, other arithmetic, blocked_inverse(): lax.linalg.triangular_solve(factor, eye_panel, left_side=True, lower=True)  79.3 us
    all_to_all x1, waiting for transfers between devices, local(): lax.all_to_all(strips, 'dp', split_axis=2, concat_axis=0, tiled=True)  51.6 us
    all_to_all x1, waiting for transfers between devices, local(): lax.all_to_all(outgoing, 'dp', split_axis=0, concat_axis=3, tiled=True)[0]  46.3 us
    all_to_all x1, starting transfers between devices, local(): lax.all_to_all(tile_send, 'dp', split_axis=0, concat_axis=3, tiled=True)[0]  24 us
  transfers between devices with their start and end apart: 6, of which 5 were waited for; matrix products, arithmetic and copies ran while one was open for 2% of the time, Pallas kernels for 0%

commit v1 on v0

v1 whole, which is shorter than its diff:
```python
import jax
import jax.numpy as jnp
from jax import lax
from jax.experimental import pallas as pl
from jax.experimental.pallas import tpu as pltpu
from jax.sharding import Mesh, PartitionSpec as P

D = 8192
FF = 28672
DAMPING_BASE = 2.0
X_CORE = 8

BASE = 128
SUB = 8


def row_of(x, j):
    return jnp.broadcast_to(x[j : j + 1, :], x.shape)


def lane_of(x, j):
    return jnp.broadcast_to(x[:, j : j + 1], x.shape)


def base_sweep(load, store):
    groups = [load(i) for i in range(BASE // SUB)]
    sub_ids = lax.broadcasted_iota(jnp.int32, (SUB, BASE), 0)
    lane_ids = lax.broadcasted_iota(jnp.int32, (SUB, BASE), 1)
    for p in range(BASE // SUB):
        pivot_lanes = (lane_ids // SUB) == p
        spread = [lane_of(groups[p], p * SUB + j) for j in range(SUB)]
        unit = jnp.where(lane_ids == sub_ids + p * SUB, 1.0, 0.0)
        rows = jnp.where(pivot_lanes, unit, groups[p])
        for j in range(SUB):
            here = sub_ids == j
            scale = 1.0 / row_of(spread[j], j)
            line = row_of(rows, j) * scale
            rows = jnp.where(here, line, rows - spread[j] * line)
            for i in range(j + 1, SUB):
                part = row_of(spread[i], j) * scale
                spread[i] = jnp.where(here, part, spread[i] - spread[j] * part)
        rows = jnp.where(pivot_lanes, -rows, rows)
        lines = [row_of(rows, j) for j in range(SUB)]
        for i in range(BASE // SUB):
            if i == p:
                continue
            total = jnp.where(pivot_lanes, 0.0, groups[i])
            for j in range(SUB):
                total = total - lane_of(groups[i], p * SUB + j) * lines[j]
            groups[i] = total
        groups[p] = rows
    for i in range(BASE // SUB):
        store(i, groups[i])


def halves(x):
    high = x.astype(jnp.bfloat16)
    return high, (x - high.astype(jnp.float32)).astype(jnp.bfloat16)


def dot3(left, right):
    def one(a, b):
        return jnp.dot(a, b, preferred_element_type=jnp.float32)

    return one(left[0], right[0]) + (one(left[0], right[1]) + one(left[1], right[0]))


def invert_kernel(
    scalar_ref, shift_ref, rows_ref, one_ref, two_ref, three_ref,
    band_ref, full_ref, m_ref, d_ref, th_ref, tl_ref,
):
    n = rows_ref.shape[1]
    wide = rows_ref.shape[0]
    count = n // wide
    mp_index = scalar_ref[1]

    def block(i):
        return slice(i * wide, (i + 1) * wide)

    def place(i):
        return pl.ds(pl.multiple_of(lax.rem(mp_index + i, count) * wide, wide), wide)

    @pl.when(scalar_ref[0] > 0)
    def _():
        eye = jnp.where(
            lax.broadcasted_iota(jnp.int32, (wide, wide), 0)
            == lax.broadcasted_iota(jnp.int32, (wide, wide), 1),
            shift_ref[0],
            0.0,
        )

        def put(i, j, value):
            if i == j:
                m_ref[block(i), block(i)] = value + eye
            else:
                m_ref[block(i), block(j)] = value
                m_ref[block(j), block(i)] = value.T

        for j in range(count):
            put(0, j, rows_ref[:, place(j)])
        put(1, 1, one_ref[:, block(0)])
        put(1, 2, one_ref[:, block(1)])
        put(2, 2, two_ref[:, block(0)])
        put(2, 3, two_ref[:, block(1)])
        put(3, 3, three_ref[:, block(0)])
        put(3, 1, three_ref[:, block(1)])

        @pl.loop(0, count)
        def _(k):
            at = pl.ds(pl.multiple_of(k * wide, wide), wide)

            d_ref[...] = m_ref[at, at]

            def sweep_half(h):
                lo = h * BASE
                base_sweep(
                    lambda i: d_ref[lo + i * SUB : lo + (i + 1) * SUB, lo : lo + BASE],
                    lambda i, v: d_ref.__setitem__(
                        (slice(lo + i * SUB, lo + (i + 1) * SUB), slice(lo, lo + BASE)), v
                    ),
                )

            one, two = slice(0, BASE), slice(BASE, wide)
            sweep_half(0)
            minus_p = halves(d_ref[one, one])
            cross = halves(d_ref[one, two])
            cross_t = halves(d_ref[two, one])
            t_halves = halves(-dot3(minus_p, cross))
            d_ref[two, two] = d_ref[two, two] - dot3(cross_t, t_halves)
            left = halves(-dot3(cross_t, minus_p))
            sweep_half(1)
            minus_p = halves(d_ref[two, two])
            up = dot3(t_halves, minus_p)
            d_ref[one, one] = d_ref[one, one] + dot3(halves(up), left)
            d_ref[one, two] = -up
            d_ref[two, one] = -dot3(minus_p, left)

            minus_p = halves(d_ref[...])
            col_h, col_l = halves(m_ref[:, at])
            rows = -dot3(minus_p, halves(m_ref[at, :]))
            m_ref[:, at] = jnp.zeros((n, wide), jnp.float32)
            m_ref[at, :] = rows
            m_ref[at, at] = d_ref[...]
            th_ref[...], tl_ref[...] = halves(m_ref[at, :])
            for i in range(count):

                @pl.when(i != k)
                def _():
                    m_ref[block(i), :] = m_ref[block(i), :] - dot3(
                        (col_h[block(i)], col_l[block(i)]), (th_ref[...], tl_ref[...])
                    )

        for j in range(count):
            band_ref[:, place(j)] = (-m_ref[block(0), block(j)]).astype(jnp.bfloat16)
            for i in range(count):
                full_ref[place(i), place(j)] = (-m_ref[block(i), block(j)]).astype(jnp.bfloat16)

    @pl.when(scalar_ref[0] <= 0)
    def _():
        band_ref[...] = jnp.zeros(band_ref.shape, jnp.bfloat16)
        full_ref[...] = jnp.zeros(full_ref.shape, jnp.bfloat16)


def invert(scalars, shift, rows, one, two, three):
    wide, n = rows.shape
    in_smem = pl.BlockSpec(memory_space=pltpu.SMEM)
    in_vmem = pl.BlockSpec(memory_space=pltpu.VMEM)
    return pl.pallas_call(
        invert_kernel,
        out_shape=(
            jax.ShapeDtypeStruct((wide, n), jnp.bfloat16),
            jax.ShapeDtypeStruct((n, n), jnp.bfloat16),
        ),
        in_specs=[in_smem] * 2 + [in_vmem] * 4,
        out_specs=(in_vmem, in_vmem),
        scratch_shapes=[
            pltpu.VMEM((n, n), jnp.float32),
            pltpu.VMEM((wide, wide), jnp.float32),
            pltpu.VMEM((wide, n), jnp.bfloat16),
            pltpu.VMEM((wide, n), jnp.bfloat16),
        ],
        compiler_params=pltpu.CompilerParams(vmem_limit_bytes=40 * 1024 * 1024),
        cost_estimate=pl.CostEstimate(
            flops=48 * n * n * n, bytes_accessed=6 * n * n, transcendentals=0
        ),
    )(scalars, shift, rows, one, two, three)


def positions(slot_ids, wanted):
    slot_range = jnp.arange(slot_ids.shape[0], dtype=jnp.int32)
    hit = slot_ids[None, :] == wanted[:, None]
    return jnp.sum(jnp.where(hit, slot_range[None, :], 0), axis=1).astype(jnp.int32)


def exchange(pieces, axes):
    return lax.all_to_all(pieces, axes, split_axis=0, concat_axis=0, tiled=True)


def from_all(piece, axes, count):
    return exchange(jnp.broadcast_to(piece[None], (count,) + piece.shape), axes)


DP = ("z", "xc")


def local(old_factors, gradients, old_slots, new_slots):
    mp_index = lax.axis_index("mp")
    mp_count = lax.axis_size("mp")
    z_count, xc_count = lax.axis_size("z"), lax.axis_size("xc")
    dp_count = z_count * xc_count
    dp_index = lax.axis_index("z") * xc_count + lax.axis_index("xc")
    band, width = old_factors.shape[2:]
    tile_count, row_count = gradients.shape[1:3]
    a_span = FF // width
    layer_blocks = a_span + D // width
    layers = tile_count // a_span
    old_flat = old_slots.reshape(dp_count)
    new_flat = new_slots.reshape(dp_count)

    rows = old_factors[0, 0]
    doubled = jnp.concatenate([rows, rows], axis=1)
    ahead = lax.dynamic_slice_in_dim(doubled, mp_index * band, 3 * band, 1)
    near = ahead[:, : 2 * band]
    far = jnp.concatenate([ahead[:, :band], ahead[:, 2 * band :]], axis=1)

    def from_next(value, step):
        return lax.ppermute(
            value, "mp", [((i + step) % mp_count, i) for i in range(mp_count)]
        )

    one = from_next(near, 1)
    two = from_next(near, 2)
    three = from_next(far, 3)

    trace = jnp.trace(ahead[:, :band])
    lanes = jnp.full((1, 128), trace, jnp.float32)
    block_trace = jnp.sum(from_all(lanes, "mp", mp_count), axis=0)
    slot_traces = from_all(block_trace, DP, dp_count)[:, 0, 0]
    layer_ids = jnp.arange(layers, dtype=jnp.int32)
    held = old_flat >= 0
    slot_input = old_flat % layer_blocks < a_span
    in_layer = held[None, :] & (old_flat[None, :] // layer_blocks == layer_ids[:, None])
    trace_input = jnp.sum(jnp.where(in_layer & slot_input[None, :], slot_traces[None, :], 0.0), axis=1)
    trace_output = jnp.sum(jnp.where(in_layer & ~slot_input[None, :], slot_traces[None, :], 0.0), axis=1)
    ratios = jnp.sqrt(trace_input / FF / (trace_output / D))
    own = lax.dynamic_index_in_dim(old_flat, dp_index, keepdims=False)
    own_block = jnp.maximum(own, 0)
    own_layer = own_block // layer_blocks
    own_input = own_block % layer_blocks < a_span
    ratio = jnp.sum(jnp.where(layer_ids == own_layer, ratios, 0.0))
    shift = jnp.where(own_input, DAMPING_BASE * ratio, DAMPING_BASE / ratio)

    lane = 128
    parts = gradients[0].reshape(2, tile_count // 2, row_count, width // lane, lane)
    parts = parts.transpose(0, 2, 3, 1, 4).reshape(dp_count, tile_count // 2, lane)
    parts = exchange(parts, DP)

    scalars = jnp.stack([(own >= 0).astype(jnp.int32), mp_index.astype(jnp.int32)])
    inverse_band, inverse = invert(scalars, shift.reshape(1), rows, one, two, three)

    spread = exchange(inverse_band.reshape(dp_count, band // dp_count, width), DP)
    slot_range = jnp.arange(dp_count, dtype=jnp.int32)
    empty = jnp.min(jnp.where(held, dp_count - 1, slot_range))
    source = jnp.where(new_flat >= 0, positions(old_flat, new_flat), empty)
    arrived = exchange(jnp.take(spread, source, axis=0), DP)
    inverses = arrived.reshape(1, 1, band, width)

    summed = jnp.sum(parts.astype(jnp.float32), axis=0).astype(jnp.bfloat16).astype(jnp.float32)
    block = jnp.maximum(old_flat, 0)
    tile_of = jnp.minimum(block // layer_blocks * a_span + block % layer_blocks, tile_count - 1)
    half_tiles = tile_count // 2
    tile_rows = jnp.take(summed, tile_of % half_tiles, axis=0)
    tile_rows = exchange(tile_rows.reshape(dp_count, 1, lane), DP)
    own_tile = jnp.minimum(own_layer * a_span + own_block % layer_blocks, tile_count - 1)
    tile_rows = lax.dynamic_slice_in_dim(
        tile_rows, own_tile // half_tiles * (dp_count // 2), dp_count // 2, 0
    )
    tile = tile_rows.reshape(row_count, width).astype(jnp.bfloat16)
    result = jnp.dot(tile, inverse, preferred_element_type=jnp.float32).astype(jnp.bfloat16)
    gathered = from_all(from_all(result, "z", z_count), "xc", xc_count)
    gathered = gathered.reshape(dp_count, row_count, width)
    tile_range = jnp.arange(tile_count, dtype=jnp.int32)
    place = positions(old_flat, tile_range // a_span * layer_blocks + tile_range % a_span)
    precond = jnp.take(gathered, place % xc_count * z_count + place // xc_count, axis=0)
    return (inverses, precond)


def solution(mesh):
    dp_count, mp_count = mesh.devices.shape
    parts = Mesh(
        mesh.devices.reshape(dp_count // X_CORE, X_CORE, mp_count), ("z", "xc", "mp")
    )
    in_specs = (P(DP, None, "mp", None), P(DP, None, "mp", None), P(), P())
    out_specs = (P(DP, None, "mp", None), P(None, "mp", None))
    return jax.shard_map(local, mesh=parts, in_specs=in_specs, out_specs=out_specs, check_vma=False)
```

time: 862 us -> 346 us (0.40)
  other arithmetic: 236 us -> 10.6 us
  waiting for transfers between devices: 341 us -> 158 us
  blocking collectives: 106 us -> 18.7 us
  matrix products: 51.2 us -> 0.38 us
  Pallas kernels: 0 us -> 47.5 us
  starting transfers between devices: 54.9 us -> 82.2 us
  between operations: 28.8 us -> 3.67 us
  local copies, waits for them, and re-layouts: 35.1 us -> 23.5 us
    another operation x38 -> x1, other arithmetic: 218 us -> 0.08 us  [local(): jnp.stack([(own >= 0).astype(jnp.int32), mp_index.astype(jnp.int32)])]
    all_gather x2 -> x0, waiting for transfers between devices: 132 us -> none  [the longest x1 132 us: local(): gathered = lax.all_gather(result, 'dp', axis=0, tiled=True)]
    psum x1 -> x0, blocking collectives: 106 us -> none  [local(): lax.psum(jnp.stack([input_terms, output_terms], axis=0), ('dp', 'mp'))]
    reduce_scatter x1 -> x0, waiting for transfers between devices: 90.3 us -> none  [local(): lax.psum_scatter(gradients[0].astype(jnp.float32), 'dp', scatter_dimensio...]
    pallas_call x0 -> x1, Pallas kernels: none -> 47.5 us  [invert(): pl.pallas_call(invert_kernel, out_shape=(jax.ShapeDtypeStruct((wide, n),...]
    dot_general x53 -> x1, matrix products: 45.8 us -> 0.38 us  [local(): jnp.dot(tile, inverse, preferred_element_type=jnp.float32)]
    all_to_all x3 -> x7, waiting for transfers between devices: 118 us -> 158 us  [exchange(): return lax.all_to_all(pieces, axes, split_axis=0, concat_axis=0, tiled=True)]
    all_to_all x0 -> x1, blocking collectives: none -> 18.7 us  [exchange(): return lax.all_to_all(pieces, axes, split_axis=0, concat_axis=0, tiled=True)]
  transfers between devices with their start and end apart: 6 -> 10, of which waited for: 5 -> 7; matrix products, arithmetic and copies ran while one was open for 2% -> 6% of each run, Pallas kernels for 0% -> 0%
where the time goes in v1:
time: 346 us; the launch traced here: 345 us
  waiting for transfers between devices  158 us (46%)
  starting transfers between devices  82.2 us (24%)
  Pallas kernels  47.5 us (14%)
  local copies, waits for them, and re-layouts  23.5 us (7%)
  blocking collectives  18.7 us (5%)
  other arithmetic  10.6 us (3%)
  between operations  3.67 us (1%)
    all_to_all x7, waiting for transfers between devices, exchange(): return lax.all_to_all(pieces, axes, split_axis=0, concat_axis=0, tiled=True)  158 us
    all_to_all x7, starting transfers between devices, exchange(): return lax.all_to_all(pieces, axes, split_axis=0, concat_axis=0, tiled=True)  71 us
    pallas_call x1, Pallas kernels, invert(): pl.pallas_call(invert_kernel, out_shape=(jax.ShapeDtypeStruct((wide, n),...  47.5 us
    all_to_all x1, blocking collectives, exchange(): return lax.all_to_all(pieces, axes, split_axis=0, concat_axis=0, tiled=True)  18.7 us
    ppermute x3, starting transfers between devices, from_next(): lax.ppermute(value, 'mp', [((i + step) % mp_count, i) for i in range(mp_c...  11.2 us
    unnamed x24, local copies, waits for them, and re-layouts  7.1 us
  transfers between devices with their start and end apart: 10, of which 7 were waited for; matrix products, arithmetic and copies ran while one was open for 6% of the time, Pallas kernels for 0%

profile of v1, /device:TPU:1, one launch (start us, length us, event | category | flops | bytes accessed | tf_op | source)
XLA Modules:
  0.0 345.0 jit_solution(17196166008798518629)
XLA Ops:
  0.6 1.2 fusion
  1.9 0.0 copy-start
  1.9 0.1 slice.25
  2.0 5.6 %collective-permute-start = (f32[256,512]{1,0:T(8,128)S(1)}, f32[256,512]{1,0:T(8,128)S(1)}, u32[]{:S(2)}, u32[]{:S(2)}) collective-permute-start(f32[256,512]{1,0:T(8,128)S(1)} %slice.25), channel_id=1, source_target_pairs={{1,0},{2,1},{3,2},{0,3},{5,4},{6,5},{7,6},{4,7},{9,8},{10,9},{11,1... | collective-permute-start | bytes 1572872 | tf_op jit(solution)/shard_map/ppermute | solution.py:227
  7.6 2.3 collective-permute-start.1
  9.8 0.7 fusion.15
  10.5 1.2 broadcast_in_dim_broadcast_in_dim_broadcast_in_dim.3
  11.7 3.9 %all-to-all-start = ((f32[4,1,128]{2,1,0:T(1,128)}), f32[4,1,128]{2,1,0:T(1,128)S(1)}, u32[]{:S(2)}, u32[]{:S(2)}) async-start(f32[4,1,128]{2,1,0:T(1,128)} %broadcast_in_dim_broadcast_in_dim_broadcast_in_dim.3), calls=%async_computation | async-start | bytes 4096 | tf_op jit(solution)/shard_map/all_to_all | solution.py:196
  15.6 0.9 pad_maximum_fusion
  16.4 3.4 collective-permute-start.2
  19.8 0.7 fusion.16
  21.2 2.0 all-to-all-done
  23.2 0.7 broadcast_in_dim.119
  23.9 26.7 %all-to-all-start.1 = ((f32[128,1,128]{2,1,0:T(1,128)}), f32[128,1,128]{2,1,0:T(1,128)S(1)}, u32[]{:S(2)}, u32[]{:S(2)}) async-start(f32[128,1,128]{2,1,0:T(1,128)} %broadcast_in_dim.119), calls=%async_computation.1 | async-start | bytes 131072 | tf_op jit(solution)/shard_map/all_to_all | solution.py:196
  50.6 0.1 pad_add_fusion.scalar_ref
  51.3 0.7 select_reduce_fusion.3
  52.0 13.3 %all-to-all-done.1 = f32[128,1,128]{2,1,0:T(1,128)S(1)} async-done(((f32[128,1,128]{2,1,0:T(1,128)}), f32[128,1,128]{2,1,0:T(1,128)S(1)}, u32[]{:S(2)}, u32[]{:S(2)}) %all-to-all-start.1) | async-done | bytes 65568 | tf_op jit(solution)/shard_map/all_to_all | solution.py:196
  65.4 1.0 slice_reduce_fusion
  66.4 0.1 fusion.1
  66.6 0.6 fusion.6
  68.5 0.0 collective-permute-done.one_ref
  68.5 0.0 copy-start.2
  68.5 0.8 copy-done.2
  69.3 0.0 collective-permute-done.1.two_ref
  69.3 0.8 copy-done.4
  70.1 0.0 collective-permute-done.2.three_ref
  70.1 0.8 copy-done.6
  70.9 1.0 copy-done.3
  72.0 1.0 copy-done.5
  73.0 1.0 copy-done.7
  74.1 47.5 %shard_map.59 = (bf16[256,1024]{1,0:T(8,128)(2,1)S(1)}, bf16[1024,1024]{1,0:T(8,128)(2,1)S(1)}) custom-call(s32[2]{0:T(128)S(1)} %pad_add_fusion.scalar_ref, f32[1]{0:T(128)} %bitcast.11.shift_ref, f32[256,1024]{1,0:T(8,128)S(1)} %bitcast.59, f32[256,512]{1,0:T(8,128)S(1)} %copy-done.3, f32[256,512]{1,0:T(8,128)S(1)} %copy-done.5, f32[256,512]{1,0:T(8,128)S(1)} %copy-done.7), custom_call_target="tpu_custom_call" | custom-call | flops 51539607552 | bytes 6291456 | tf_op jit(solution)/shard_map/pallas_call | solution.py:168
  121.6 0.0 copy-start.1
  121.6 0.8 copy-done.1
  122.4 2.0 reshape.246
  124.4 5.9 %all-to-all-start.2 = ((bf16[128,2,1024]{2,1,0:T(2,128)(2,1)}), bf16[128,2,1024]{2,1,0:T(2,128)(2,1)S(1)}, u32[]{:S(2)}, u32[]{:S(2)}) async-start(bf16[128,2,1024]{2,1,0:T(2,128)(2,1)} %reshape.246), calls=%async_computation.2 | async-start | bytes 1048576 | tf_op jit(solution)/shard_map/all_to_all | solution.py:196
  130.3 1.4 copy.17
  131.8 0.0 copy-start.11
  131.8 1.6 copy.18
  133.4 28.3 %all-to-all-done.2 = bf16[128,2,1024]{2,1,0:T(2,128)(2,1)S(1)} async-done(((bf16[128,2,1024]{2,1,0:T(2,128)(2,1)}), bf16[128,2,1024]{2,1,0:T(2,128)(2,1)S(1)}, u32[]{:S(2)}, u32[]{:S(2)}) %all-to-all-start.2) | async-done | bytes 524320 | tf_op jit(solution)/shard_map/all_to_all | solution.py:196
  161.6 0.8 copy-done.9
  162.4 8.8 %all-to-all-start.4 = ((bf16[128,28,128]{2,1,0:T(8,128)(2,1)}), bf16[128,28,128]{2,1,0:T(8,128)(2,1)S(1)}, u32[]{:S(2)}, u32[]{:S(2)}) async-start(bf16[128,28,128]{2,1,0:T(8,128)(2,1)} %copy.18), calls=%async_computation.4 | async-start | bytes 2097152 | tf_op jit(solution)/shard_map/all_to_all | solution.py:196
  171.2 0.2 select_reduce_fusion.1
  171.4 0.7 and_bitcast_fusion.1
  172.2 3.4 gather_fusion
  175.6 47.5 %all-to-all-done.4 = bf16[128,28,128]{2,1,0:T(8,128)(2,1)S(1)} async-done(((bf16[128,28,128]{2,1,0:T(8,128)(2,1)}), bf16[128,28,128]{2,1,0:T(8,128)(2,1)S(1)}, u32[]{:S(2)}, u32[]{:S(2)}) %all-to-all-start.4) | async-done | bytes 917536 | tf_op jit(solution)/shard_map/all_to_all | solution.py:196
  223.1 0.2 reduce_sum.88
  223.3 0.6 gather_fusion.1
  223.9 0.1 bitcast_select_fusion
  224.0 0.7 convert.5
  224.7 10.2 %all-to-all-start.5 = ((bf16[128,1,128]{2,1,0:T(2,128)(2,1)}), bf16[128,1,128]{2,1,0:T(2,128)(2,1)S(1)}, u32[]{:S(2)}, u32[]{:S(2)}) async-start(bf16[128,1,128]{2,1,0:T(2,128)(2,1)} %convert.5), calls=%async_computation.5 | async-start | bytes 131072 | tf_op jit(solution)/shard_map/all_to_all | solution.py:196
  234.9 2.4 broadcast_select_fusion
  237.3 12.4 %all-to-all-done.5 = bf16[128,1,128]{2,1,0:T(2,128)(2,1)S(1)} async-done(((bf16[128,1,128]{2,1,0:T(2,128)(2,1)}), bf16[128,1,128]{2,1,0:T(2,128)(2,1)S(1)}, u32[]{:S(2)}, u32[]{:S(2)}) %all-to-all-start.5) | async-done | bytes 32800 | tf_op jit(solution)/shard_map/all_to_all | solution.py:196
  249.7 5.7 %all-to-all-start.3 = ((bf16[128,2,1024]{2,1,0:T(2,128)(2,1)}), bf16[128,2,1024]{2,1,0:T(2,128)(2,1)S(1)}, u32[]{:S(2)}, u32[]{:S(2)}) async-start(bf16[128,2,1024]{2,1,0:T(2,128)(2,1)} %broadcast_select_fusion), calls=%async_computation.3 | async-start | bytes 1048576 | tf_op jit(solution)/shard_map/all_to_all | solution.py:196
  255.4 0.1 convert_reduce_fusion
  255.6 0.4 convolution_convert_fusion
  255.9 30.7 %all-to-all-done.3 = bf16[128,2,1024]{2,1,0:T(2,128)(2,1)S(1)} async-done(((bf16[128,2,1024]{2,1,0:T(2,128)(2,1)}), bf16[128,2,1024]{2,1,0:T(2,128)(2,1)S(1)}, u32[]{:S(2)}, u32[]{:S(2)}) %all-to-all-start.3) | async-done | bytes 524320 | tf_op jit(solution)/shard_map/all_to_all | solution.py:196
  286.7 18.7 %all_to_all.40 = bf16[16,8,1024]{2,1,0:T(8,128)(2,1)S(1)} all-to-all(bf16[16,8,1024]{2,1,0:T(8,128)(2,1)S(1)} %broadcast_in_dim.130), channel_id=1, replica_groups=mesh['z'=16,'xc'=8,'mp'=4] {'z'}, dimensions={0} | all-to-all | bytes 524288 | tf_op jit(solution)/shard_map/all_to_all | solution.py:196
  305.4 1.6 broadcast_in_dim.131
  307.0 9.9 %all-to-all-start.7 = ((bf16[8,16,8,1024]{3,2,1,0:T(8,128)(2,1)}), bf16[8,16,8,1024]{3,2,1,0:T(8,128)(2,1)S(1)}, u32[]{:S(2)}, u32[]{:S(2)}) async-start(bf16[8,16,8,1024]{3,2,1,0:T(8,128)(2,1)} %broadcast_in_dim.131), calls=%async_computation.7 | async-start | bytes 4194304 | tf_op jit(solution)/shard_map/all_to_all | solution.py:196
  316.9 0.2 select_reduce_fusion.2
  317.2 2.0 reshape.247
  319.2 24.1 %all-to-all-done.7 = bf16[8,16,8,1024]{3,2,1,0:T(8,128)(2,1)S(1)} async-done(((bf16[8,16,8,1024]{3,2,1,0:T(8,128)(2,1)}), bf16[8,16,8,1024]{3,2,1,0:T(8,128)(2,1)S(1)}, u32[]{:S(2)}, u32[]{:S(2)}) %all-to-all-start.7) | async-done | bytes 2097184 | tf_op jit(solution)/shard_map/all_to_all | solution.py:196
  343.3 0.6 gather_fusion.2
  343.9 1.1 broadcast_select_fusion.1
  (24 shorter events, 0.2 us)
Async XLA Ops:
  0.6 19.2 %copy-start.10 = (s32[128,1]{0,1:T(1,128)S(1)}, s32[128,1]{0,1:T(1,128)}, u32[]{:S(2)}) copy-start(s32[128,1]{0,1:T(1,128)} %param.6) | copy-start | bytes 1540
  1.9 69.0 %copy-start = (f32[1,1,256,1024]{3,2,1,0:T(8,128)S(1)}, f32[1,1,256,1024]{3,2,1,0:T(8,128)}, u32[]{:S(2)}) copy-start(f32[1,1,256,1024]{3,2,1,0:T(8,128)} %param.4) | copy-start | bytes 3145732
  2.0 66.6 %collective-permute-start = (f32[256,512]{1,0:T(8,128)S(1)}, f32[256,512]{1,0:T(8,128)S(1)}, u32[]{:S(2)}, u32[]{:S(2)}) collective-permute-start(f32[256,512]{1,0:T(8,128)S(1)} %slice.25), channel_id=1, source_target_pairs={{1,0},{2,1},{3,2},{0,3},{5,4},{6,5},{7,6},{4,7},{9,8},{10,9},{11,1... | collective-permute-start | bytes 1572872 | tf_op jit(solution)/shard_map/ppermute | solution.py:227
  7.6 61.8 %collective-permute-start.1 = (f32[256,512]{1,0:T(8,128)S(1)}, f32[256,512]{1,0:T(8,128)S(1)}, u32[]{:S(2)}, u32[]{:S(2)}) collective-permute-start(f32[256,512]{1,0:T(8,128)S(1)} %slice.25), channel_id=1, source_target_pairs={{2,0},{3,1},{0,2},{1,3},{6,4},{7,5},{4,6},{5,7},{10,8},{11,9},{8,1... | collective-permute-start | bytes 1572872 | tf_op jit(solution)/shard_map/ppermute | solution.py:227
  11.7 11.5 %all-to-all-start = ((f32[4,1,128]{2,1,0:T(1,128)}), f32[4,1,128]{2,1,0:T(1,128)S(1)}, u32[]{:S(2)}, u32[]{:S(2)}) async-start(f32[4,1,128]{2,1,0:T(1,128)} %broadcast_in_dim_broadcast_in_dim_broadcast_in_dim.3), calls=%async_computation | async-start | bytes 4096 | tf_op jit(solution)/shard_map/all_to_all | solution.py:196
  16.4 53.7 %collective-permute-start.2 = (f32[256,512]{1,0:T(8,128)}, f32[256,512]{1,0:T(8,128)S(1)}, u32[]{:S(2)}, u32[]{:S(2)}) collective-permute-start(f32[256,512]{1,0:T(8,128)} %pad_maximum_fusion), channel_id=1, source_target_pairs={{3,0},{0,1},{1,2},{2,3},{7,4},{4,5},{5,6},{6,7},{11,8},{8,9},{9,10... | collective-permute-start | bytes 1572872 | tf_op jit(solution)/shard_map/ppermute | solution.py:227
  23.9 41.5 %all-to-all-start.1 = ((f32[128,1,128]{2,1,0:T(1,128)}), f32[128,1,128]{2,1,0:T(1,128)S(1)}, u32[]{:S(2)}, u32[]{:S(2)}) async-start(f32[128,1,128]{2,1,0:T(1,128)} %broadcast_in_dim.119), calls=%async_computation.1 | async-start | bytes 131072 | tf_op jit(solution)/shard_map/all_to_all | solution.py:196
  68.5 0.8 copy-start.2
  69.3 0.8 copy-start.4
  70.1 0.8 copy-start.6
  70.9 1.0 copy-start.3
  72.0 1.0 copy-start.5
  73.0 1.0 copy-start.7
  121.6 0.8 copy-start.1
  124.4 37.2 %all-to-all-start.2 = ((bf16[128,2,1024]{2,1,0:T(2,128)(2,1)}), bf16[128,2,1024]{2,1,0:T(2,128)(2,1)S(1)}, u32[]{:S(2)}, u32[]{:S(2)}) async-start(bf16[128,2,1024]{2,1,0:T(2,128)(2,1)} %reshape.246), calls=%async_computation.2 | async-start | bytes 1048576 | tf_op jit(solution)/shard_map/all_to_all | solution.py:196
  131.8 39.4 %copy-start.11 = (s32[128,1]{0,1:T(1,128)S(1)}, s32[128,1]{0,1:T(1,128)}, u32[]{:S(2)}) copy-start(s32[128,1]{0,1:T(1,128)} %param.7) | copy-start | bytes 1540
  161.6 0.8 copy-start.9
  162.4 60.6 %all-to-all-start.4 = ((bf16[128,28,128]{2,1,0:T(8,128)(2,1)}), bf16[128,28,128]{2,1,0:T(8,128)(2,1)S(1)}, u32[]{:S(2)}, u32[]{:S(2)}) async-start(bf16[128,28,128]{2,1,0:T(8,128)(2,1)} %copy.18), calls=%async_computation.4 | async-start | bytes 2097152 | tf_op jit(solution)/shard_map/all_to_all | solution.py:196
  224.7 25.0 %all-to-all-start.5 = ((bf16[128,1,128]{2,1,0:T(2,128)(2,1)}), bf16[128,1,128]{2,1,0:T(2,128)(2,1)S(1)}, u32[]{:S(2)}, u32[]{:S(2)}) async-start(bf16[128,1,128]{2,1,0:T(2,128)(2,1)} %convert.5), calls=%async_computation.5 | async-start | bytes 131072 | tf_op jit(solution)/shard_map/all_to_all | solution.py:196
  249.7 37.0 %all-to-all-start.3 = ((bf16[128,2,1024]{2,1,0:T(2,128)(2,1)}), bf16[128,2,1024]{2,1,0:T(2,128)(2,1)S(1)}, u32[]{:S(2)}, u32[]{:S(2)}) async-start(bf16[128,2,1024]{2,1,0:T(2,128)(2,1)} %broadcast_select_fusion), calls=%async_computation.3 | async-start | bytes 1048576 | tf_op jit(solution)/shard_map/all_to_all | solution.py:196
  286.7 20.3 %copy-start.8 = (bf16[128,2,1024]{2,1,0:T(2,128)(2,1)}, bf16[128,2,1024]{2,1,0:T(2,128)(2,1)S(1)}, u32[]{:S(2)}) copy-start(bf16[128,2,1024]{2,1,0:T(2,128)(2,1)S(1)} %all-to-all-done.3) | copy-start | bytes 1572868
  307.0 36.3 %all-to-all-start.7 = ((bf16[8,16,8,1024]{3,2,1,0:T(8,128)(2,1)}), bf16[8,16,8,1024]{3,2,1,0:T(8,128)(2,1)S(1)}, u32[]{:S(2)}, u32[]{:S(2)}) async-start(bf16[8,16,8,1024]{3,2,1,0:T(8,128)(2,1)} %broadcast_in_dim.131), calls=%async_computation.7 | async-start | bytes 4194304 | tf_op jit(solution)/shard_map/all_to_all | solution.py:196

commit v2 on v1

v2 whole, which is shorter than its diff:
```python
import jax
import jax.numpy as jnp
from jax import lax
from jax.experimental import pallas as pl
from jax.experimental.pallas import tpu as pltpu
from jax.sharding import Mesh, PartitionSpec as P

D = 8192
FF = 28672
DAMPING_BASE = 2.0
X_COUNT, CORES = 4, 2
DP = ("z", "x", "c")

BASE = 128
SUB = 8
ROWS, LANES = 16, 128


def row_of(x, j):
    return jnp.broadcast_to(x[j : j + 1, :], x.shape)


def lane_of(x, j):
    return jnp.broadcast_to(x[:, j : j + 1], x.shape)


def reciprocal(x):
    return pltpu.reciprocal(x, approx=True)


def base_sweep(load, store):
    count = BASE // SUB
    groups = [load(i) for i in range(count)]
    sub_ids = lax.broadcasted_iota(jnp.int32, (SUB, BASE), 0)
    lane_ids = lax.broadcasted_iota(jnp.int32, (SUB, BASE), 1)
    for p in range(count):
        pivot_lanes = (lane_ids // SUB) == p
        spread = [lane_of(groups[p], p * SUB + j) for j in range(SUB)]
        rows = jnp.where(pivot_lanes, jnp.where(lane_ids == sub_ids + p * SUB, 1.0, 0.0), groups[p])
        pivot = row_of(spread[0], 0)
        for j in range(SUB):
            here = sub_ids == j
            scale = reciprocal(pivot)
            if j + 1 < SUB:
                cross = row_of(spread[j], j + 1) * row_of(spread[j + 1], j)
                pivot = row_of(spread[j + 1], j + 1) - cross * scale
            column = jnp.where(here, -1.0, spread[j])

            def eliminate(x):
                line = row_of(x, j)
                return jnp.where(here, 0.0, x) - (column * line) * scale

            rows = eliminate(rows)
            for i in range(j + 1, SUB):
                spread[i] = eliminate(spread[i])
        rows = jnp.where(pivot_lanes, -rows, rows)
        lines = [row_of(rows, j) for j in range(SUB)]
        for step in range(1, count):
            i = (p + step) % count
            terms = [lane_of(groups[i], p * SUB + j) * lines[j] for j in range(SUB)]
            while len(terms) > 1:
                terms = [a + b for a, b in zip(terms[::2], terms[1::2])]
            groups[i] = jnp.where(pivot_lanes, 0.0, groups[i]) - terms[0]
        groups[p] = rows
    for i in range(count):
        store(i, groups[i])


def halves(x):
    high = x.astype(jnp.bfloat16)
    return high, (x - high.astype(jnp.float32)).astype(jnp.bfloat16)


def dot3(left, right):
    def one(a, b):
        return jnp.dot(a, b, preferred_element_type=jnp.float32)

    return one(left[0], right[0]) + (one(left[0], right[1]) + one(left[1], right[0]))


def invert_kernel(
    scalar_ref, shift_ref, rows_ref, one_ref, two_ref, three_ref,
    band_ref, full_ref, m_ref, d_ref, th_ref, tl_ref,
):
    n = rows_ref.shape[1]
    wide = rows_ref.shape[0]
    count = n // wide
    mp_index = scalar_ref[1]

    def block(i):
        return slice(i * wide, (i + 1) * wide)

    def place(i):
        return pl.ds(pl.multiple_of(lax.rem(mp_index + i, count) * wide, wide), wide)

    @pl.when(scalar_ref[0] > 0)
    def _():
        eye = jnp.where(
            lax.broadcasted_iota(jnp.int32, (wide, wide), 0)
            == lax.broadcasted_iota(jnp.int32, (wide, wide), 1),
            shift_ref[0],
            0.0,
        )

        def put(i, j, value):
            if i == j:
                m_ref[block(i), block(i)] = value + eye
            else:
                m_ref[block(i), block(j)] = value
                m_ref[block(j), block(i)] = value.T

        for j in range(count):
            put(0, j, rows_ref[:, place(j)])
        put(1, 1, one_ref[:, block(0)])
        put(1, 2, one_ref[:, block(1)])
        put(2, 2, two_ref[:, block(0)])
        put(2, 3, two_ref[:, block(1)])
        put(3, 3, three_ref[:, block(0)])
        put(3, 1, three_ref[:, block(1)])

        @pl.loop(0, count)
        def _(k):
            at = pl.ds(pl.multiple_of(k * wide, wide), wide)

            d_ref[...] = m_ref[at, at]

            def sweep_half(h):
                lo = h * BASE
                base_sweep(
                    lambda i: d_ref[lo + i * SUB : lo + (i + 1) * SUB, lo : lo + BASE],
                    lambda i, v: d_ref.__setitem__(
                        (slice(lo + i * SUB, lo + (i + 1) * SUB), slice(lo, lo + BASE)), v
                    ),
                )

            one, two = slice(0, BASE), slice(BASE, wide)
            sweep_half(0)
            minus_p = halves(d_ref[one, one])
            cross = halves(d_ref[one, two])
            cross_t = halves(d_ref[two, one])
            t_halves = halves(-dot3(minus_p, cross))
            d_ref[two, two] = d_ref[two, two] - dot3(cross_t, t_halves)
            left = halves(-dot3(cross_t, minus_p))
            sweep_half(1)
            minus_p = halves(d_ref[two, two])
            up = dot3(t_halves, minus_p)
            d_ref[one, one] = d_ref[one, one] + dot3(halves(up), left)
            d_ref[one, two] = -up
            d_ref[two, one] = -dot3(minus_p, left)

            minus_p = halves(d_ref[...])
            col_h, col_l = halves(m_ref[:, at])
            rows = -dot3(minus_p, halves(m_ref[at, :]))
            m_ref[:, at] = jnp.zeros((n, wide), jnp.float32)
            m_ref[at, :] = rows
            m_ref[at, at] = d_ref[...]
            th_ref[...], tl_ref[...] = halves(m_ref[at, :])
            for i in range(count):

                @pl.when(i != k)
                def _():
                    m_ref[block(i), :] = m_ref[block(i), :] - dot3(
                        (col_h[block(i)], col_l[block(i)]), (th_ref[...], tl_ref[...])
                    )

        for j in range(count):
            band = (-m_ref[block(0), block(j)]).astype(jnp.bfloat16)
            for r in range(wide // ROWS):
                for c in range(wide // LANES):
                    at = lax.rem(mp_index + j, count) * (wide // LANES) + r * (n // LANES) + c
                    band_ref[at] = band[r * ROWS : (r + 1) * ROWS, c * LANES : (c + 1) * LANES]
            for i in range(count):
                full_ref[place(i), place(j)] = (-m_ref[block(i), block(j)]).astype(jnp.bfloat16)

    @pl.when(scalar_ref[0] <= 0)
    def _():
        band_ref[...] = jnp.zeros(band_ref.shape, jnp.bfloat16)
        full_ref[...] = jnp.zeros(full_ref.shape, jnp.bfloat16)


def invert(scalars, shift, rows, one, two, three):
    wide, n = rows.shape
    in_smem = pl.BlockSpec(memory_space=pltpu.SMEM)
    in_vmem = pl.BlockSpec(memory_space=pltpu.VMEM)
    return pl.pallas_call(
        invert_kernel,
        out_shape=(
            jax.ShapeDtypeStruct((wide * n // (ROWS * LANES), ROWS, LANES), jnp.bfloat16),
            jax.ShapeDtypeStruct((n, n), jnp.bfloat16),
        ),
        in_specs=[in_smem] * 2 + [in_vmem] * 4,
        out_specs=(in_vmem, in_vmem),
        scratch_shapes=[
            pltpu.VMEM((n, n), jnp.float32),
            pltpu.VMEM((wide, wide), jnp.float32),
            pltpu.VMEM((wide, n), jnp.bfloat16),
            pltpu.VMEM((wide, n), jnp.bfloat16),
        ],
        compiler_params=pltpu.CompilerParams(vmem_limit_bytes=24 * 1024 * 1024),
        cost_estimate=pl.CostEstimate(
            flops=36 * n * n * n, bytes_accessed=6 * n * n, transcendentals=0
        ),
    )(scalars, shift, rows, one, two, three)


def pick_kernel(index_ref, src_ref, out_ref):
    @pl.loop(0, out_ref.shape[0], unroll=8)
    def _(i):
        out_ref[i] = src_ref[index_ref[i]]


def pick(index, source):
    in_vmem = pl.BlockSpec(memory_space=pltpu.VMEM)
    return pl.pallas_call(
        pick_kernel,
        out_shape=jax.ShapeDtypeStruct(index.shape + source.shape[1:], source.dtype),
        in_specs=[pl.BlockSpec(memory_space=pltpu.SMEM), in_vmem],
        out_specs=in_vmem,
        compiler_params=pltpu.CompilerParams(vmem_limit_bytes=4 * 1024 * 1024),
    )(index, source)


def take(source, index):
    return source.at[index].get(mode="promise_in_bounds")


def positions(slot_ids, wanted):
    slot_range = jnp.arange(slot_ids.shape[0], dtype=jnp.int32)
    hit = slot_ids[None, :] == wanted[:, None]
    return jnp.sum(jnp.where(hit, slot_range[None, :], 0), axis=1).astype(jnp.int32)


def exchange(pieces, axes):
    return lax.all_to_all(pieces, axes, split_axis=0, concat_axis=0, tiled=True)


def from_ahead(value, axis, step):
    count = lax.axis_size(axis)
    return lax.ppermute(value, axis, [((i + step) % count, i) for i in range(count)])


def sum_of_all(value, axes, count):
    return jnp.sum(exchange(jnp.broadcast_to(value[None], (count,) + value.shape), axes), axis=0)


def local(old_factors, gradients, old_slots, new_slots):
    mp_index = lax.axis_index("mp")
    mp_count = lax.axis_size("mp")
    z_count, x_count, c_count = lax.axis_size("z"), lax.axis_size("x"), lax.axis_size("c")
    z, x, c = lax.axis_index("z"), lax.axis_index("x"), lax.axis_index("c")
    dp_count = z_count * x_count * c_count
    dp_index = (z * x_count + x) * c_count + c
    band, width = old_factors.shape[2:]
    tile_count, row_count = gradients.shape[1:3]
    a_span = FF // width
    layer_blocks = a_span + D // width
    layers = tile_count // a_span
    old_flat = old_slots.reshape(dp_count)
    new_flat = new_slots.reshape(dp_count)
    own = lax.dynamic_index_in_dim(old_flat, dp_index, keepdims=False)
    own_block = jnp.maximum(own, 0)
    own_layer = own_block // layer_blocks
    own_input = own_block % layer_blocks < a_span

    rows = old_factors[0, 0]
    trace = jnp.trace(lax.dynamic_slice_in_dim(rows, mp_index * band, band, 1))
    bins = lax.broadcasted_iota(jnp.int32, (1, 128), 1)
    own_bin = jnp.where(own >= 0, 2 * own_layer + jnp.where(own_input, 0, 1), -1)
    binned = jnp.where(bins == own_bin, trace, 0.0)
    binned = sum_of_all(binned, ("x", "c", "mp"), x_count * c_count * mp_count)
    binned = sum_of_all(binned, "z", z_count)
    trace_input = jnp.sum(jnp.where(bins == 2 * own_layer, binned, 0.0))
    trace_output = jnp.sum(jnp.where(bins == 2 * own_layer + 1, binned, 0.0))
    ratio = jnp.sqrt(trace_input / FF / (trace_output / D))
    shift = jnp.where(own_input, DAMPING_BASE * ratio, DAMPING_BASE / ratio)

    doubled = jnp.concatenate([rows, rows], axis=1)
    ahead = lax.dynamic_slice_in_dim(doubled, mp_index * band, 3 * band, 1)
    near = ahead[:, : 2 * band]
    far = jnp.concatenate([ahead[:, :band], ahead[:, 2 * band :]], axis=1)
    one = from_ahead(near, "mp", 1)
    two = from_ahead(near, "mp", 2)
    three = from_ahead(far, "mp", 3)

    block = jnp.maximum(old_flat, 0)
    tile_of = jnp.minimum(block // layer_blocks * a_span + block % layer_blocks, tile_count - 1)
    tile_of = tile_of.reshape(z_count, x_count, c_count).transpose(2, 1, 0)

    def tiles_of(core):
        index = lax.dynamic_index_in_dim(tile_of, core, keepdims=False)
        return take(gradients[0], index.reshape(-1))

    def split(value):
        return value.astype(jnp.float32).reshape(x_count, z_count, row_count, width)

    arrived = from_ahead(tiles_of(1 - c), "c", 1)
    partial = split(tiles_of(c)) + split(arrived)
    total = lax.dynamic_index_in_dim(partial, x, keepdims=False)
    for step in range(1, x_count):
        piece = lax.dynamic_index_in_dim(partial, (x + x_count - step) % x_count, keepdims=False)
        total = total + from_ahead(piece, "x", step)
    shift, total = lax.optimization_barrier((shift, total))
    tile = jnp.sum(exchange(total, "z"), axis=0).astype(jnp.bfloat16)

    scalars = jnp.stack([(own >= 0).astype(jnp.int32), mp_index.astype(jnp.int32)])
    inverse_band, inverse = invert(scalars, shift.reshape(1), rows, one, two, three)
    inverse_band, tile = lax.optimization_barrier((inverse_band, tile))

    spread = exchange(inverse_band, DP)
    slot_range = jnp.arange(dp_count, dtype=jnp.int32)
    empty = jnp.min(jnp.where(old_flat >= 0, dp_count - 1, slot_range))
    source = jnp.where(new_flat >= 0, positions(old_flat, new_flat), empty)
    arrived = exchange(pick(source, spread), DP)
    arrived = arrived.reshape(band // ROWS, width // LANES, ROWS, LANES)
    inverses = arrived.transpose(0, 2, 1, 3).reshape(1, 1, band, width)

    held = jnp.dot(tile, inverse, preferred_element_type=jnp.float32).astype(jnp.bfloat16)
    for axis, steps in (("z", (4, 8, 12)), ("z", (1, 2, 15)), ("x", (1, 2, 3)), ("c", (1,))):
        held = jnp.stack([held] + [from_ahead(held, axis, step) for step in steps])
    held = held.reshape(dp_count, row_count, width)
    tile_range = jnp.arange(tile_count, dtype=jnp.int32)
    place = positions(old_flat, tile_range // a_span * layer_blocks + tile_range % a_span)
    far_z = (place // (x_count * c_count) - z + z_count) % z_count
    far_x = (place // c_count - x + x_count) % x_count
    far_c = (place - c + c_count) % c_count
    low = far_z % 4
    high = (far_z + jnp.where(low == 3, 1, 0)) // 4 % 4
    precond = take(held, ((far_c * x_count + far_x) * 4 + low) * 4 + high)
    return (inverses, precond)


def solution(mesh):
    dp_count, mp_count = mesh.devices.shape
    z_count = dp_count // (X_COUNT * CORES)
    parts = Mesh(
        mesh.devices.reshape(z_count, X_COUNT, CORES, mp_count), DP + ("mp",)
    )
    in_specs = (P(DP, None, "mp", None), P(DP, None, "mp", None), P(), P())
    out_specs = (P(DP, None, "mp", None), P(None, "mp", None))
    return jax.shard_map(local, mesh=parts, in_specs=in_specs, out_specs=out_specs, check_vma=False)
```

time: 346 us -> 287 us (0.83)
  starting transfers between devices: 82.2 us -> 157 us
  waiting for transfers between devices: 158 us -> 91.3 us
  Pallas kernels: 47.5 us -> 2.49 us
  blocking collectives: 18.7 us -> 0 us
  local copies, waits for them, and re-layouts: 23.5 us -> 15.4 us
    all_to_all x7 -> x5, waiting for transfers between devices: 158 us -> 62.5 us  [exchange(): return lax.all_to_all(pieces, axes, split_axis=0, concat_axis=0, tiled=True)]
    ppermute x3 -> x17, starting transfers between devices: 11.2 us -> 65.8 us  [from_ahead(): lax.ppermute(value, axis, [((i + step) % count, i) for i in range(count)])]
    pallas_call x1 -> x2, Pallas kernels: 47.5 us -> 2.49 us  [the longest x1 1.55 us: pick(): pl.pallas_call(pick_kernel, out_shape=jax.ShapeDtypeStruct(index.shape +...]
    ppermute x3 -> x17, waiting for transfers between devices: 0.01 us -> 28.8 us  [from_ahead(): lax.ppermute(value, axis, [((i + step) % count, i) for i in range(count)])]
    all_to_all x7 -> x5, starting transfers between devices: 71 us -> 91 us  [exchange(): return lax.all_to_all(pieces, axes, split_axis=0, concat_axis=0, tiled=True)]
    all_to_all x1 -> x0, blocking collectives: 18.7 us -> none  [exchange(): return lax.all_to_all(pieces, axes, split_axis=0, concat_axis=0, tiled=True)]
    add x0 -> x2, other arithmetic: none -> 5.41 us  [the longest x1 2.94 us: local(): partial = split(tiles_of(c)) + split(arrived)]
    reshape x3, local copies, waits for them, and re-layouts: 5.64 us -> 1.19 us  [the longest x1 1.02 us: local(): inverses = arrived.transpose(0, 2, 1, 3).reshape(1, 1, band, width)]
  transfers between devices with their start and end apart: 10 -> 22, of which waited for: 7 -> 13; matrix products, arithmetic and copies ran while one was open for 6% -> 5% of each run, Pallas kernels for 0% -> 0%
where the time goes in v2:
time: 287 us; the launch traced here: 285 us
  starting transfers between devices  157 us (55%)
  waiting for transfers between devices  91.3 us (32%)
  local copies, waits for them, and re-layouts  15.4 us (5%)
  other arithmetic  13.8 us (5%)
  between operations  4.56 us (2%)
    all_to_all x5, starting transfers between devices, exchange(): return lax.all_to_all(pieces, axes, split_axis=0, concat_axis=0, tiled=True)  91 us
    ppermute x17, starting transfers between devices, from_ahead(): lax.ppermute(value, axis, [((i + step) % count, i) for i in range(count)])  65.8 us
    all_to_all x5, waiting for transfers between devices, exchange(): return lax.all_to_all(pieces, axes, split_axis=0, concat_axis=0, tiled=True)  62.5 us
    ppermute x17, waiting for transfers between devices, from_ahead(): lax.ppermute(value, axis, [((i + step) % count, i) for i in range(count)])  28.8 us
  transfers between devices with their start and end apart: 22, of which 13 were waited for; matrix products, arithmetic and copies ran while one was open for 5% of the time, Pallas kernels for 0%

profile of v2, /device:TPU:1, one launch (start us, length us, event | category | flops | bytes accessed | tf_op | source)
XLA Modules:
  0.0 285.4 jit_solution(9283222774030847121)
XLA Ops:
  0.6 0.8 remainder_reduce_fusion
  1.4 0.7 compare_reduce_fusion
  3.1 0.6 gather_fusion.1
  3.8 8.8 %collective-permute-start = (bf16[64,8,1024]{2,1,0:T(8,128)(2,1)S(1)}, bf16[64,8,1024]{2,1,0:T(8,128)(2,1)}, u32[]{:S(2)}, u32[]{:S(2)}) collective-permute-start(bf16[64,8,1024]{2,1,0:T(8,128)(2,1)S(1)} %gather_fusion.1), channel_id=1, source_target_pairs={{4,0},{0,4},{5,1},{1,5},{6,2},{2,6},{7,3},{3,7},{12,8},{8,12},{13,... | collective-permute-start | bytes 3145736 | tf_op jit(solution)/shard_map/ppermute | solution.py:239
  12.6 0.6 gather_fusion
  13.3 1.7 collective-permute-done
  15.0 2.9 %convert_add_fusion = f32[64,8,1024]{2,1,0:T(8,128)} fusion(bf16[64,8,1024]{2,1,0:T(8,128)(2,1)} %collective-permute-done, bf16[64,8,1024]{2,1,0:T(8,128)(2,1)S(1)} %gather_fusion), kind=kLoop, calls=%fused_computation.6 | loop fusion | flops 1572864 | bytes 4194304 | tf_op jit(solution)/shard_map/add | solution.py:297
  17.9 2.6 dynamic-slice_bitcast_fusion.2
  20.5 2.0 collective-permute-start.1
  22.6 0.2 fusion
  22.8 0.9 slice.18
  23.7 1.9 collective-permute-start.4
  25.6 2.1 collective-permute-start.5
  27.7 2.4 collective-permute-start.2
  30.1 2.7 collective-permute-start.3
  32.9 0.7 fusion.29
  34.8 0.7 fusion.3
  35.6 0.4 collective-permute-done.1
  36.0 3.0 %collective-permute-start.6 = (f32[256,512]{1,0:T(8,128)S(1)}, f32[256,512]{1,0:T(8,128)S(1)}, u32[]{:S(2)}, u32[]{:S(2)}) collective-permute-start(f32[256,512]{1,0:T(8,128)S(1)} %pad_maximum_fusion.2), channel_id=1, source_target_pairs={{3,0},{0,1},{1,2},{2,3},{7,4},{4,5},{5,6},{6,7},{11,8},{8,9},{9,10... | collective-permute-start | bytes 1572872 | tf_op jit(solution)/shard_map/ppermute | solution.py:239
  39.0 0.6 compare_select_fusion.15
  39.6 0.6 broadcast_in_dim.76
  40.2 14.0 %all-to-all-start = ((f32[32,1,128]{2,1,0:T(1,128)}), f32[32,1,128]{2,1,0:T(1,128)S(1)}, u32[]{:S(2)}, u32[]{:S(2)}) async-start(f32[32,1,128]{2,1,0:T(1,128)} %broadcast_in_dim.76), calls=%async_computation | async-start | bytes 32768 | tf_op jit(solution)/shard_map/all_to_all | solution.py:234
  54.9 6.2 %all-to-all-done = f32[32,1,128]{2,1,0:T(1,128)S(1)} async-done(((f32[32,1,128]{2,1,0:T(1,128)}), f32[32,1,128]{2,1,0:T(1,128)S(1)}, u32[]{:S(2)}, u32[]{:S(2)}) %all-to-all-start) | async-done | bytes 16416 | tf_op jit(solution)/shard_map/all_to_all | solution.py:234
  61.2 0.6 broadcast_in_dim.77
  61.8 16.2 %all-to-all-start.1 = ((f32[16,1,128]{2,1,0:T(1,128)}), f32[16,1,128]{2,1,0:T(1,128)S(1)}, u32[]{:S(2)}, u32[]{:S(2)}) async-start(f32[16,1,128]{2,1,0:T(1,128)} %broadcast_in_dim.77), calls=%async_computation.1 | async-start | bytes 16384 | tf_op jit(solution)/shard_map/all_to_all | solution.py:234
  78.0 11.1 %all-to-all-done.1 = f32[16,1,128]{2,1,0:T(1,128)S(1)} async-done(((f32[16,1,128]{2,1,0:T(1,128)}), f32[16,1,128]{2,1,0:T(1,128)S(1)}, u32[]{:S(2)}, u32[]{:S(2)}) %all-to-all-start.1) | async-done | bytes 8224 | tf_op jit(solution)/shard_map/all_to_all | solution.py:234
  89.2 0.7 fusion.13
  91.4 2.5 fusion.2
  93.9 4.2 %all-to-all-start.2 = ((f32[16,8,1024]{2,1,0:T(8,128)}), f32[16,8,1024]{2,1,0:T(8,128)}, u32[]{:S(2)}, u32[]{:S(2)}) async-start(f32[16,8,1024]{2,1,0:T(8,128)} %fusion.2), calls=%async_computation.2 | async-start | bytes 1048576 | tf_op jit(solution)/shard_map/all_to_all | solution.py:234
  98.1 0.8 copy-done.6
  98.9 0.8 copy-done.4
  99.7 1.2 copy-done.2
  101.0 1.0 copy-done.5
  102.0 1.0 copy-done.7
  103.0 0.9 shard_map.59
  104.0 0.8 copy-done.3
  104.8 15.8 %all-to-all-done.2 = f32[16,8,1024]{2,1,0:T(8,128)} async-done(((f32[16,8,1024]{2,1,0:T(8,128)}), f32[16,8,1024]{2,1,0:T(8,128)}, u32[]{:S(2)}, u32[]{:S(2)}) %all-to-all-start.2) | async-done | bytes 524320 | tf_op jit(solution)/shard_map/all_to_all | solution.py:234
  120.6 1.7 reduce_sum.81
  122.3 47.5 %all-to-all-start.3 = ((bf16[128,16,128]{2,1,0:T(8,128)(2,1)}), bf16[128,16,128]{2,1,0:T(8,128)(2,1)S(1)}, u32[]{:S(2)}, u32[]{:S(2)}) async-start(bf16[128,16,128]{2,1,0:T(8,128)(2,1)} %copy-done.3), calls=%async_computation.3 | async-start | bytes 1048576 | tf_op jit(solution)/shard_map/all_to_all | solution.py:234
  169.8 0.7 fusion.11
  170.6 0.6 compare_select_fusion.18.index_ref
  171.3 29.3 %all-to-all-done.3.src_ref = bf16[128,16,128]{2,1,0:T(8,128)(2,1)S(1)} async-done(((bf16[128,16,128]{2,1,0:T(8,128)(2,1)}), bf16[128,16,128]{2,1,0:T(8,128)(2,1)S(1)}, u32[]{:S(2)}, u32[]{:S(2)}) %all-to-all-start.3) | async-done | bytes 524320 | tf_op jit(solution)/shard_map/all_to_all | solution.py:234
  200.6 1.6 shard_map.60
  202.2 9.1 %all-to-all-start.4 = ((bf16[128,16,128]{2,1,0:T(8,128)(2,1)}), bf16[128,16,128]{2,1,0:T(8,128)(2,1)S(1)}, u32[]{:S(2)}, u32[]{:S(2)}) async-start(bf16[128,16,128]{2,1,0:T(8,128)(2,1)} %shard_map.60), calls=%async_computation.4 | async-start | bytes 1048576 | tf_op jit(solution)/shard_map/all_to_all | solution.py:234
  211.3 1.1 convolution_convert_fusion
  212.4 7.7 %collective-permute-start.7 = (bf16[8,1024]{1,0:T(8,128)(2,1)S(1)}, bf16[8,1024]{1,0:T(8,128)(2,1)S(1)}, u32[]{:S(2)}, u32[]{:S(2)}) collective-permute-start(bf16[8,1024]{1,0:T(8,128)(2,1)S(1)} %convolution_convert_fusion), channel_id=1, source_target_pairs={{128,0},{160,32},{192,64},{224,96},{256,128},{288,160},{320,192},{... | collective-permute-start | bytes 49160 | tf_op jit(solution)/shard_map/ppermute | solution.py:239
  220.1 6.6 %collective-permute-start.8 = (bf16[8,1024]{1,0:T(8,128)(2,1)S(1)}, bf16[8,1024]{1,0:T(8,128)(2,1)S(1)}, u32[]{:S(2)}, u32[]{:S(2)}) collective-permute-start(bf16[8,1024]{1,0:T(8,128)(2,1)S(1)} %convolution_convert_fusion), channel_id=1, source_target_pairs={{256,0},{288,32},{320,64},{352,96},{384,128},{416,160},{448,192},{... | collective-permute-start | bytes 49160 | tf_op jit(solution)/shard_map/ppermute | solution.py:239
  226.7 7.2 %collective-permute-start.9 = (bf16[8,1024]{1,0:T(8,128)(2,1)S(1)}, bf16[8,1024]{1,0:T(8,128)(2,1)S(1)}, u32[]{:S(2)}, u32[]{:S(2)}) collective-permute-start(bf16[8,1024]{1,0:T(8,128)(2,1)S(1)} %convolution_convert_fusion), channel_id=1, source_target_pairs={{384,0},{416,32},{448,64},{480,96},{0,128},{32,160},{64,192},{96,2... | collective-permute-start | bytes 49160 | tf_op jit(solution)/shard_map/ppermute | solution.py:239
  233.9 2.7 collective-permute-done.7
  236.6 9.1 %collective-permute-done.8 = bf16[8,1024]{1,0:T(8,128)(2,1)S(1)} collective-permute-done((bf16[8,1024]{1,0:T(8,128)(2,1)S(1)}, bf16[8,1024]{1,0:T(8,128)(2,1)S(1)}, u32[]{:S(2)}, u32[]{:S(2)}) %collective-permute-start.8) | collective-permute-done | bytes 16416 | tf_op jit(solution)/shard_map/ppermute | solution.py:239
  245.7 1.9 collective-permute-start.10
  247.6 2.6 collective-permute-start.11
  250.2 3.4 %collective-permute-start.12 = (bf16[4,8,1024]{2,1,0:T(8,128)(2,1)S(1)}, bf16[4,8,1024]{2,1,0:T(8,128)(2,1)S(1)}, u32[]{:S(2)}, u32[]{:S(2)}) collective-permute-start(bf16[4,8,1024]{2,1,0:T(8,128)(2,1)S(1)} %get-tuple-element.28), channel_id=1, source_target_pairs={{480,0},{0,32},{32,64},{64,96},{96,128},{128,160},{160,192},{192,2... | collective-permute-start | bytes 196616 | tf_op jit(solution)/shard_map/ppermute | solution.py:239
  253.7 2.8 collective-permute-done.12
  256.5 3.9 %collective-permute-start.13 = (bf16[4,4,8,1024]{3,2,1,0:T(8,128)(2,1)S(1)}, bf16[4,4,8,1024]{3,2,1,0:T(8,128)(2,1)S(1)}, u32[]{:S(2)}, u32[]{:S(2)}) collective-permute-start(bf16[4,4,8,1024]{3,2,1,0:T(8,128)(2,1)S(1)} %get-tuple-element.26), channel_id=1, source_target_pairs={{8,0},{16,8},{24,16},{0,24},{9,1},{17,9},{25,17},{1,25},{10,2},{18... | collective-permute-start | bytes 786440 | tf_op jit(solution)/shard_map/ppermute | solution.py:239
  260.4 3.0 %collective-permute-start.14 = (bf16[4,4,8,1024]{3,2,1,0:T(8,128)(2,1)S(1)}, bf16[4,4,8,1024]{3,2,1,0:T(8,128)(2,1)S(1)}, u32[]{:S(2)}, u32[]{:S(2)}) collective-permute-start(bf16[4,4,8,1024]{3,2,1,0:T(8,128)(2,1)S(1)} %get-tuple-element.26), channel_id=1, source_target_pairs={{16,0},{24,8},{0,16},{8,24},{17,1},{25,9},{1,17},{9,25},{18,2},{26... | collective-permute-start | bytes 786440 | tf_op jit(solution)/shard_map/ppermute | solution.py:239
  263.4 2.2 collective-permute-start.15
  265.6 3.4 %collective-permute-done.14 = bf16[4,4,8,1024]{3,2,1,0:T(8,128)(2,1)S(1)} collective-permute-done((bf16[4,4,8,1024]{3,2,1,0:T(8,128)(2,1)S(1)}, bf16[4,4,8,1024]{3,2,1,0:T(8,128)(2,1)S(1)}, u32[]{:S(2)}, u32[]{:S(2)}) %collective-permute-start.14) | collective-permute-done | bytes 262176 | tf_op jit(solution)/shard_map/ppermute | solution.py:239
  269.1 6.6 %collective-permute-done.15 = bf16[4,4,8,1024]{3,2,1,0:T(8,128)(2,1)S(1)} collective-permute-done((bf16[4,4,8,1024]{3,2,1,0:T(8,128)(2,1)S(1)}, bf16[4,4,8,1024]{3,2,1,0:T(8,128)(2,1)S(1)}, u32[]{:S(2)}, u32[]{:S(2)}) %collective-permute-start.15) | collective-permute-done | bytes 262176 | tf_op jit(solution)/shard_map/ppermute | solution.py:239
  275.9 4.4 %collective-permute-start.16 = (bf16[4,4,4,8,1024]{4,3,2,1,0:T(8,128)(2,1)S(1)}, bf16[4,4,4,8,1024]{4,3,2,1,0:T(8,128)(2,1)S(1)}, u32[]{:S(2)}, u32[]{:S(2)}) collective-permute-start(bf16[4,4,4,8,1024]{4,3,2,1,0:T(8,128)(2,1)S(1)} %get-tuple-element.22), channel_id=1, source_target_pairs={{4,0},{0,4},{5,1},{1,5},{6,2},{2,6},{7,3},{3,7},{12,8},{8,12},{13,... | collective-permute-start | bytes 3145736 | tf_op jit(solution)/shard_map/ppermute | solution.py:239
  280.5 2.0 collective-permute-done.16
  282.5 0.2 pad_maximum_fusion
  282.7 1.6 gather_fusion.2
  284.4 1.0 reshape.517
  (50 shorter events, 2.1 us)
Async XLA Ops:
  0.6 2.5 copy-start
  3.8 11.2 %collective-permute-start = (bf16[64,8,1024]{2,1,0:T(8,128)(2,1)S(1)}, bf16[64,8,1024]{2,1,0:T(8,128)(2,1)}, u32[]{:S(2)}, u32[]{:S(2)}) collective-permute-start(bf16[64,8,1024]{2,1,0:T(8,128)(2,1)S(1)} %gather_fusion.1), channel_id=1, source_target_pairs={{4,0},{0,4},{5,1},{1,5},{6,2},{2,6},{7,3},{3,7},{12,8},{8,12},{13,... | collective-permute-start | bytes 3145736 | tf_op jit(solution)/shard_map/ppermute | solution.py:239
  17.9 4.7 %copy-start.1 = (f32[1,1,256,1024]{3,2,1,0:T(8,128)S(1)}, f32[1,1,256,1024]{3,2,1,0:T(8,128)}, u32[]{:S(2)}) copy-start(f32[1,1,256,1024]{3,2,1,0:T(8,128)} %param.4) | copy-start | bytes 3145732
  20.5 12.3 %copy-start.9 = (s32[128,1]{0,1:T(1,128)S(1)}, s32[128,1]{0,1:T(1,128)}, u32[]{:S(2)}) copy-start(s32[128,1]{0,1:T(1,128)} %param.6) | copy-start | bytes 1540
  20.5 15.5 %collective-permute-start.1 = (f32[16,8,1024]{2,1,0:T(8,128)}, f32[16,8,1024]{2,1,0:T(8,128)}, u32[]{:S(2)}, u32[]{:S(2)}) collective-permute-start(f32[16,8,1024]{2,1,0:T(8,128)} %get-tuple-element.18), channel_id=1, source_target_pairs={{8,0},{16,8},{24,16},{0,24},{9,1},{17,9},{25,17},{1,25},{10,2},{18... | collective-permute-start | bytes 1572872 | tf_op jit(solution)/shard_map/ppermute | solution.py:239
  23.7 75.3 %collective-permute-start.4 = (f32[256,512]{1,0:T(8,128)}, f32[256,512]{1,0:T(8,128)S(1)}, u32[]{:S(2)}, u32[]{:S(2)}) collective-permute-start(f32[256,512]{1,0:T(8,128)} %slice.18), channel_id=1, source_target_pairs={{1,0},{2,1},{3,2},{0,3},{5,4},{6,5},{7,6},{4,7},{9,8},{10,9},{11,1... | collective-permute-start | bytes 1572872 | tf_op jit(solution)/shard_map/ppermute | solution.py:239
  25.6 73.3 %collective-permute-start.5 = (f32[256,512]{1,0:T(8,128)}, f32[256,512]{1,0:T(8,128)S(1)}, u32[]{:S(2)}, u32[]{:S(2)}) collective-permute-start(f32[256,512]{1,0:T(8,128)} %slice.18), channel_id=1, source_target_pairs={{2,0},{3,1},{0,2},{1,3},{6,4},{7,5},{4,6},{5,7},{10,8},{11,9},{8,1... | collective-permute-start | bytes 1572872 | tf_op jit(solution)/shard_map/ppermute | solution.py:239
  27.7 63.7 %collective-permute-start.2 = (f32[16,8,1024]{2,1,0:T(8,128)}, f32[16,8,1024]{2,1,0:T(8,128)}, u32[]{:S(2)}, u32[]{:S(2)}) collective-permute-start(f32[16,8,1024]{2,1,0:T(8,128)} %get-tuple-element.20), channel_id=1, source_target_pairs={{16,0},{24,8},{0,16},{8,24},{17,1},{25,9},{1,17},{9,25},{18,2},{26... | collective-permute-start | bytes 1572872 | tf_op jit(solution)/shard_map/ppermute | solution.py:239
  30.1 61.3 %collective-permute-start.3 = (f32[16,8,1024]{2,1,0:T(8,128)}, f32[16,8,1024]{2,1,0:T(8,128)}, u32[]{:S(2)}, u32[]{:S(2)}) collective-permute-start(f32[16,8,1024]{2,1,0:T(8,128)} %get-tuple-element.19), channel_id=1, source_target_pairs={{24,0},{0,8},{8,16},{16,24},{25,1},{1,9},{9,17},{17,25},{26,2},{2,... | collective-permute-start | bytes 1572872 | tf_op jit(solution)/shard_map/ppermute | solution.py:239
  36.0 62.1 %collective-permute-start.6 = (f32[256,512]{1,0:T(8,128)S(1)}, f32[256,512]{1,0:T(8,128)S(1)}, u32[]{:S(2)}, u32[]{:S(2)}) collective-permute-start(f32[256,512]{1,0:T(8,128)S(1)} %pad_maximum_fusion.2), channel_id=1, source_target_pairs={{3,0},{0,1},{1,2},{2,3},{7,4},{4,5},{5,6},{6,7},{11,8},{8,9},{9,10... | collective-permute-start | bytes 1572872 | tf_op jit(solution)/shard_map/ppermute | solution.py:239
  40.2 20.9 %all-to-all-start = ((f32[32,1,128]{2,1,0:T(1,128)}), f32[32,1,128]{2,1,0:T(1,128)S(1)}, u32[]{:S(2)}, u32[]{:S(2)}) async-start(f32[32,1,128]{2,1,0:T(1,128)} %broadcast_in_dim.76), calls=%async_computation | async-start | bytes 32768 | tf_op jit(solution)/shard_map/all_to_all | solution.py:234
  61.8 27.4 %all-to-all-start.1 = ((f32[16,1,128]{2,1,0:T(1,128)}), f32[16,1,128]{2,1,0:T(1,128)S(1)}, u32[]{:S(2)}, u32[]{:S(2)}) async-start(f32[16,1,128]{2,1,0:T(1,128)} %broadcast_in_dim.77), calls=%async_computation.1 | async-start | bytes 16384 | tf_op jit(solution)/shard_map/all_to_all | solution.py:234
  93.9 26.8 %all-to-all-start.2 = ((f32[16,8,1024]{2,1,0:T(8,128)}), f32[16,8,1024]{2,1,0:T(8,128)}, u32[]{:S(2)}, u32[]{:S(2)}) async-start(f32[16,8,1024]{2,1,0:T(8,128)} %fusion.2), calls=%async_computation.2 | async-start | bytes 1048576 | tf_op jit(solution)/shard_map/all_to_all | solution.py:234
  98.1 0.8 copy-start.6
  98.9 0.8 copy-start.4
  99.7 1.2 copy-start.2
  100.9 1.0 copy-start.5
  102.0 1.0 copy-start.7
  103.0 67.4 %copy-start.8 = (s32[128,1]{0,1:T(1,128)S(1)}, s32[128,1]{0,1:T(1,128)}, u32[]{:S(2)}) copy-start(s32[128,1]{0,1:T(1,128)} %param.7) | copy-start | bytes 1540
  104.0 0.8 copy-start.3
  122.3 78.3 %all-to-all-start.3 = ((bf16[128,16,128]{2,1,0:T(8,128)(2,1)}), bf16[128,16,128]{2,1,0:T(8,128)(2,1)S(1)}, u32[]{:S(2)}, u32[]{:S(2)}) async-start(bf16[128,16,128]{2,1,0:T(8,128)(2,1)} %copy-done.3), calls=%async_computation.3 | async-start | bytes 1048576 | tf_op jit(solution)/shard_map/all_to_all | solution.py:234
  202.2 82.1 %all-to-all-start.4 = ((bf16[128,16,128]{2,1,0:T(8,128)(2,1)}), bf16[128,16,128]{2,1,0:T(8,128)(2,1)S(1)}, u32[]{:S(2)}, u32[]{:S(2)}) async-start(bf16[128,16,128]{2,1,0:T(8,128)(2,1)} %shard_map.60), calls=%async_computation.4 | async-start | bytes 1048576 | tf_op jit(solution)/shard_map/all_to_all | solution.py:234
  212.4 24.2 %collective-permute-start.7 = (bf16[8,1024]{1,0:T(8,128)(2,1)S(1)}, bf16[8,1024]{1,0:T(8,128)(2,1)S(1)}, u32[]{:S(2)}, u32[]{:S(2)}) collective-permute-start(bf16[8,1024]{1,0:T(8,128)(2,1)S(1)} %convolution_convert_fusion), channel_id=1, source_target_pairs={{128,0},{160,32},{192,64},{224,96},{256,128},{288,160},{320,192},{... | collective-permute-start | bytes 49160 | tf_op jit(solution)/shard_map/ppermute | solution.py:239
  220.1 25.5 %collective-permute-start.8 = (bf16[8,1024]{1,0:T(8,128)(2,1)S(1)}, bf16[8,1024]{1,0:T(8,128)(2,1)S(1)}, u32[]{:S(2)}, u32[]{:S(2)}) collective-permute-start(bf16[8,1024]{1,0:T(8,128)(2,1)S(1)} %convolution_convert_fusion), channel_id=1, source_target_pairs={{256,0},{288,32},{320,64},{352,96},{384,128},{416,160},{448,192},{... | collective-permute-start | bytes 49160 | tf_op jit(solution)/shard_map/ppermute | solution.py:239
  226.7 19.0 %collective-permute-start.9 = (bf16[8,1024]{1,0:T(8,128)(2,1)S(1)}, bf16[8,1024]{1,0:T(8,128)(2,1)S(1)}, u32[]{:S(2)}, u32[]{:S(2)}) collective-permute-start(bf16[8,1024]{1,0:T(8,128)(2,1)S(1)} %convolution_convert_fusion), channel_id=1, source_target_pairs={{384,0},{416,32},{448,64},{480,96},{0,128},{32,160},{64,192},{96,2... | collective-permute-start | bytes 49160 | tf_op jit(solution)/shard_map/ppermute | solution.py:239
  245.7 8.0 %collective-permute-start.10 = (bf16[4,8,1024]{2,1,0:T(8,128)(2,1)S(1)}, bf16[4,8,1024]{2,1,0:T(8,128)(2,1)S(1)}, u32[]{:S(2)}, u32[]{:S(2)}) collective-permute-start(bf16[4,8,1024]{2,1,0:T(8,128)(2,1)S(1)} %get-tuple-element.28), channel_id=1, source_target_pairs={{32,0},{64,32},{96,64},{128,96},{160,128},{192,160},{224,192},{256... | collective-permute-start | bytes 196616 | tf_op jit(solution)/shard_map/ppermute | solution.py:239
  247.6 6.1 %collective-permute-start.11 = (bf16[4,8,1024]{2,1,0:T(8,128)(2,1)S(1)}, bf16[4,8,1024]{2,1,0:T(8,128)(2,1)S(1)}, u32[]{:S(2)}, u32[]{:S(2)}) collective-permute-start(bf16[4,8,1024]{2,1,0:T(8,128)(2,1)S(1)} %get-tuple-element.28), channel_id=1, source_target_pairs={{64,0},{96,32},{128,64},{160,96},{192,128},{224,160},{256,192},{28... | collective-permute-start | bytes 196616 | tf_op jit(solution)/shard_map/ppermute | solution.py:239
  250.2 6.2 %collective-permute-start.12 = (bf16[4,8,1024]{2,1,0:T(8,128)(2,1)S(1)}, bf16[4,8,1024]{2,1,0:T(8,128)(2,1)S(1)}, u32[]{:S(2)}, u32[]{:S(2)}) collective-permute-start(bf16[4,8,1024]{2,1,0:T(8,128)(2,1)S(1)} %get-tuple-element.28), channel_id=1, source_target_pairs={{480,0},{0,32},{32,64},{64,96},{96,128},{128,160},{160,192},{192,2... | collective-permute-start | bytes 196616 | tf_op jit(solution)/shard_map/ppermute | solution.py:239
  256.5 9.1 %collective-permute-start.13 = (bf16[4,4,8,1024]{3,2,1,0:T(8,128)(2,1)S(1)}, bf16[4,4,8,1024]{3,2,1,0:T(8,128)(2,1)S(1)}, u32[]{:S(2)}, u32[]{:S(2)}) collective-permute-start(bf16[4,4,8,1024]{3,2,1,0:T(8,128)(2,1)S(1)} %get-tuple-element.26), channel_id=1, source_target_pairs={{8,0},{16,8},{24,16},{0,24},{9,1},{17,9},{25,17},{1,25},{10,2},{18... | collective-permute-start | bytes 786440 | tf_op jit(solution)/shard_map/ppermute | solution.py:239
  260.4 8.6 %collective-permute-start.14 = (bf16[4,4,8,1024]{3,2,1,0:T(8,128)(2,1)S(1)}, bf16[4,4,8,1024]{3,2,1,0:T(8,128)(2,1)S(1)}, u32[]{:S(2)}, u32[]{:S(2)}) collective-permute-start(bf16[4,4,8,1024]{3,2,1,0:T(8,128)(2,1)S(1)} %get-tuple-element.26), channel_id=1, source_target_pairs={{16,0},{24,8},{0,16},{8,24},{17,1},{25,9},{1,17},{9,25},{18,2},{26... | collective-permute-start | bytes 786440 | tf_op jit(solution)/shard_map/ppermute | solution.py:239
  263.4 12.3 %collective-permute-start.15 = (bf16[4,4,8,1024]{3,2,1,0:T(8,128)(2,1)S(1)}, bf16[4,4,8,1024]{3,2,1,0:T(8,128)(2,1)S(1)}, u32[]{:S(2)}, u32[]{:S(2)}) collective-permute-start(bf16[4,4,8,1024]{3,2,1,0:T(8,128)(2,1)S(1)} %get-tuple-element.26), channel_id=1, source_target_pairs={{24,0},{0,8},{8,16},{16,24},{25,1},{1,9},{9,17},{17,25},{26,2},{2,... | collective-permute-start | bytes 786440 | tf_op jit(solution)/shard_map/ppermute | solution.py:239
  275.9 6.7 %collective-permute-start.16 = (bf16[4,4,4,8,1024]{4,3,2,1,0:T(8,128)(2,1)S(1)}, bf16[4,4,4,8,1024]{4,3,2,1,0:T(8,128)(2,1)S(1)}, u32[]{:S(2)}, u32[]{:S(2)}) collective-permute-start(bf16[4,4,4,8,1024]{4,3,2,1,0:T(8,128)(2,1)S(1)} %get-tuple-element.22), channel_id=1, source_target_pairs={{4,0},{0,4},{5,1},{1,5},{6,2},{2,6},{7,3},{3,7},{12,8},{8,12},{13,... | collective-permute-start | bytes 3145736 | tf_op jit(solution)/shard_map/ppermute | solution.py:239

commit v3 on v2

--- a/solution.py
+++ b/solution.py
@@ -11,7 +11,7 @@
 X_COUNT, CORES = 4, 2
 DP = ("z", "x", "c")
 
-BASE = 128
+BASE = 32
 SUB = 8
 ROWS, LANES = 16, 128
 
@@ -28,15 +28,34 @@
     return pltpu.reciprocal(x, approx=True)
 
 
-def base_sweep(load, store):
-    count = BASE // SUB
-    groups = [load(i) for i in range(count)]
-    sub_ids = lax.broadcasted_iota(jnp.int32, (SUB, BASE), 0)
-    lane_ids = lax.broadcasted_iota(jnp.int32, (SUB, BASE), 1)
-    for p in range(count):
-        pivot_lanes = (lane_ids // SUB) == p
-        spread = [lane_of(groups[p], p * SUB + j) for j in range(SUB)]
-        rows = jnp.where(pivot_lanes, jnp.where(lane_ids == sub_ids + p * SUB, 1.0, 0.0), groups[p])
+def halves(x):
+    high = x.astype(jnp.bfloat16)
+    return high, (x - high.astype(jnp.float32)).astype(jnp.bfloat16)
+
+
+def stacked(x, order, axis):
+    parts = halves(x)
+    return jnp.concatenate([parts[i] for i in order], axis=axis)
+
+
+LEFT, RIGHT = (0, 0, 1), (0, 1, 0)
+
+
+def dot(left, right):
+    return jnp.dot(left, right, preferred_element_type=jnp.float32)
+
+
+def panel_sweep(groups, first):
+    sub_ids = lax.broadcasted_iota(jnp.int32, (SUB, LANES), 0)
+    lane_ids = lax.broadcasted_iota(jnp.int32, (SUB, LANES), 1)
+    for p in range(len(groups)):
+        tile, lane = divmod(first + p * SUB, LANES)
+        pivot_lanes = (lane_ids // SUB) == lane // SUB
+        spread = [lane_of(groups[p][tile], lane + j) for j in range(SUB)]
+        rows = list(groups[p])
+        rows[tile] = jnp.where(
+            pivot_lanes, jnp.where(lane_ids == sub_ids + lane, 1.0, 0.0), rows[tile]
+        )
         pivot = row_of(spread[0], 0)
         for j in range(SUB):
             here = sub_ids == j
@@ -50,37 +69,52 @@
                 line = row_of(x, j)
                 return jnp.where(here, 0.0, x) - (column * line) * scale
 
-            rows = eliminate(rows)
+            rows = [eliminate(x) for x in rows]
             for i in range(j + 1, SUB):
                 spread[i] = eliminate(spread[i])
-        rows = jnp.where(pivot_lanes, -rows, rows)
-        lines = [row_of(rows, j) for j in range(SUB)]
-        for step in range(1, count):
-            i = (p + step) % count
-            terms = [lane_of(groups[i], p * SUB + j) * lines[j] for j in range(SUB)]
-            while len(terms) > 1:
-                terms = [a + b for a, b in zip(terms[::2], terms[1::2])]
-            groups[i] = jnp.where(pivot_lanes, 0.0, groups[i]) - terms[0]
+        rows[tile] = jnp.where(pivot_lanes, -rows[tile], rows[tile])
+        lines = [[row_of(x, j) for x in rows] for j in range(SUB)]
+        for g in range(len(groups)):
+            if g == p:
+                continue
+            factors = [lane_of(groups[g][tile], lane + j) for j in range(SUB)]
+            for t in range(len(rows)):
+                terms = [factors[j] * lines[j][t] for j in range(SUB)]
+                while len(terms) > 1:
+                    terms = [a + b for a, b in zip(terms[::2], terms[1::2])]
+                kept = groups[g][t]
+                if t == tile:
+                    kept = jnp.where(pivot_lanes, 0.0, kept)
+                groups[g][t] = kept - terms[0]
         groups[p] = rows
-    for i in range(count):
-        store(i, groups[i])
-
-
-def halves(x):
-    high = x.astype(jnp.bfloat16)
-    return high, (x - high.astype(jnp.float32)).astype(jnp.bfloat16)
-
-
-def dot3(left, right):
-    def one(a, b):
-        return jnp.dot(a, b, preferred_element_type=jnp.float32)
-
-    return one(left[0], right[0]) + (one(left[0], right[1]) + one(left[1], right[0]))
+    return groups
+
+
+def block_sweep(d_ref):
+    wide = d_ref.shape[0]
+    lane_ids = lax.broadcasted_iota(jnp.int32, (wide, wide), 1)
+    for first in range(0, wide, BASE):
+        old = d_ref[first : first + BASE, :]
+        groups = [
+            [old[g : g + SUB, t : t + LANES] for t in range(0, wide, LANES)]
+            for g in range(0, BASE, SUB)
+        ]
+        groups = panel_sweep(groups, first)
+        new = jnp.concatenate([jnp.concatenate(g, axis=1) for g in groups], axis=0)
+        update = lax.dot_general(
+            stacked(old, LEFT, 0),
+            stacked(new, RIGHT, 0),
+            (((0,), (0,)), ((), ())),
+            preferred_element_type=jnp.float32,
+        )
+        kept = jnp.where(lane_ids // BASE == first // BASE, 0.0, d_ref[...])
+        d_ref[...] = kept - update
+        d_ref[first : first + BASE, :] = new
 
 
 def invert_kernel(
-    scalar_ref, shift_ref, rows_ref, one_ref, two_ref, three_ref,
-    band_ref, full_ref, m_ref, d_ref, th_ref, tl_ref,
+    scalar_ref, shift_ref, rows_ref, one_hbm, two_hbm, three_hbm,
+    band_ref, full_ref, m_ref, d_ref, left_ref, right_ref, far_ref, far_sem,
 ):
     n = rows_ref.shape[1]
     wide = rows_ref.shape[0]
@@ -95,6 +129,12 @@
 
     @pl.when(scalar_ref[0] > 0)
     def _():
+        copies = [
+            pltpu.make_async_copy(source, far_ref.at[i], far_sem.at[i])
+            for i, source in enumerate((one_hbm, two_hbm, three_hbm))
+        ]
+        for copy in copies:
+            copy.start()
         eye = jnp.where(
             lax.broadcasted_iota(jnp.int32, (wide, wide), 0)
             == lax.broadcasted_iota(jnp.int32, (wide, wide), 1),
@@ -111,57 +151,29 @@
 
         for j in range(count):
             put(0, j, rows_ref[:, place(j)])
-        put(1, 1, one_ref[:, block(0)])
-        put(1, 2, one_ref[:, block(1)])
-        put(2, 2, two_ref[:, block(0)])
-        put(2, 3, two_ref[:, block(1)])
-        put(3, 3, three_ref[:, block(0)])
-        put(3, 1, three_ref[:, block(1)])
+        for i in range(1, count):
+            copies[i - 1].wait()
+            put(i, i, far_ref[i - 1, :, block(0)])
+            put(i, i % (count - 1) + 1, far_ref[i - 1, :, block(1)])
 
         @pl.loop(0, count)
         def _(k):
             at = pl.ds(pl.multiple_of(k * wide, wide), wide)
-
             d_ref[...] = m_ref[at, at]
-
-            def sweep_half(h):
-                lo = h * BASE
-                base_sweep(
-                    lambda i: d_ref[lo + i * SUB : lo + (i + 1) * SUB, lo : lo + BASE],
-                    lambda i, v: d_ref.__setitem__(
-                        (slice(lo + i * SUB, lo + (i + 1) * SUB), slice(lo, lo + BASE)), v
-                    ),
-                )
-
-            one, two = slice(0, BASE), slice(BASE, wide)
-            sweep_half(0)
-            minus_p = halves(d_ref[one, one])
-            cross = halves(d_ref[one, two])
-            cross_t = halves(d_ref[two, one])
-            t_halves = halves(-dot3(minus_p, cross))
-            d_ref[two, two] = d_ref[two, two] - dot3(cross_t, t_halves)
-            left = halves(-dot3(cross_t, minus_p))
-            sweep_half(1)
-            minus_p = halves(d_ref[two, two])
-            up = dot3(t_halves, minus_p)
-            d_ref[one, one] = d_ref[one, one] + dot3(halves(up), left)
-            d_ref[one, two] = -up
-            d_ref[two, one] = -dot3(minus_p, left)
-
-            minus_p = halves(d_ref[...])
-            col_h, col_l = halves(m_ref[:, at])
-            rows = -dot3(minus_p, halves(m_ref[at, :]))
+            block_sweep(d_ref)
+
+            left_ref[...] = stacked(m_ref[:, at], LEFT, 1)
+            right_ref[...] = stacked(m_ref[at, :], RIGHT, 0)
+            rows = -dot(stacked(d_ref[...], LEFT, 1), right_ref[...])
             m_ref[:, at] = jnp.zeros((n, wide), jnp.float32)
             m_ref[at, :] = rows
             m_ref[at, at] = d_ref[...]
-            th_ref[...], tl_ref[...] = halves(m_ref[at, :])
+            right_ref[...] = stacked(m_ref[at, :], RIGHT, 0)
             for i in range(count):
 
                 @pl.when(i != k)
                 def _():
-                    m_ref[block(i), :] = m_ref[block(i), :] - dot3(
-                        (col_h[block(i)], col_l[block(i)]), (th_ref[...], tl_ref[...])
-                    )
+                    m_ref[block(i), :] = m_ref[block(i), :] - dot(left_ref[block(i), :], right_ref[...])
 
         for j in range(count):
             band = (-m_ref[block(0), block(j)]).astype(jnp.bfloat16)
@@ -182,19 +194,22 @@
     wide, n = rows.shape
     in_smem = pl.BlockSpec(memory_space=pltpu.SMEM)
     in_vmem = pl.BlockSpec(memory_space=pltpu.VMEM)
+    anywhere = pl.BlockSpec(memory_space=pl.ANY)
     return pl.pallas_call(
         invert_kernel,
         out_shape=(
             jax.ShapeDtypeStruct((wide * n // (ROWS * LANES), ROWS, LANES), jnp.bfloat16),
             jax.ShapeDtypeStruct((n, n), jnp.bfloat16),
         ),
-        in_specs=[in_smem] * 2 + [in_vmem] * 4,
+        in_specs=[in_smem] * 2 + [in_vmem] + [anywhere] * 3,
         out_specs=(in_vmem, in_vmem),
         scratch_shapes=[
             pltpu.VMEM((n, n), jnp.float32),
             pltpu.VMEM((wide, wide), jnp.float32),
-            pltpu.VMEM((wide, n), jnp.bfloat16),
-            pltpu.VMEM((wide, n), jnp.bfloat16),
+            pltpu.VMEM((n, 3 * wide), jnp.bfloat16),
+            pltpu.VMEM((3 * wide, n), jnp.bfloat16),
+            pltpu.VMEM((3, wide, 2 * wide), jnp.float32),
+            pltpu.SemaphoreType.DMA((3,)),
         ],
         compiler_params=pltpu.CompilerParams(vmem_limit_bytes=24 * 1024 * 1024),
         cost_estimate=pl.CostEstimate(
@@ -267,7 +282,9 @@
     bins = lax.broadcasted_iota(jnp.int32, (1, 128), 1)
     own_bin = jnp.where(own >= 0, 2 * own_layer + jnp.where(own_input, 0, 1), -1)
     binned = jnp.where(bins == own_bin, trace, 0.0)
+    binned, rows = lax.optimization_barrier((binned, rows))
     binned = sum_of_all(binned, ("x", "c", "mp"), x_count * c_count * mp_count)
+    binned, tiles = lax.optimization_barrier((binned, gradients[0]))
     binned = sum_of_all(binned, "z", z_count)
     trace_input = jnp.sum(jnp.where(bins == 2 * own_layer, binned, 0.0))
     trace_output = jnp.sum(jnp.where(bins == 2 * own_layer + 1, binned, 0.0))
@@ -288,7 +305,7 @@
 
     def tiles_of(core):
         index = lax.dynamic_index_in_dim(tile_of, core, keepdims=False)
-        return take(gradients[0], index.reshape(-1))
+        return take(tiles, index.reshape(-1))
 
     def split(value):
         return value.astype(jnp.float32).reshape(x_count, z_count, row_count, width)
@@ -306,17 +323,20 @@
     inverse_band, inverse = invert(scalars, shift.reshape(1), rows, one, two, three)
     inverse_band, tile = lax.optimization_barrier((inverse_band, tile))
 
+    def gather(value, axis, steps):
+        return jnp.stack([value] + [from_ahead(value, axis, step) for step in steps])
+
+    held = jnp.dot(tile, inverse, preferred_element_type=jnp.float32).astype(jnp.bfloat16)
     spread = exchange(inverse_band, DP)
+    held = gather(gather(held, "z", (4, 8, 12)), "z", (1, 2, 15))
     slot_range = jnp.arange(dp_count, dtype=jnp.int32)
     empty = jnp.min(jnp.where(old_flat >= 0, dp_count - 1, slot_range))
     source = jnp.where(new_flat >= 0, positions(old_flat, new_flat), empty)
-    arrived = exchange(pick(source, spread), DP)
+    outgoing, held = lax.optimization_barrier((pick(source, spread), held))
+    arrived = exchange(outgoing, DP)
     arrived = arrived.reshape(band // ROWS, width // LANES, ROWS, LANES)
     inverses = arrived.transpose(0, 2, 1, 3).reshape(1, 1, band, width)
-
-    held = jnp.dot(tile, inverse, preferred_element_type=jnp.float32).astype(jnp.bfloat16)
-    for axis, steps in (("z", (4, 8, 12)), ("z", (1, 2, 15)), ("x", (1, 2, 3)), ("c", (1,))):
-        held = jnp.stack([held] + [from_ahead(held, axis, step) for step in steps])
+    held = gather(gather(held, "x", (1, 2, 3)), "c", (1,))
     held = held.reshape(dp_count, row_count, width)
     tile_range = jnp.arange(tile_count, dtype=jnp.int32)
     place = positions(old_flat, tile_range // a_span * layer_blocks + tile_range % a_span)

time: 287 us -> 256 us (0.89)
  Pallas kernels: 2.49 us -> 50.3 us
  waiting for transfers between devices: 91.3 us -> 48.5 us
  starting transfers between devices: 157 us -> 120 us
    pallas_call x1, Pallas kernels: 0.93 us -> 48.7 us  [invert(): pl.pallas_call(invert_kernel, out_shape=(jax.ShapeDtypeStruct((wide * n /...]
    all_to_all x5, waiting for transfers between devices: 62.5 us -> 15.7 us  [exchange(): return lax.all_to_all(pieces, axes, split_axis=0, concat_axis=0, tiled=True)]
    all_to_all x5, starting transfers between devices: 91 us -> 60.1 us  [exchange(): return lax.all_to_all(pieces, axes, split_axis=0, concat_axis=0, tiled=True)]
    ppermute x17, starting transfers between devices: 65.8 us -> 60.3 us  [from_ahead(): lax.ppermute(value, axis, [((i + step) % count, i) for i in range(count)])]
    ppermute x17, waiting for transfers between devices: 28.8 us -> 32.8 us  [from_ahead(): lax.ppermute(value, axis, [((i + step) % count, i) for i in range(count)])]
  transfers between devices with their start and end apart: 22 -> 22, of which waited for: 13 -> 10; matrix products, arithmetic and copies ran while one was open for 5% -> 5% of each run, Pallas kernels for 0% -> 19%
where the time goes in v3:
time: 256 us; the launch traced here: 254 us
  starting transfers between devices  120 us (47%)
  Pallas kernels  50.3 us (20%)
  waiting for transfers between devices  48.5 us (19%)
  other arithmetic  16.1 us (6%)
  local copies, waits for them, and re-layouts  14.3 us (6%)
  between operations  4.25 us (2%)
    ppermute x17, starting transfers between devices, from_ahead(): lax.ppermute(value, axis, [((i + step) % count, i) for i in range(count)])  60.3 us
    all_to_all x5, starting transfers between devices, exchange(): return lax.all_to_all(pieces, axes, split_axis=0, concat_axis=0, tiled=True)  60.1 us
    pallas_call x1, Pallas kernels, invert(): pl.pallas_call(invert_kernel, out_shape=(jax.ShapeDtypeStruct((wide * n /...  48.7 us
    ppermute x17, waiting for transfers between devices, from_ahead(): lax.ppermute(value, axis, [((i + step) % count, i) for i in range(count)])  32.8 us
    all_to_all x5, waiting for transfers between devices, exchange(): return lax.all_to_all(pieces, axes, split_axis=0, concat_axis=0, tiled=True)  15.7 us
    unnamed x22, local copies, waits for them, and re-layouts  5.7 us
  transfers between devices with their start and end apart: 22, of which 10 were waited for; matrix products, arithmetic and copies ran while one was open for 5% of the time, Pallas kernels for 19%

profile of v3, /device:TPU:1, one launch (start us, length us, event | category | flops | bytes accessed | tf_op | source)
XLA Modules:
  0.0 254.2 jit_solution(1035249755658175198)
XLA Ops:
  0.7 1.3 fusion.28
  3.2 1.6 fusion.3
  4.8 0.6 compare_select_fusion.15
  5.5 0.6 broadcast_in_dim.83
  6.1 10.4 %all-to-all-start = ((f32[32,1,128]{2,1,0:T(1,128)}), f32[32,1,128]{2,1,0:T(1,128)S(1)}, u32[]{:S(2)}, u32[]{:S(2)}) async-start(f32[32,1,128]{2,1,0:T(1,128)} %broadcast_in_dim.83), calls=%async_computation | async-start | bytes 32768 | tf_op jit(solution)/shard_map/all_to_all | solution.py:249
  16.5 0.7 remainder_reduce_fusion
  17.1 0.7 compare_reduce_fusion
  18.9 4.5 %all-to-all-done = f32[32,1,128]{2,1,0:T(1,128)S(1)} async-done(((f32[32,1,128]{2,1,0:T(1,128)}), f32[32,1,128]{2,1,0:T(1,128)S(1)}, u32[]{:S(2)}, u32[]{:S(2)}) %all-to-all-start) | async-done | bytes 16416 | tf_op jit(solution)/shard_map/all_to_all | solution.py:249
  23.4 0.6 gather_fusion.1
  24.0 2.6 %collective-permute-start = (bf16[64,8,1024]{2,1,0:T(8,128)(2,1)S(1)}, bf16[64,8,1024]{2,1,0:T(8,128)(2,1)}, u32[]{:S(2)}, u32[]{:S(2)}) collective-permute-start(bf16[64,8,1024]{2,1,0:T(8,128)(2,1)S(1)} %gather_fusion.1), channel_id=1, source_target_pairs={{4,0},{0,4},{5,1},{1,5},{6,2},{2,6},{7,3},{3,7},{12,8},{8,12},{13,... | collective-permute-start | bytes 3145736 | tf_op jit(solution)/shard_map/ppermute | solution.py:254
  26.7 0.6 gather_fusion
  27.3 1.7 collective-permute-done
  29.0 2.9 %convert_add_fusion = f32[64,8,1024]{2,1,0:T(8,128)} fusion(bf16[64,8,1024]{2,1,0:T(8,128)(2,1)} %collective-permute-done, bf16[64,8,1024]{2,1,0:T(8,128)(2,1)S(1)} %gather_fusion), kind=kLoop, calls=%fused_computation.6 | loop fusion | flops 1572864 | bytes 4194304 | tf_op jit(solution)/shard_map/add | solution.py:314
  31.9 1.5 dynamic-slice_bitcast_fusion.2
  33.5 2.7 %collective-permute-start.1 = (f32[16,8,1024]{2,1,0:T(8,128)S(1)}, f32[16,8,1024]{2,1,0:T(8,128)}, u32[]{:S(2)}, u32[]{:S(2)}) collective-permute-start(f32[16,8,1024]{2,1,0:T(8,128)S(1)} %get-tuple-element.30), channel_id=1, source_target_pairs={{8,0},{16,8},{24,16},{0,24},{9,1},{17,9},{25,17},{1,25},{10,2},{18... | collective-permute-start | bytes 1572872 | tf_op jit(solution)/shard_map/ppermute | solution.py:254
  36.3 0.2 fusion
  36.5 3.2 %collective-permute-start.2 = (f32[16,8,1024]{2,1,0:T(8,128)S(1)}, f32[16,8,1024]{2,1,0:T(8,128)}, u32[]{:S(2)}, u32[]{:S(2)}) collective-permute-start(f32[16,8,1024]{2,1,0:T(8,128)S(1)} %get-tuple-element.32), channel_id=1, source_target_pairs={{16,0},{24,8},{0,16},{8,24},{17,1},{25,9},{1,17},{9,25},{18,2},{26... | collective-permute-start | bytes 1572872 | tf_op jit(solution)/shard_map/ppermute | solution.py:254
  39.7 1.9 collective-permute-start.3
  41.6 0.9 pad_maximum_fusion.2
  42.5 2.2 collective-permute-start.6
  44.7 0.9 slice.18
  45.5 4.3 %collective-permute-start.4 = (f32[256,512]{1,0:T(8,128)}, f32[256,512]{1,0:T(8,128)S(1)}, u32[]{:S(2)}, u32[]{:S(2)}) collective-permute-start(f32[256,512]{1,0:T(8,128)} %slice.18), channel_id=1, source_target_pairs={{1,0},{2,1},{3,2},{0,3},{5,4},{6,5},{7,6},{4,7},{9,8},{10,9},{11,1... | collective-permute-start | bytes 1572872 | tf_op jit(solution)/shard_map/ppermute | solution.py:254
  49.9 1.9 collective-permute-start.5
  52.3 0.6 broadcast_in_dim.85
  52.9 13.0 %all-to-all-start.1 = ((f32[16,1,128]{2,1,0:T(1,128)}), f32[16,1,128]{2,1,0:T(1,128)S(1)}, u32[]{:S(2)}, u32[]{:S(2)}) async-start(f32[16,1,128]{2,1,0:T(1,128)} %broadcast_in_dim.85), calls=%async_computation.1 | async-start | bytes 16384 | tf_op jit(solution)/shard_map/all_to_all | solution.py:249
  66.0 11.2 %all-to-all-done.1 = f32[16,1,128]{2,1,0:T(1,128)S(1)} async-done(((f32[16,1,128]{2,1,0:T(1,128)}), f32[16,1,128]{2,1,0:T(1,128)S(1)}, u32[]{:S(2)}, u32[]{:S(2)}) %all-to-all-start.1) | async-done | bytes 8224 | tf_op jit(solution)/shard_map/all_to_all | solution.py:249
  77.2 0.7 fusion.13
  79.2 2.5 fusion.2
  81.7 4.2 %all-to-all-start.2 = ((f32[16,8,1024]{2,1,0:T(8,128)}), f32[16,8,1024]{2,1,0:T(8,128)}, u32[]{:S(2)}, u32[]{:S(2)}) async-start(f32[16,8,1024]{2,1,0:T(8,128)} %fusion.2), calls=%async_computation.2 | async-start | bytes 1048576 | tf_op jit(solution)/shard_map/all_to_all | solution.py:249
  86.0 0.8 copy-done.4
  86.8 0.8 copy-done.6
  87.6 1.2 copy-done.2
  88.8 1.0 copy-done.5
  89.8 1.0 copy-done.7
  90.9 48.7 %shard_map.59 = (bf16[128,16,128]{2,1,0:T(8,128)(2,1)S(1)}, bf16[1024,1024]{1,0:T(8,128)(2,1)S(1)}) custom-call(s32[2]{0:T(128)S(1)} %pad_add_fusion.scalar_ref, f32[1]{0:T(128)} %bitcast.25.shift_ref, f32[256,1024]{1,0:T(8,128)S(1)} %bitcast.96, f32[256,512]{1,0:T(8,128)S(1)} %copy-done.5, f32[256,512]{1,0:T(8,128)S(1)} %copy-done.7, ...), custom_call_target="tpu_custom_call" | custom-call | flops 38654705664 | bytes 6291456 | tf_op jit(solution)/shard_map/pallas_call | solution.py:198
  139.6 0.8 copy-done.3
  140.4 1.1 reduce_sum.84
  141.5 18.9 %all-to-all-start.3 = ((bf16[128,16,128]{2,1,0:T(8,128)(2,1)}), bf16[128,16,128]{2,1,0:T(8,128)(2,1)S(1)}, u32[]{:S(2)}, u32[]{:S(2)}) async-start(bf16[128,16,128]{2,1,0:T(8,128)(2,1)} %copy-done.3), calls=%async_computation.3 | async-start | bytes 1048576 | tf_op jit(solution)/shard_map/all_to_all | solution.py:249
  160.5 0.9 select_reduce_fusion
  161.4 0.4 convolution_convert_fusion
  161.7 7.7 %collective-permute-start.7 = (bf16[8,1024]{1,0:T(8,128)(2,1)S(1)}, bf16[8,1024]{1,0:T(8,128)(2,1)S(1)}, u32[]{:S(2)}, u32[]{:S(2)}) collective-permute-start(bf16[8,1024]{1,0:T(8,128)(2,1)S(1)} %convolution_convert_fusion), channel_id=1, source_target_pairs={{128,0},{160,32},{192,64},{224,96},{256,128},{288,160},{320,192},{... | collective-permute-start | bytes 49160 | tf_op jit(solution)/shard_map/ppermute | solution.py:254
  169.5 6.6 %collective-permute-start.8 = (bf16[8,1024]{1,0:T(8,128)(2,1)S(1)}, bf16[8,1024]{1,0:T(8,128)(2,1)S(1)}, u32[]{:S(2)}, u32[]{:S(2)}) collective-permute-start(bf16[8,1024]{1,0:T(8,128)(2,1)S(1)} %convolution_convert_fusion), channel_id=1, source_target_pairs={{256,0},{288,32},{320,64},{352,96},{384,128},{416,160},{448,192},{... | collective-permute-start | bytes 49160 | tf_op jit(solution)/shard_map/ppermute | solution.py:254
  176.1 7.2 %collective-permute-start.9 = (bf16[8,1024]{1,0:T(8,128)(2,1)S(1)}, bf16[8,1024]{1,0:T(8,128)(2,1)S(1)}, u32[]{:S(2)}, u32[]{:S(2)}) collective-permute-start(bf16[8,1024]{1,0:T(8,128)(2,1)S(1)} %convolution_convert_fusion), channel_id=1, source_target_pairs={{384,0},{416,32},{448,64},{480,96},{0,128},{32,160},{64,192},{96,2... | collective-permute-start | bytes 49160 | tf_op jit(solution)/shard_map/ppermute | solution.py:254
  183.3 0.6 fusion.11
  183.9 1.8 collective-permute-done.7
  185.8 9.0 %collective-permute-done.8 = bf16[8,1024]{1,0:T(8,128)(2,1)S(1)} collective-permute-done((bf16[8,1024]{1,0:T(8,128)(2,1)S(1)}, bf16[8,1024]{1,0:T(8,128)(2,1)S(1)}, u32[]{:S(2)}, u32[]{:S(2)}) %collective-permute-start.8) | collective-permute-done | bytes 16416 | tf_op jit(solution)/shard_map/ppermute | solution.py:254
  194.8 1.9 collective-permute-start.10
  196.7 2.7 %collective-permute-start.11 = (bf16[4,8,1024]{2,1,0:T(8,128)(2,1)S(1)}, bf16[4,8,1024]{2,1,0:T(8,128)(2,1)S(1)}, u32[]{:S(2)}, u32[]{:S(2)}) collective-permute-start(bf16[4,8,1024]{2,1,0:T(8,128)(2,1)S(1)} %get-tuple-element.38), channel_id=1, source_target_pairs={{64,0},{96,32},{128,64},{160,96},{192,128},{224,160},{256,192},{28... | collective-permute-start | bytes 196616 | tf_op jit(solution)/shard_map/ppermute | solution.py:254
  199.4 3.4 %collective-permute-start.12 = (bf16[4,8,1024]{2,1,0:T(8,128)(2,1)S(1)}, bf16[4,8,1024]{2,1,0:T(8,128)(2,1)S(1)}, u32[]{:S(2)}, u32[]{:S(2)}) collective-permute-start(bf16[4,8,1024]{2,1,0:T(8,128)(2,1)S(1)} %get-tuple-element.38), channel_id=1, source_target_pairs={{480,0},{0,32},{32,64},{64,96},{96,128},{128,160},{160,192},{192,2... | collective-permute-start | bytes 196616 | tf_op jit(solution)/shard_map/ppermute | solution.py:254
  202.8 0.7 compare_select_fusion.18.index_ref
  203.5 2.2 collective-permute-done.12
  205.7 1.6 shard_map.60
  207.2 13.5 %all-to-all-start.4 = ((bf16[128,16,128]{2,1,0:T(8,128)(2,1)}), bf16[128,16,128]{2,1,0:T(8,128)(2,1)S(1)}, u32[]{:S(2)}, u32[]{:S(2)}) async-start(bf16[128,16,128]{2,1,0:T(8,128)(2,1)} %shard_map.60), calls=%async_computation.4 | async-start | bytes 1048576 | tf_op jit(solution)/shard_map/all_to_all | solution.py:249
  220.8 4.5 %collective-permute-start.13 = (bf16[4,4,8,1024]{3,2,1,0:T(8,128)(2,1)S(1)}, bf16[4,4,8,1024]{3,2,1,0:T(8,128)(2,1)S(1)}, u32[]{:S(2)}, u32[]{:S(2)}) collective-permute-start(bf16[4,4,8,1024]{3,2,1,0:T(8,128)(2,1)S(1)} %pad_maximum_fusion.3), channel_id=1, source_target_pairs={{8,0},{16,8},{24,16},{0,24},{9,1},{17,9},{25,17},{1,25},{10,2},{18... | collective-permute-start | bytes 786440 | tf_op jit(solution)/shard_map/ppermute | solution.py:254
  225.3 2.5 collective-permute-start.14
  227.8 2.5 collective-permute-start.15
  230.3 3.6 %collective-permute-done.13 = bf16[4,4,8,1024]{3,2,1,0:T(8,128)(2,1)S(1)} collective-permute-done((bf16[4,4,8,1024]{3,2,1,0:T(8,128)(2,1)S(1)}, bf16[4,4,8,1024]{3,2,1,0:T(8,128)(2,1)S(1)}, u32[]{:S(2)}, u32[]{:S(2)}) %collective-permute-start.13) | collective-permute-done | bytes 262176 | tf_op jit(solution)/shard_map/ppermute | solution.py:254
  233.9 3.8 %collective-permute-done.14 = bf16[4,4,8,1024]{3,2,1,0:T(8,128)(2,1)S(1)} collective-permute-done((bf16[4,4,8,1024]{3,2,1,0:T(8,128)(2,1)S(1)}, bf16[4,4,8,1024]{3,2,1,0:T(8,128)(2,1)S(1)}, u32[]{:S(2)}, u32[]{:S(2)}) %collective-permute-start.14) | collective-permute-done | bytes 262176 | tf_op jit(solution)/shard_map/ppermute | solution.py:254
  237.7 8.7 %collective-permute-done.15 = bf16[4,4,8,1024]{3,2,1,0:T(8,128)(2,1)S(1)} collective-permute-done((bf16[4,4,8,1024]{3,2,1,0:T(8,128)(2,1)S(1)}, bf16[4,4,8,1024]{3,2,1,0:T(8,128)(2,1)S(1)}, u32[]{:S(2)}, u32[]{:S(2)}) %collective-permute-start.15) | collective-permute-done | bytes 262176 | tf_op jit(solution)/shard_map/ppermute | solution.py:254
  246.5 2.5 collective-permute-start.16
  249.3 2.0 collective-permute-done.16
  251.3 0.2 pad_maximum_fusion
  251.5 1.6 gather_fusion.2
  253.2 1.0 reshape.521
  (52 shorter events, 1.9 us)
Async XLA Ops:
  0.6 22.8 %copy-start = (bf16[1,56,8,1024]{3,2,1,0:T(8,128)(2,1)S(1)}, bf16[1,56,8,1024]{3,2,1,0:T(8,128)(2,1)}, u32[]{:S(2)}) copy-start(bf16[1,56,8,1024]{3,2,1,0:T(8,128)(2,1)} %param.5) | copy-start | bytes 2752516
  6.1 17.3 %all-to-all-start = ((f32[32,1,128]{2,1,0:T(1,128)}), f32[32,1,128]{2,1,0:T(1,128)S(1)}, u32[]{:S(2)}, u32[]{:S(2)}) async-start(f32[32,1,128]{2,1,0:T(1,128)} %broadcast_in_dim.83), calls=%async_computation | async-start | bytes 32768 | tf_op jit(solution)/shard_map/all_to_all | solution.py:249
  24.0 5.0 %collective-permute-start = (bf16[64,8,1024]{2,1,0:T(8,128)(2,1)S(1)}, bf16[64,8,1024]{2,1,0:T(8,128)(2,1)}, u32[]{:S(2)}, u32[]{:S(2)}) collective-permute-start(bf16[64,8,1024]{2,1,0:T(8,128)(2,1)S(1)} %gather_fusion.1), channel_id=1, source_target_pairs={{4,0},{0,4},{5,1},{1,5},{6,2},{2,6},{7,3},{3,7},{12,8},{8,12},{13,... | collective-permute-start | bytes 3145736 | tf_op jit(solution)/shard_map/ppermute | solution.py:254
  31.9 4.3 %copy-start.1 = (f32[1,1,256,1024]{3,2,1,0:T(8,128)S(1)}, f32[1,1,256,1024]{3,2,1,0:T(8,128)}, u32[]{:S(2)}) copy-start(f32[1,1,256,1024]{3,2,1,0:T(8,128)} %param.4) | copy-start | bytes 3145732
  33.5 16.3 %collective-permute-start.1 = (f32[16,8,1024]{2,1,0:T(8,128)S(1)}, f32[16,8,1024]{2,1,0:T(8,128)}, u32[]{:S(2)}, u32[]{:S(2)}) collective-permute-start(f32[16,8,1024]{2,1,0:T(8,128)S(1)} %get-tuple-element.30), channel_id=1, source_target_pairs={{8,0},{16,8},{24,16},{0,24},{9,1},{17,9},{25,17},{1,25},{10,2},{18... | collective-permute-start | bytes 1572872 | tf_op jit(solution)/shard_map/ppermute | solution.py:254
  36.5 42.7 %collective-permute-start.2 = (f32[16,8,1024]{2,1,0:T(8,128)S(1)}, f32[16,8,1024]{2,1,0:T(8,128)}, u32[]{:S(2)}, u32[]{:S(2)}) collective-permute-start(f32[16,8,1024]{2,1,0:T(8,128)S(1)} %get-tuple-element.32), channel_id=1, source_target_pairs={{16,0},{24,8},{0,16},{8,24},{17,1},{25,9},{1,17},{9,25},{18,2},{26... | collective-permute-start | bytes 1572872 | tf_op jit(solution)/shard_map/ppermute | solution.py:254
  39.7 39.5 %collective-permute-start.3 = (f32[16,8,1024]{2,1,0:T(8,128)S(1)}, f32[16,8,1024]{2,1,0:T(8,128)}, u32[]{:S(2)}, u32[]{:S(2)}) collective-permute-start(f32[16,8,1024]{2,1,0:T(8,128)S(1)} %get-tuple-element.31), channel_id=1, source_target_pairs={{24,0},{0,8},{8,16},{16,24},{25,1},{1,9},{9,17},{17,25},{26,2},{2,... | collective-permute-start | bytes 1572872 | tf_op jit(solution)/shard_map/ppermute | solution.py:254
  42.5 43.5 %collective-permute-start.6 = (f32[256,512]{1,0:T(8,128)}, f32[256,512]{1,0:T(8,128)S(1)}, u32[]{:S(2)}, u32[]{:S(2)}) collective-permute-start(f32[256,512]{1,0:T(8,128)} %pad_maximum_fusion.2), channel_id=1, source_target_pairs={{3,0},{0,1},{1,2},{2,3},{7,4},{4,5},{5,6},{6,7},{11,8},{8,9},{9,10... | collective-permute-start | bytes 1572872 | tf_op jit(solution)/shard_map/ppermute | solution.py:254
  45.5 40.4 %collective-permute-start.4 = (f32[256,512]{1,0:T(8,128)}, f32[256,512]{1,0:T(8,128)S(1)}, u32[]{:S(2)}, u32[]{:S(2)}) collective-permute-start(f32[256,512]{1,0:T(8,128)} %slice.18), channel_id=1, source_target_pairs={{1,0},{2,1},{3,2},{0,3},{5,4},{6,5},{7,6},{4,7},{9,8},{10,9},{11,1... | collective-permute-start | bytes 1572872 | tf_op jit(solution)/shard_map/ppermute | solution.py:254
  49.9 36.9 %collective-permute-start.5 = (f32[256,512]{1,0:T(8,128)}, f32[256,512]{1,0:T(8,128)S(1)}, u32[]{:S(2)}, u32[]{:S(2)}) collective-permute-start(f32[256,512]{1,0:T(8,128)} %slice.18), channel_id=1, source_target_pairs={{2,0},{3,1},{0,2},{1,3},{6,4},{7,5},{4,6},{5,7},{10,8},{11,9},{8,1... | collective-permute-start | bytes 1572872 | tf_op jit(solution)/shard_map/ppermute | solution.py:254
  52.9 24.3 %all-to-all-start.1 = ((f32[16,1,128]{2,1,0:T(1,128)}), f32[16,1,128]{2,1,0:T(1,128)S(1)}, u32[]{:S(2)}, u32[]{:S(2)}) async-start(f32[16,1,128]{2,1,0:T(1,128)} %broadcast_in_dim.85), calls=%async_computation.1 | async-start | bytes 16384 | tf_op jit(solution)/shard_map/all_to_all | solution.py:249
  81.7 58.7 %all-to-all-start.2 = ((f32[16,8,1024]{2,1,0:T(8,128)}), f32[16,8,1024]{2,1,0:T(8,128)}, u32[]{:S(2)}, u32[]{:S(2)}) async-start(f32[16,8,1024]{2,1,0:T(8,128)} %fusion.2), calls=%async_computation.2 | async-start | bytes 1048576 | tf_op jit(solution)/shard_map/all_to_all | solution.py:249
  86.0 0.8 copy-start.4
  86.8 0.8 copy-start.6
  87.6 1.2 copy-start.2
  88.8 1.0 copy-start.5
  89.8 1.0 copy-start.7
  139.6 0.8 copy-start.3
  141.5 64.2 %all-to-all-start.3 = ((bf16[128,16,128]{2,1,0:T(8,128)(2,1)}), bf16[128,16,128]{2,1,0:T(8,128)(2,1)S(1)}, u32[]{:S(2)}, u32[]{:S(2)}) async-start(bf16[128,16,128]{2,1,0:T(8,128)(2,1)} %copy-done.3), calls=%async_computation.3 | async-start | bytes 1048576 | tf_op jit(solution)/shard_map/all_to_all | solution.py:249
  160.4 22.8 %copy-start.9 = (s32[128,1]{0,1:T(1,128)S(1)}, s32[128,1]{0,1:T(1,128)}, u32[]{:S(2)}) copy-start(s32[128,1]{0,1:T(1,128)} %param.6) | copy-start | bytes 1540
  160.4 42.3 %copy-start.8 = (s32[128,1]{0,1:T(1,128)S(1)}, s32[128,1]{0,1:T(1,128)}, u32[]{:S(2)}) copy-start(s32[128,1]{0,1:T(1,128)} %param.7) | copy-start | bytes 1540
  161.7 24.0 %collective-permute-start.7 = (bf16[8,1024]{1,0:T(8,128)(2,1)S(1)}, bf16[8,1024]{1,0:T(8,128)(2,1)S(1)}, u32[]{:S(2)}, u32[]{:S(2)}) collective-permute-start(bf16[8,1024]{1,0:T(8,128)(2,1)S(1)} %convolution_convert_fusion), channel_id=1, source_target_pairs={{128,0},{160,32},{192,64},{224,96},{256,128},{288,160},{320,192},{... | collective-permute-start | bytes 49160 | tf_op jit(solution)/shard_map/ppermute | solution.py:254
  169.5 25.2 %collective-permute-start.8 = (bf16[8,1024]{1,0:T(8,128)(2,1)S(1)}, bf16[8,1024]{1,0:T(8,128)(2,1)S(1)}, u32[]{:S(2)}, u32[]{:S(2)}) collective-permute-start(bf16[8,1024]{1,0:T(8,128)(2,1)S(1)} %convolution_convert_fusion), channel_id=1, source_target_pairs={{256,0},{288,32},{320,64},{352,96},{384,128},{416,160},{448,192},{... | collective-permute-start | bytes 49160 | tf_op jit(solution)/shard_map/ppermute | solution.py:254
  176.1 18.7 %collective-permute-start.9 = (bf16[8,1024]{1,0:T(8,128)(2,1)S(1)}, bf16[8,1024]{1,0:T(8,128)(2,1)S(1)}, u32[]{:S(2)}, u32[]{:S(2)}) collective-permute-start(bf16[8,1024]{1,0:T(8,128)(2,1)S(1)} %convolution_convert_fusion), channel_id=1, source_target_pairs={{384,0},{416,32},{448,64},{480,96},{0,128},{32,160},{64,192},{96,2... | collective-permute-start | bytes 49160 | tf_op jit(solution)/shard_map/ppermute | solution.py:254
  194.8 8.7 %collective-permute-start.10 = (bf16[4,8,1024]{2,1,0:T(8,128)(2,1)S(1)}, bf16[4,8,1024]{2,1,0:T(8,128)(2,1)S(1)}, u32[]{:S(2)}, u32[]{:S(2)}) collective-permute-start(bf16[4,8,1024]{2,1,0:T(8,128)(2,1)S(1)} %get-tuple-element.38), channel_id=1, source_target_pairs={{32,0},{64,32},{96,64},{128,96},{160,128},{192,160},{224,192},{256... | collective-permute-start | bytes 196616 | tf_op jit(solution)/shard_map/ppermute | solution.py:254
  196.7 6.8 %collective-permute-start.11 = (bf16[4,8,1024]{2,1,0:T(8,128)(2,1)S(1)}, bf16[4,8,1024]{2,1,0:T(8,128)(2,1)S(1)}, u32[]{:S(2)}, u32[]{:S(2)}) collective-permute-start(bf16[4,8,1024]{2,1,0:T(8,128)(2,1)S(1)} %get-tuple-element.38), channel_id=1, source_target_pairs={{64,0},{96,32},{128,64},{160,96},{192,128},{224,160},{256,192},{28... | collective-permute-start | bytes 196616 | tf_op jit(solution)/shard_map/ppermute | solution.py:254
  199.4 6.2 %collective-permute-start.12 = (bf16[4,8,1024]{2,1,0:T(8,128)(2,1)S(1)}, bf16[4,8,1024]{2,1,0:T(8,128)(2,1)S(1)}, u32[]{:S(2)}, u32[]{:S(2)}) collective-permute-start(bf16[4,8,1024]{2,1,0:T(8,128)(2,1)S(1)} %get-tuple-element.38), channel_id=1, source_target_pairs={{480,0},{0,32},{32,64},{64,96},{96,128},{128,160},{160,192},{192,2... | collective-permute-start | bytes 196616 | tf_op jit(solution)/shard_map/ppermute | solution.py:254
  207.2 41.8 %copy-start.10 = (s32[128,1]{0,1:T(1,128)S(1)}, s32[128,1]{0,1:T(1,128)}, u32[]{:S(2)}) copy-start(s32[128,1]{0,1:T(1,128)} %param.6) | copy-start | bytes 1540
  207.2 45.8 %all-to-all-start.4 = ((bf16[128,16,128]{2,1,0:T(8,128)(2,1)}), bf16[128,16,128]{2,1,0:T(8,128)(2,1)S(1)}, u32[]{:S(2)}, u32[]{:S(2)}) async-start(bf16[128,16,128]{2,1,0:T(8,128)(2,1)} %shard_map.60), calls=%async_computation.4 | async-start | bytes 1048576 | tf_op jit(solution)/shard_map/all_to_all | solution.py:249
  220.8 13.1 %collective-permute-start.13 = (bf16[4,4,8,1024]{3,2,1,0:T(8,128)(2,1)S(1)}, bf16[4,4,8,1024]{3,2,1,0:T(8,128)(2,1)S(1)}, u32[]{:S(2)}, u32[]{:S(2)}) collective-permute-start(bf16[4,4,8,1024]{3,2,1,0:T(8,128)(2,1)S(1)} %pad_maximum_fusion.3), channel_id=1, source_target_pairs={{8,0},{16,8},{24,16},{0,24},{9,1},{17,9},{25,17},{1,25},{10,2},{18... | collective-permute-start | bytes 786440 | tf_op jit(solution)/shard_map/ppermute | solution.py:254
  225.3 12.4 %collective-permute-start.14 = (bf16[4,4,8,1024]{3,2,1,0:T(8,128)(2,1)S(1)}, bf16[4,4,8,1024]{3,2,1,0:T(8,128)(2,1)S(1)}, u32[]{:S(2)}, u32[]{:S(2)}) collective-permute-start(bf16[4,4,8,1024]{3,2,1,0:T(8,128)(2,1)S(1)} %pad_maximum_fusion.3), channel_id=1, source_target_pairs={{16,0},{24,8},{0,16},{8,24},{17,1},{25,9},{1,17},{9,25},{18,2},{26... | collective-permute-start | bytes 786440 | tf_op jit(solution)/shard_map/ppermute | solution.py:254
  227.8 18.6 %collective-permute-start.15 = (bf16[4,4,8,1024]{3,2,1,0:T(8,128)(2,1)S(1)}, bf16[4,4,8,1024]{3,2,1,0:T(8,128)(2,1)S(1)}, u32[]{:S(2)}, u32[]{:S(2)}) collective-permute-start(bf16[4,4,8,1024]{3,2,1,0:T(8,128)(2,1)S(1)} %pad_maximum_fusion.3), channel_id=1, source_target_pairs={{24,0},{0,8},{8,16},{16,24},{25,1},{1,9},{9,17},{17,25},{26,2},{2,... | collective-permute-start | bytes 786440 | tf_op jit(solution)/shard_map/ppermute | solution.py:254
  246.5 4.8 %collective-permute-start.16 = (bf16[4,4,4,8,1024]{4,3,2,1,0:T(8,128)(2,1)S(1)}, bf16[4,4,4,8,1024]{4,3,2,1,0:T(8,128)(2,1)S(1)}, u32[]{:S(2)}, u32[]{:S(2)}) collective-permute-start(bf16[4,4,4,8,1024]{4,3,2,1,0:T(8,128)(2,1)S(1)} %get-tuple-element.34), channel_id=1, source_target_pairs={{4,0},{0,4},{5,1},{1,5},{6,2},{2,6},{7,3},{3,7},{12,8},{8,12},{13,... | collective-permute-start | bytes 3145736 | tf_op jit(solution)/shard_map/ppermute | solution.py:254

commit v4 on v3

--- a/solution.py
+++ b/solution.py
@@ -43,6 +43,35 @@
 
 def dot(left, right):
     return jnp.dot(left, right, preferred_element_type=jnp.float32)
+
+
+def invert_small(u, size):
+    def at(i, j):
+        return u[min(i, j), max(i, j)]
+
+    for a in range(0, size, 2):
+        b = a + 1
+        aa, ab, bb = u[a, a], u[a, b], u[b, b]
+        scale = reciprocal(aa * bb - ab * ab)
+        others = [i for i in range(size) if i not in (a, b)]
+        row_a = {i: bb * at(a, i) - ab * at(b, i) for i in others}
+        row_b = {i: aa * at(b, i) - ab * at(a, i) for i in others}
+        new = {(a, a): -bb * scale, (a, b): ab * scale, (b, b): -aa * scale}
+        for i in others:
+            new[min(a, i), max(a, i)] = row_a[i] * scale
+            new[min(b, i), max(b, i)] = row_b[i] * scale
+            for j in others:
+                if i <= j:
+                    cross = at(a, i) * row_a[j] + at(b, i) * row_b[j]
+                    new[i, j] = u[i, j] - cross * scale
+        u = new
+    return u
+
+
+def tree_sum(terms):
+    while len(terms) > 1:
+        terms = [a + b for a, b in zip(terms[::2], terms[1::2])]
+    return terms[0]
 
 
 def panel_sweep(groups, first):
@@ -52,41 +81,37 @@
         tile, lane = divmod(first + p * SUB, LANES)
         pivot_lanes = (lane_ids // SUB) == lane // SUB
         spread = [lane_of(groups[p][tile], lane + j) for j in range(SUB)]
-        rows = list(groups[p])
-        rows[tile] = jnp.where(
-            pivot_lanes, jnp.where(lane_ids == sub_ids + lane, 1.0, 0.0), rows[tile]
-        )
-        pivot = row_of(spread[0], 0)
+        u = {(i, j): row_of(spread[j], i) for j in range(SUB) for i in range(j + 1)}
+        sources = []
         for j in range(SUB):
-            here = sub_ids == j
-            scale = reciprocal(pivot)
-            if j + 1 < SUB:
-                cross = row_of(spread[j], j + 1) * row_of(spread[j + 1], j)
-                pivot = row_of(spread[j + 1], j + 1) - cross * scale
-            column = jnp.where(here, -1.0, spread[j])
-
-            def eliminate(x):
-                line = row_of(x, j)
-                return jnp.where(here, 0.0, x) - (column * line) * scale
-
-            rows = [eliminate(x) for x in rows]
-            for i in range(j + 1, SUB):
-                spread[i] = eliminate(spread[i])
-        rows[tile] = jnp.where(pivot_lanes, -rows[tile], rows[tile])
-        lines = [[row_of(x, j) for x in rows] for j in range(SUB)]
+            line = [-row_of(x, j) for x in groups[p]]
+            line[tile] = jnp.where(
+                pivot_lanes, jnp.where(lane_ids == lane + j, 1.0, 0.0), line[tile]
+            )
+            sources.append(line)
+        u = invert_small(u, SUB)
+        tiles = range(len(groups[p]))
+        lines = [
+            [
+                tree_sum([u[min(i, j), max(i, j)] * sources[j][t] for j in range(SUB)])
+                for t in tiles
+            ]
+            for i in range(SUB)
+        ]
         for g in range(len(groups)):
             if g == p:
                 continue
             factors = [lane_of(groups[g][tile], lane + j) for j in range(SUB)]
-            for t in range(len(rows)):
-                terms = [factors[j] * lines[j][t] for j in range(SUB)]
-                while len(terms) > 1:
-                    terms = [a + b for a, b in zip(terms[::2], terms[1::2])]
+            for t in tiles:
                 kept = groups[g][t]
                 if t == tile:
                     kept = jnp.where(pivot_lanes, 0.0, kept)
-                groups[g][t] = kept - terms[0]
-        groups[p] = rows
+                groups[g][t] = kept - tree_sum([factors[j] * lines[j][t] for j in range(SUB)])
+        for t in tiles:
+            row = lines[0][t]
+            for j in range(1, SUB):
+                row = jnp.where(sub_ids == j, lines[j][t], row)
+            groups[p][t] = row
     return groups
 
 
@@ -113,11 +138,10 @@
 
 
 def invert_kernel(
-    scalar_ref, shift_ref, rows_ref, one_hbm, two_hbm, three_hbm,
-    band_ref, full_ref, m_ref, d_ref, left_ref, right_ref, far_ref, far_sem,
+    scalar_ref, traces_ref, rows_hbm, one_hbm, two_hbm, three_hbm,
+    band_hbm, full_ref, m_ref, d_ref, left_ref, right_ref, band_ref, in_sems, out_sem,
 ):
-    n = rows_ref.shape[1]
-    wide = rows_ref.shape[0]
+    wide, n = rows_hbm.shape
     count = n // wide
     mp_index = scalar_ref[1]
 
@@ -129,32 +153,45 @@
 
     @pl.when(scalar_ref[0] > 0)
     def _():
+        arrivals = [(rows_hbm.at[:, place(j)], 0, j) for j in range(count)]
+        for i, source in enumerate((one_hbm, two_hbm, three_hbm)):
+            arrivals.append((source.at[:, block(0)], i + 1, i + 1))
+            arrivals.append((source.at[:, block(1)], i + 1, (i + 1) % (count - 1) + 1))
         copies = [
-            pltpu.make_async_copy(source, far_ref.at[i], far_sem.at[i])
-            for i, source in enumerate((one_hbm, two_hbm, three_hbm))
+            pltpu.make_async_copy(source, m_ref.at[block(i), block(j)], in_sems.at[at])
+            for at, (source, i, j) in enumerate(arrivals)
         ]
         for copy in copies:
             copy.start()
-        eye = jnp.where(
-            lax.broadcasted_iota(jnp.int32, (wide, wide), 0)
-            == lax.broadcasted_iota(jnp.int32, (wide, wide), 1),
-            shift_ref[0],
-            0.0,
+
+        traces = jnp.sum(traces_ref[...], axis=0, keepdims=True)
+        lane_ids = lax.broadcasted_iota(jnp.int32, traces.shape, 1)
+
+        def pick_lane(lane):
+            return jnp.sum(jnp.where(lane_ids == lane, traces, 0.0), axis=1, keepdims=True)
+
+        lane = 2 * scalar_ref[2]
+        ratio = jnp.sqrt(pick_lane(lane) / FF / (pick_lane(lane + 1) / D))
+        shift = jnp.where(scalar_ref[3] > 0, DAMPING_BASE * ratio, DAMPING_BASE / ratio)
+        diagonal = lax.broadcasted_iota(jnp.int32, (wide, wide), 0) == lax.broadcasted_iota(
+            jnp.int32, (wide, wide), 1
         )
-
-        def put(i, j, value):
+        for copy in copies:
+            copy.wait()
+
+        total = jnp.zeros((wide, wide), jnp.float32)
+        for i in range(count):
+            total = total + jnp.where(diagonal, m_ref[block(i), block(i)] + shift, 0.0)
+        total = jnp.sum(jnp.sum(total, axis=0, keepdims=True), axis=1, keepdims=True)
+        scale = n / total
+        for _, i, j in arrivals:
+            value = m_ref[block(i), block(j)]
             if i == j:
-                m_ref[block(i), block(i)] = value + eye
+                m_ref[block(i), block(i)] = jnp.where(diagonal, value + shift, value) * scale
             else:
+                value = value * scale
                 m_ref[block(i), block(j)] = value
                 m_ref[block(j), block(i)] = value.T
-
-        for j in range(count):
-            put(0, j, rows_ref[:, place(j)])
-        for i in range(1, count):
-            copies[i - 1].wait()
-            put(i, i, far_ref[i - 1, :, block(0)])
-            put(i, i % (count - 1) + 1, far_ref[i - 1, :, block(1)])
 
         @pl.loop(0, count)
         def _(k):
@@ -176,46 +213,90 @@
                     m_ref[block(i), :] = m_ref[block(i), :] - dot(left_ref[block(i), :], right_ref[...])
 
         for j in range(count):
-            band = (-m_ref[block(0), block(j)]).astype(jnp.bfloat16)
+            band = (m_ref[block(0), block(j)] * -scale).astype(jnp.bfloat16)
             for r in range(wide // ROWS):
                 for c in range(wide // LANES):
                     at = lax.rem(mp_index + j, count) * (wide // LANES) + r * (n // LANES) + c
                     band_ref[at] = band[r * ROWS : (r + 1) * ROWS, c * LANES : (c + 1) * LANES]
+        sent = pltpu.make_async_copy(band_ref, band_hbm, out_sem)
+        sent.start()
+        for j in range(count):
             for i in range(count):
-                full_ref[place(i), place(j)] = (-m_ref[block(i), block(j)]).astype(jnp.bfloat16)
+                full_ref[place(i), place(j)] = (m_ref[block(i), block(j)] * -scale).astype(jnp.bfloat16)
+        sent.wait()
 
     @pl.when(scalar_ref[0] <= 0)
     def _():
         band_ref[...] = jnp.zeros(band_ref.shape, jnp.bfloat16)
         full_ref[...] = jnp.zeros(full_ref.shape, jnp.bfloat16)
-
-
-def invert(scalars, shift, rows, one, two, three):
+        sent = pltpu.make_async_copy(band_ref, band_hbm, out_sem)
+        sent.start()
+        sent.wait()
+
+
+def invert(scalars, traces, rows, one, two, three):
     wide, n = rows.shape
     in_smem = pl.BlockSpec(memory_space=pltpu.SMEM)
     in_vmem = pl.BlockSpec(memory_space=pltpu.VMEM)
-    anywhere = pl.BlockSpec(memory_space=pl.ANY)
+    in_hbm = pl.BlockSpec(memory_space=pltpu.HBM)
+    pieces = (wide * n // (ROWS * LANES), ROWS, LANES)
     return pl.pallas_call(
         invert_kernel,
         out_shape=(
-            jax.ShapeDtypeStruct((wide * n // (ROWS * LANES), ROWS, LANES), jnp.bfloat16),
+            jax.ShapeDtypeStruct(pieces, jnp.bfloat16),
             jax.ShapeDtypeStruct((n, n), jnp.bfloat16),
         ),
-        in_specs=[in_smem] * 2 + [in_vmem] + [anywhere] * 3,
-        out_specs=(in_vmem, in_vmem),
+        in_specs=[in_smem, in_vmem] + [in_hbm] * 4,
+        out_specs=(in_hbm, in_vmem),
         scratch_shapes=[
             pltpu.VMEM((n, n), jnp.float32),
             pltpu.VMEM((wide, wide), jnp.float32),
             pltpu.VMEM((n, 3 * wide), jnp.bfloat16),
             pltpu.VMEM((3 * wide, n), jnp.bfloat16),
-            pltpu.VMEM((3, wide, 2 * wide), jnp.float32),
-            pltpu.SemaphoreType.DMA((3,)),
+            pltpu.VMEM(pieces, jnp.bfloat16),
+            pltpu.SemaphoreType.DMA((10,)),
+            pltpu.SemaphoreType.DMA,
         ],
         compiler_params=pltpu.CompilerParams(vmem_limit_bytes=24 * 1024 * 1024),
         cost_estimate=pl.CostEstimate(
             flops=36 * n * n * n, bytes_accessed=6 * n * n, transcendentals=0
         ),
-    )(scalars, shift, rows, one, two, three)
+    )(scalars, traces, rows, one, two, three)
+
+
+def prepare_kernel(mp_ref, rows_ref, near_ref, far_ref, trace_ref):
+    wide, n = rows_ref.shape
+
+    def place(i):
+        return pl.ds(pl.multiple_of(lax.rem(mp_ref[0] + i, n // wide) * wide, wide), wide)
+
+    own = rows_ref[:, place(0)]
+    diagonal = lax.broadcasted_iota(jnp.int32, own.shape, 0) == lax.broadcasted_iota(
+        jnp.int32, own.shape, 1
+    )
+    trace = jnp.sum(jnp.where(diagonal, own, 0.0), axis=0, keepdims=True)
+    trace = jnp.sum(trace, axis=1, keepdims=True)
+    trace_ref[...] = jnp.broadcast_to(trace[None], trace_ref.shape)
+    near_ref[:, :wide] = own
+    near_ref[:, wide:] = rows_ref[:, place(1)]
+    far_ref[:, :wide] = own
+    far_ref[:, wide:] = rows_ref[:, place(2)]
+
+
+def prepare(mp_index, rows, copies):
+    wide, n = rows.shape
+    in_vmem = pl.BlockSpec(memory_space=pltpu.VMEM)
+    return pl.pallas_call(
+        prepare_kernel,
+        out_shape=(
+            jax.ShapeDtypeStruct((wide, 2 * wide), jnp.float32),
+            jax.ShapeDtypeStruct((wide, 2 * wide), jnp.float32),
+            jax.ShapeDtypeStruct((copies, 1, LANES), jnp.float32),
+        ),
+        in_specs=[pl.BlockSpec(memory_space=pltpu.SMEM), in_vmem],
+        out_specs=(in_vmem,) * 3,
+        compiler_params=pltpu.CompilerParams(vmem_limit_bytes=8 * 1024 * 1024),
+    )(mp_index.reshape(1).astype(jnp.int32), rows)
 
 
 def pick_kernel(index_ref, src_ref, out_ref):
@@ -252,10 +333,6 @@
 def from_ahead(value, axis, step):
     count = lax.axis_size(axis)
     return lax.ppermute(value, axis, [((i + step) % count, i) for i in range(count)])
-
-
-def sum_of_all(value, axes, count):
-    return jnp.sum(exchange(jnp.broadcast_to(value[None], (count,) + value.shape), axes), axis=0)
 
 
 def local(old_factors, gradients, old_slots, new_slots):
@@ -278,57 +355,48 @@
     own_input = own_block % layer_blocks < a_span
 
     rows = old_factors[0, 0]
-    trace = jnp.trace(lax.dynamic_slice_in_dim(rows, mp_index * band, band, 1))
-    bins = lax.broadcasted_iota(jnp.int32, (1, 128), 1)
-    own_bin = jnp.where(own >= 0, 2 * own_layer + jnp.where(own_input, 0, 1), -1)
-    binned = jnp.where(bins == own_bin, trace, 0.0)
-    binned, rows = lax.optimization_barrier((binned, rows))
-    binned = sum_of_all(binned, ("x", "c", "mp"), x_count * c_count * mp_count)
-    binned, tiles = lax.optimization_barrier((binned, gradients[0]))
-    binned = sum_of_all(binned, "z", z_count)
-    trace_input = jnp.sum(jnp.where(bins == 2 * own_layer, binned, 0.0))
-    trace_output = jnp.sum(jnp.where(bins == 2 * own_layer + 1, binned, 0.0))
-    ratio = jnp.sqrt(trace_input / FF / (trace_output / D))
-    shift = jnp.where(own_input, DAMPING_BASE * ratio, DAMPING_BASE / ratio)
-
-    doubled = jnp.concatenate([rows, rows], axis=1)
-    ahead = lax.dynamic_slice_in_dim(doubled, mp_index * band, 3 * band, 1)
-    near = ahead[:, : 2 * band]
-    far = jnp.concatenate([ahead[:, :band], ahead[:, 2 * band :]], axis=1)
+    near, far, trace = prepare(mp_index, rows, x_count * c_count * mp_count)
+    trace = exchange(trace, ("x", "c", "mp")).reshape(x_count * c_count, mp_count, LANES)
+    plane = lax.dynamic_slice_in_dim(old_flat, z * x_count * c_count, x_count * c_count)
+    plane_bin = 2 * (plane // layer_blocks) + jnp.where(plane % layer_blocks < a_span, 0, 1)
+    plane_bin = jnp.where(plane >= 0, plane_bin, -1)
+    lane_ids = lax.broadcasted_iota(jnp.int32, (1, 1, LANES), 2)
+    binned = jnp.sum(jnp.where(lane_ids == plane_bin[:, None, None], trace, 0.0), axis=(0, 1))
+    binned, near, far, tiles = lax.optimization_barrier((binned, near, far, gradients[0]))
+    binned = jnp.broadcast_to(binned[None, None], (z_count, 1, LANES))
+    traces = exchange(binned, "z").reshape(z_count, LANES)
+
     one = from_ahead(near, "mp", 1)
     two = from_ahead(near, "mp", 2)
     three = from_ahead(far, "mp", 3)
 
     block = jnp.maximum(old_flat, 0)
     tile_of = jnp.minimum(block // layer_blocks * a_span + block % layer_blocks, tile_count - 1)
-    tile_of = tile_of.reshape(z_count, x_count, c_count).transpose(2, 1, 0)
+    tile_of = tile_of.reshape(z_count * x_count, c_count)
 
     def tiles_of(core):
-        index = lax.dynamic_index_in_dim(tile_of, core, keepdims=False)
-        return take(tiles, index.reshape(-1))
-
-    def split(value):
-        return value.astype(jnp.float32).reshape(x_count, z_count, row_count, width)
+        return take(tiles, lax.dynamic_index_in_dim(tile_of, core, 1, keepdims=False))
 
     arrived = from_ahead(tiles_of(1 - c), "c", 1)
-    partial = split(tiles_of(c)) + split(arrived)
-    total = lax.dynamic_index_in_dim(partial, x, keepdims=False)
-    for step in range(1, x_count):
-        piece = lax.dynamic_index_in_dim(partial, (x + x_count - step) % x_count, keepdims=False)
-        total = total + from_ahead(piece, "x", step)
-    shift, total = lax.optimization_barrier((shift, total))
-    tile = jnp.sum(exchange(total, "z"), axis=0).astype(jnp.bfloat16)
-
-    scalars = jnp.stack([(own >= 0).astype(jnp.int32), mp_index.astype(jnp.int32)])
-    inverse_band, inverse = invert(scalars, shift.reshape(1), rows, one, two, three)
+    partial = tiles_of(c).astype(jnp.float32) + arrived.astype(jnp.float32)
+    partial, traces = lax.optimization_barrier((partial.astype(jnp.bfloat16), traces))
+    partial = exchange(partial, ("z", "x"))
+    tile = jnp.sum(partial.astype(jnp.float32), axis=0).astype(jnp.bfloat16)
+
+    scalars = jnp.stack(
+        [v.astype(jnp.int32) for v in (own >= 0, mp_index, own_layer, own_input)]
+    )
+    inverse_band, inverse = invert(scalars, traces, rows, one, two, three)
     inverse_band, tile = lax.optimization_barrier((inverse_band, tile))
 
     def gather(value, axis, steps):
         return jnp.stack([value] + [from_ahead(value, axis, step) for step in steps])
 
     held = jnp.dot(tile, inverse, preferred_element_type=jnp.float32).astype(jnp.bfloat16)
+    held = gather(held, "z", (4, 8, 12))
+    inverse_band, held = lax.optimization_barrier((inverse_band, held))
     spread = exchange(inverse_band, DP)
-    held = gather(gather(held, "z", (4, 8, 12)), "z", (1, 2, 15))
+    held = gather(held, "z", (1, 2, 15))
     slot_range = jnp.arange(dp_count, dtype=jnp.int32)
     empty = jnp.min(jnp.where(old_flat >= 0, dp_count - 1, slot_range))
     source = jnp.where(new_flat >= 0, positions(old_flat, new_flat), empty)

time: 256 us -> 244 us (0.953)
  Pallas kernels: 50.3 us -> 3.99 us
  waiting for transfers between devices: 48.5 us -> 90.2 us
  other arithmetic: 16.1 us -> 9.56 us
    pallas_call x1 -> x2, Pallas kernels: 48.7 us -> 2.44 us  [the longest x1 1.69 us: invert(): pl.pallas_call(invert_kernel, out_shape=(jax.ShapeDtypeStruct(pieces, jnp...]
    all_to_all x5, waiting for transfers between devices: 15.7 us -> 54.4 us  [exchange(): return lax.all_to_all(pieces, axes, split_axis=0, concat_axis=0, tiled=True)]
    add x2 -> x0, other arithmetic: 5.41 us -> none  [the longest x1 2.94 us: local(): partial = split(tiles_of(c)) + split(arrived)]
    ppermute x17 -> x14, waiting for transfers between devices: 32.8 us -> 35.8 us  [from_ahead(): lax.ppermute(value, axis, [((i + step) % count, i) for i in range(count)])]
    convert_element_type x0 -> x1, other arithmetic: none -> 2.93 us  [local(): partial.astype(jnp.bfloat16)]
    ppermute x17 -> x14, starting transfers between devices: 60.3 us -> 63.2 us  [from_ahead(): lax.ppermute(value, axis, [((i + step) % count, i) for i in range(count)])]
    all_to_all x5, starting transfers between devices: 60.1 us -> 57.5 us  [exchange(): return lax.all_to_all(pieces, axes, split_axis=0, concat_axis=0, tiled=True)]
    unnamed x22 -> x18, local copies, waits for them, and re-layouts: 5.7 us -> 6.21 us
  transfers between devices with their start and end apart: 22 -> 19, of which waited for: 10 -> 13; matrix products, arithmetic and copies ran while one was open for 5% -> 5% of each run, Pallas kernels for 19% -> 1%
where the time goes in v4:
time: 244 us; the launch traced here: 242 us
  starting transfers between devices  121 us (50%)
  waiting for transfers between devices  90.2 us (37%)
  local copies, waits for them, and re-layouts  13.2 us (5%)
  other arithmetic  9.56 us (4%)
  Pallas kernels  3.99 us (2%)
  between operations  3.59 us (1%)
    ppermute x14, starting transfers between devices, from_ahead(): lax.ppermute(value, axis, [((i + step) % count, i) for i in range(count)])  63.2 us
    all_to_all x5, starting transfers between devices, exchange(): return lax.all_to_all(pieces, axes, split_axis=0, concat_axis=0, tiled=True)  57.5 us
    all_to_all x5, waiting for transfers between devices, exchange(): return lax.all_to_all(pieces, axes, split_axis=0, concat_axis=0, tiled=True)  54.4 us
    ppermute x14, waiting for transfers between devices, from_ahead(): lax.ppermute(value, axis, [((i + step) % count, i) for i in range(count)])  35.8 us
    unnamed x18, local copies, waits for them, and re-layouts  6.21 us
  transfers between devices with their start and end apart: 19, of which 13 were waited for; matrix products, arithmetic and copies ran while one was open for 5% of the time, Pallas kernels for 1%

profile of v4, /device:TPU:1, one launch (start us, length us, event | category | flops | bytes accessed | tf_op | source)
XLA Modules:
  0.0 241.5 jit_solution(11270146295188171813)
XLA Ops:
  0.7 1.3 copy-done.1
  2.0 0.8 shard_map.59
  2.7 10.4 %all-to-all-start = ((f32[32,1,128]{2,1,0:T(1,128)}), f32[32,1,128]{2,1,0:T(1,128)S(1)}, u32[]{:S(2)}, u32[]{:S(2)}) async-start(f32[32,1,128]{2,1,0:T(1,128)} %get-tuple-element.19), calls=%async_computation | async-start | bytes 32768 | tf_op jit(solution)/shard_map/all_to_all | solution.py:330
  13.1 0.7 compare_reduce_fusion
  13.8 0.7 remainder_reduce_fusion
  14.5 0.7 bitcast_select_fusion
  15.3 0.1 ne.276
  15.4 0.1 rem.194
  15.6 0.1 div.69
  15.7 0.2 fusion.3
  15.9 4.1 %all-to-all-done = f32[32,1,128]{2,1,0:T(1,128)S(1)} async-done(((f32[32,1,128]{2,1,0:T(1,128)}), f32[32,1,128]{2,1,0:T(1,128)S(1)}, u32[]{:S(2)}, u32[]{:S(2)}) %all-to-all-start) | async-done | bytes 16416 | tf_op jit(solution)/shard_map/all_to_all | solution.py:330
  20.1 1.6 gather_fusion.1
  21.7 2.5 %collective-permute-start = (bf16[64,8,1024]{2,1,0:T(8,128)(2,1)}, bf16[64,8,1024]{2,1,0:T(8,128)(2,1)}, u32[]{:S(2)}, u32[]{:S(2)}) collective-permute-start(bf16[64,8,1024]{2,1,0:T(8,128)(2,1)} %gather_fusion.1), channel_id=1, source_target_pairs={{4,0},{0,4},{5,1},{1,5},{6,2},{2,6},{7,3},{3,7},{12,8},{8,12},{13,... | collective-permute-start | bytes 3145736 | tf_op jit(solution)/shard_map/ppermute | solution.py:335
  24.3 2.8 %collective-permute-start.2 = (f32[256,512]{1,0:T(8,128)S(1)}, f32[256,512]{1,0:T(8,128)S(1)}, u32[]{:S(2)}, u32[]{:S(2)}) collective-permute-start(f32[256,512]{1,0:T(8,128)S(1)} %get-tuple-element.25), channel_id=1, source_target_pairs={{2,0},{3,1},{0,2},{1,3},{6,4},{7,5},{4,6},{5,7},{10,8},{11,9},{8,1... | collective-permute-start | bytes 1572872 | tf_op jit(solution)/shard_map/ppermute | solution.py:335
  27.1 3.7 %collective-permute-start.1 = (f32[256,512]{1,0:T(8,128)S(1)}, f32[256,512]{1,0:T(8,128)S(1)}, u32[]{:S(2)}, u32[]{:S(2)}) collective-permute-start(f32[256,512]{1,0:T(8,128)S(1)} %get-tuple-element.25), channel_id=1, source_target_pairs={{1,0},{2,1},{3,2},{0,3},{5,4},{6,5},{7,6},{4,7},{9,8},{10,9},{11,1... | collective-permute-start | bytes 1572872 | tf_op jit(solution)/shard_map/ppermute | solution.py:335
  30.8 0.6 broadcast_in_dim.76
  31.4 13.0 %all-to-all-start.1 = ((f32[16,1,128]{2,1,0:T(1,128)}), f32[16,1,128]{2,1,0:T(1,128)S(1)}, u32[]{:S(2)}, u32[]{:S(2)}) async-start(f32[16,1,128]{2,1,0:T(1,128)} %broadcast_in_dim.76), calls=%async_computation.1 | async-start | bytes 16384 | tf_op jit(solution)/shard_map/all_to_all | solution.py:330
  44.5 1.9 collective-permute-start.3
  46.4 1.6 gather_fusion
  48.0 2.9 %add_convert_fusion = bf16[64,8,1024]{2,1,0:T(8,128)(2,1)} fusion(bf16[64,8,1024]{2,1,0:T(8,128)(2,1)} %collective-permute-done, bf16[64,8,1024]{2,1,0:T(8,128)(2,1)} %gather_fusion), kind=kLoop, calls=%fused_computation.4 | loop fusion | flops 2097152 | bytes 3145728 | tf_op jit(solution)/shard_map/convert_element_type | solution.py:382
  50.9 4.8 %all-to-all-done.1 = f32[16,1,128]{2,1,0:T(1,128)S(1)} async-done(((f32[16,1,128]{2,1,0:T(1,128)}), f32[16,1,128]{2,1,0:T(1,128)S(1)}, u32[]{:S(2)}, u32[]{:S(2)}) %all-to-all-start.1) | async-done | bytes 8224 | tf_op jit(solution)/shard_map/all_to_all | solution.py:330
  55.7 8.5 %all-to-all-start.2 = ((bf16[64,8,1024]{2,1,0:T(8,128)(2,1)}), bf16[64,8,1024]{2,1,0:T(8,128)(2,1)}, u32[]{:S(2)}, u32[]{:S(2)}) async-start(bf16[64,8,1024]{2,1,0:T(8,128)(2,1)} %add_convert_fusion), calls=%async_computation.2 | async-start | bytes 2097152 | tf_op jit(solution)/shard_map/all_to_all | solution.py:330
  64.2 0.6 fusion.23
  67.4 0.1 pad_add_fusion.scalar_ref
  67.5 0.8 copy-done.5
  68.3 0.8 copy-done.3
  69.1 1.2 copy-done.2
  70.4 1.0 copy-done.4
  71.4 1.0 copy-done.6
  72.4 1.7 shard_map.60
  74.1 40.7 %all-to-all-done.2 = bf16[64,8,1024]{2,1,0:T(8,128)(2,1)} async-done(((bf16[64,8,1024]{2,1,0:T(8,128)(2,1)}), bf16[64,8,1024]{2,1,0:T(8,128)(2,1)}, u32[]{:S(2)}, u32[]{:S(2)}) %all-to-all-start.2) | async-done | bytes 1048608 | tf_op jit(solution)/shard_map/all_to_all | solution.py:330
  114.9 1.4 reduce_sum.43
  116.3 0.4 convolution_convert_fusion
  116.7 17.9 %collective-permute-start.6 = (bf16[8,1024]{1,0:T(8,128)(2,1)S(1)}, bf16[8,1024]{1,0:T(8,128)(2,1)S(1)}, u32[]{:S(2)}, u32[]{:S(2)}) collective-permute-start(bf16[8,1024]{1,0:T(8,128)(2,1)S(1)} %convolution_convert_fusion), channel_id=1, source_target_pairs={{384,0},{416,32},{448,64},{480,96},{0,128},{32,160},{64,192},{96,2... | collective-permute-start | bytes 49160 | tf_op jit(solution)/shard_map/ppermute | solution.py:335
  134.6 7.2 %collective-permute-start.5 = (bf16[8,1024]{1,0:T(8,128)(2,1)S(1)}, bf16[8,1024]{1,0:T(8,128)(2,1)S(1)}, u32[]{:S(2)}, u32[]{:S(2)}) collective-permute-start(bf16[8,1024]{1,0:T(8,128)(2,1)S(1)} %convolution_convert_fusion), channel_id=1, source_target_pairs={{256,0},{288,32},{320,64},{352,96},{384,128},{416,160},{448,192},{... | collective-permute-start | bytes 49160 | tf_op jit(solution)/shard_map/ppermute | solution.py:335
  141.8 1.9 collective-permute-start.4
  143.7 4.2 %collective-permute-done.5 = bf16[8,1024]{1,0:T(8,128)(2,1)S(1)} collective-permute-done((bf16[8,1024]{1,0:T(8,128)(2,1)S(1)}, bf16[8,1024]{1,0:T(8,128)(2,1)S(1)}, u32[]{:S(2)}, u32[]{:S(2)}) %collective-permute-start.5) | collective-permute-done | bytes 16416 | tf_op jit(solution)/shard_map/ppermute | solution.py:335
  147.9 2.9 %collective-permute-done.4 = bf16[8,1024]{1,0:T(8,128)(2,1)S(1)} collective-permute-done((bf16[8,1024]{1,0:T(8,128)(2,1)S(1)}, bf16[8,1024]{1,0:T(8,128)(2,1)S(1)}, u32[]{:S(2)}, u32[]{:S(2)}) %collective-permute-start.4) | collective-permute-done | bytes 16416 | tf_op jit(solution)/shard_map/ppermute | solution.py:335
  150.8 13.4 %all-to-all-start.3 = ((bf16[128,16,128]{2,1,0:T(8,128)(2,1)}), bf16[128,16,128]{2,1,0:T(8,128)(2,1)S(1)}, u32[]{:S(2)}, u32[]{:S(2)}) async-start(bf16[128,16,128]{2,1,0:T(8,128)(2,1)} %get-tuple-element.32), calls=%async_computation.3 | async-start | bytes 1048576 | tf_op jit(solution)/shard_map/all_to_all | solution.py:330
  164.2 0.6 fusion.11
  164.8 0.2 select_reduce_fusion
  165.0 3.3 %collective-permute-start.9 = (bf16[4,8,1024]{2,1,0:T(8,128)(2,1)S(1)}, bf16[4,8,1024]{2,1,0:T(8,128)(2,1)S(1)}, u32[]{:S(2)}, u32[]{:S(2)}) collective-permute-start(bf16[4,8,1024]{2,1,0:T(8,128)(2,1)S(1)} %pad_maximum_fusion.3), channel_id=1, source_target_pairs={{480,0},{0,32},{32,64},{64,96},{96,128},{128,160},{160,192},{192,2... | collective-permute-start | bytes 196616 | tf_op jit(solution)/shard_map/ppermute | solution.py:335
  168.3 5.0 %collective-permute-start.8 = (bf16[4,8,1024]{2,1,0:T(8,128)(2,1)S(1)}, bf16[4,8,1024]{2,1,0:T(8,128)(2,1)S(1)}, u32[]{:S(2)}, u32[]{:S(2)}) collective-permute-start(bf16[4,8,1024]{2,1,0:T(8,128)(2,1)S(1)} %pad_maximum_fusion.3), channel_id=1, source_target_pairs={{64,0},{96,32},{128,64},{160,96},{192,128},{224,160},{256,192},{28... | collective-permute-start | bytes 196616 | tf_op jit(solution)/shard_map/ppermute | solution.py:335
  173.3 3.0 %collective-permute-start.7 = (bf16[4,8,1024]{2,1,0:T(8,128)(2,1)S(1)}, bf16[4,8,1024]{2,1,0:T(8,128)(2,1)S(1)}, u32[]{:S(2)}, u32[]{:S(2)}) collective-permute-start(bf16[4,8,1024]{2,1,0:T(8,128)(2,1)S(1)} %pad_maximum_fusion.3), channel_id=1, source_target_pairs={{32,0},{64,32},{96,64},{128,96},{160,128},{192,160},{224,192},{256... | collective-permute-start | bytes 196616 | tf_op jit(solution)/shard_map/ppermute | solution.py:335
  176.4 0.7 compare_select_fusion.16.index_ref
  177.0 13.5 %collective-permute-done.9 = bf16[4,8,1024]{2,1,0:T(8,128)(2,1)S(1)} collective-permute-done((bf16[4,8,1024]{2,1,0:T(8,128)(2,1)S(1)}, bf16[4,8,1024]{2,1,0:T(8,128)(2,1)S(1)}, u32[]{:S(2)}, u32[]{:S(2)}) %collective-permute-start.9) | collective-permute-done | bytes 65568 | tf_op jit(solution)/shard_map/ppermute | solution.py:335
  190.5 1.8 collective-permute-done.7
  192.3 3.5 %all-to-all-done.3.src_ref = bf16[128,16,128]{2,1,0:T(8,128)(2,1)S(1)} async-done(((bf16[128,16,128]{2,1,0:T(8,128)(2,1)}), bf16[128,16,128]{2,1,0:T(8,128)(2,1)S(1)}, u32[]{:S(2)}, u32[]{:S(2)}) %all-to-all-start.3) | async-done | bytes 524320 | tf_op jit(solution)/shard_map/all_to_all | solution.py:330
  195.8 1.6 shard_map.61
  197.4 12.2 %all-to-all-start.4 = ((bf16[128,16,128]{2,1,0:T(8,128)(2,1)}), bf16[128,16,128]{2,1,0:T(8,128)(2,1)S(1)}, u32[]{:S(2)}, u32[]{:S(2)}) async-start(bf16[128,16,128]{2,1,0:T(8,128)(2,1)} %shard_map.61), calls=%async_computation.4 | async-start | bytes 1048576 | tf_op jit(solution)/shard_map/all_to_all | solution.py:330
  209.5 3.3 %collective-permute-start.12 = (bf16[4,4,8,1024]{3,2,1,0:T(8,128)(2,1)S(1)}, bf16[4,4,8,1024]{3,2,1,0:T(8,128)(2,1)S(1)}, u32[]{:S(2)}, u32[]{:S(2)}) collective-permute-start(bf16[4,4,8,1024]{3,2,1,0:T(8,128)(2,1)S(1)} %pad_maximum_fusion.2), channel_id=1, source_target_pairs={{24,0},{0,8},{8,16},{16,24},{25,1},{1,9},{9,17},{17,25},{26,2},{2,... | collective-permute-start | bytes 786440 | tf_op jit(solution)/shard_map/ppermute | solution.py:335
  212.8 4.3 %collective-permute-start.11 = (bf16[4,4,8,1024]{3,2,1,0:T(8,128)(2,1)S(1)}, bf16[4,4,8,1024]{3,2,1,0:T(8,128)(2,1)S(1)}, u32[]{:S(2)}, u32[]{:S(2)}) collective-permute-start(bf16[4,4,8,1024]{3,2,1,0:T(8,128)(2,1)S(1)} %pad_maximum_fusion.2), channel_id=1, source_target_pairs={{16,0},{24,8},{0,16},{8,24},{17,1},{25,9},{1,17},{9,25},{18,2},{26... | collective-permute-start | bytes 786440 | tf_op jit(solution)/shard_map/ppermute | solution.py:335
  217.2 3.1 %collective-permute-start.10 = (bf16[4,4,8,1024]{3,2,1,0:T(8,128)(2,1)S(1)}, bf16[4,4,8,1024]{3,2,1,0:T(8,128)(2,1)S(1)}, u32[]{:S(2)}, u32[]{:S(2)}) collective-permute-start(bf16[4,4,8,1024]{3,2,1,0:T(8,128)(2,1)S(1)} %pad_maximum_fusion.2), channel_id=1, source_target_pairs={{8,0},{16,8},{24,16},{0,24},{9,1},{17,9},{25,17},{1,25},{10,2},{18... | collective-permute-start | bytes 786440 | tf_op jit(solution)/shard_map/ppermute | solution.py:335
  220.3 9.9 %collective-permute-done.11 = bf16[4,4,8,1024]{3,2,1,0:T(8,128)(2,1)S(1)} collective-permute-done((bf16[4,4,8,1024]{3,2,1,0:T(8,128)(2,1)S(1)}, bf16[4,4,8,1024]{3,2,1,0:T(8,128)(2,1)S(1)}, u32[]{:S(2)}, u32[]{:S(2)}) %collective-permute-start.11) | collective-permute-done | bytes 262176 | tf_op jit(solution)/shard_map/ppermute | solution.py:335
  230.2 1.5 collective-permute-done.10
  231.7 0.2 fusion.22
  231.9 3.1 %collective-permute-start.13 = (bf16[4,4,4,8,1024]{4,3,2,1,0:T(8,128)(2,1)S(1)}, bf16[4,4,4,8,1024]{4,3,2,1,0:T(8,128)(2,1)S(1)}, u32[]{:S(2)}, u32[]{:S(2)}) collective-permute-start(bf16[4,4,4,8,1024]{4,3,2,1,0:T(8,128)(2,1)S(1)} %get-tuple-element.41), channel_id=1, source_target_pairs={{4,0},{0,4},{5,1},{1,5},{6,2},{2,6},{7,3},{3,7},{12,8},{8,12},{13,... | collective-permute-start | bytes 3145736 | tf_op jit(solution)/shard_map/ppermute | solution.py:335
  235.1 0.2 select_reduce_fusion.1
  235.3 2.0 collective-permute-done.13
  237.3 0.2 pad_maximum_fusion
  237.5 1.6 gather_fusion.2
  239.1 1.3 all-to-all-done.4
  240.4 0.1 copy.12
  240.5 1.0 reshape.483
  (30 shorter events, 0.4 us)
Async XLA Ops:
  0.6 19.5 %copy-start = (bf16[1,56,8,1024]{3,2,1,0:T(8,128)(2,1)S(1)}, bf16[1,56,8,1024]{3,2,1,0:T(8,128)(2,1)}, u32[]{:S(2)}) copy-start(bf16[1,56,8,1024]{3,2,1,0:T(8,128)(2,1)} %param.5) | copy-start | bytes 2752516
  0.6 1.3 copy-start.1
  2.7 17.3 %all-to-all-start = ((f32[32,1,128]{2,1,0:T(1,128)}), f32[32,1,128]{2,1,0:T(1,128)S(1)}, u32[]{:S(2)}, u32[]{:S(2)}) async-start(f32[32,1,128]{2,1,0:T(1,128)} %get-tuple-element.19), calls=%async_computation | async-start | bytes 32768 | tf_op jit(solution)/shard_map/all_to_all | solution.py:330
  21.7 26.2 %collective-permute-start = (bf16[64,8,1024]{2,1,0:T(8,128)(2,1)}, bf16[64,8,1024]{2,1,0:T(8,128)(2,1)}, u32[]{:S(2)}, u32[]{:S(2)}) collective-permute-start(bf16[64,8,1024]{2,1,0:T(8,128)(2,1)} %gather_fusion.1), channel_id=1, source_target_pairs={{4,0},{0,4},{5,1},{1,5},{6,2},{2,6},{7,3},{3,7},{12,8},{8,12},{13,... | collective-permute-start | bytes 3145736 | tf_op jit(solution)/shard_map/ppermute | solution.py:335
  24.3 44.0 %collective-permute-start.2 = (f32[256,512]{1,0:T(8,128)S(1)}, f32[256,512]{1,0:T(8,128)S(1)}, u32[]{:S(2)}, u32[]{:S(2)}) collective-permute-start(f32[256,512]{1,0:T(8,128)S(1)} %get-tuple-element.25), channel_id=1, source_target_pairs={{2,0},{3,1},{0,2},{1,3},{6,4},{7,5},{4,6},{5,7},{10,8},{11,9},{8,1... | collective-permute-start | bytes 1572872 | tf_op jit(solution)/shard_map/ppermute | solution.py:335
  27.1 41.2 %collective-permute-start.1 = (f32[256,512]{1,0:T(8,128)S(1)}, f32[256,512]{1,0:T(8,128)S(1)}, u32[]{:S(2)}, u32[]{:S(2)}) collective-permute-start(f32[256,512]{1,0:T(8,128)S(1)} %get-tuple-element.25), channel_id=1, source_target_pairs={{1,0},{2,1},{3,2},{0,3},{5,4},{6,5},{7,6},{4,7},{9,8},{10,9},{11,1... | collective-permute-start | bytes 1572872 | tf_op jit(solution)/shard_map/ppermute | solution.py:335
  31.4 24.3 %all-to-all-start.1 = ((f32[16,1,128]{2,1,0:T(1,128)}), f32[16,1,128]{2,1,0:T(1,128)S(1)}, u32[]{:S(2)}, u32[]{:S(2)}) async-start(f32[16,1,128]{2,1,0:T(1,128)} %broadcast_in_dim.76), calls=%async_computation.1 | async-start | bytes 16384 | tf_op jit(solution)/shard_map/all_to_all | solution.py:330
  44.5 23.1 %collective-permute-start.3 = (f32[256,512]{1,0:T(8,128)S(1)}, f32[256,512]{1,0:T(8,128)S(1)}, u32[]{:S(2)}, u32[]{:S(2)}) collective-permute-start(f32[256,512]{1,0:T(8,128)S(1)} %get-tuple-element.26), channel_id=1, source_target_pairs={{3,0},{0,1},{1,2},{2,3},{7,4},{4,5},{5,6},{6,7},{11,8},{8,9},{9,10... | collective-permute-start | bytes 1572872 | tf_op jit(solution)/shard_map/ppermute | solution.py:335
  48.0 16.3 %copy-start.8 = (s32[128,1]{0,1:T(1,128)S(1)}, s32[128,1]{0,1:T(1,128)}, u32[]{:S(2)}) copy-start(s32[128,1]{0,1:T(1,128)} %param.6) | copy-start | bytes 1540
  55.7 59.2 %all-to-all-start.2 = ((bf16[64,8,1024]{2,1,0:T(8,128)(2,1)}), bf16[64,8,1024]{2,1,0:T(8,128)(2,1)}, u32[]{:S(2)}, u32[]{:S(2)}) async-start(bf16[64,8,1024]{2,1,0:T(8,128)(2,1)} %add_convert_fusion), calls=%async_computation.2 | async-start | bytes 2097152 | tf_op jit(solution)/shard_map/all_to_all | solution.py:330
  67.5 0.8 copy-start.5
  68.3 0.8 copy-start.3
  69.1 1.2 copy-start.2
  70.4 1.0 copy-start.4
  71.4 1.0 copy-start.6
  74.1 90.7 %copy-start.7 = (s32[128,1]{0,1:T(1,128)S(1)}, s32[128,1]{0,1:T(1,128)}, u32[]{:S(2)}) copy-start(s32[128,1]{0,1:T(1,128)} %param.7) | copy-start | bytes 1540
  116.7 27.1 %collective-permute-start.6 = (bf16[8,1024]{1,0:T(8,128)(2,1)S(1)}, bf16[8,1024]{1,0:T(8,128)(2,1)S(1)}, u32[]{:S(2)}, u32[]{:S(2)}) collective-permute-start(bf16[8,1024]{1,0:T(8,128)(2,1)S(1)} %convolution_convert_fusion), channel_id=1, source_target_pairs={{384,0},{416,32},{448,64},{480,96},{0,128},{32,160},{64,192},{96,2... | collective-permute-start | bytes 49160 | tf_op jit(solution)/shard_map/ppermute | solution.py:335
  134.6 13.3 %collective-permute-start.5 = (bf16[8,1024]{1,0:T(8,128)(2,1)S(1)}, bf16[8,1024]{1,0:T(8,128)(2,1)S(1)}, u32[]{:S(2)}, u32[]{:S(2)}) collective-permute-start(bf16[8,1024]{1,0:T(8,128)(2,1)S(1)} %convolution_convert_fusion), channel_id=1, source_target_pairs={{256,0},{288,32},{320,64},{352,96},{384,128},{416,160},{448,192},{... | collective-permute-start | bytes 49160 | tf_op jit(solution)/shard_map/ppermute | solution.py:335
  141.8 9.0 %collective-permute-start.4 = (bf16[8,1024]{1,0:T(8,128)(2,1)S(1)}, bf16[8,1024]{1,0:T(8,128)(2,1)S(1)}, u32[]{:S(2)}, u32[]{:S(2)}) collective-permute-start(bf16[8,1024]{1,0:T(8,128)(2,1)S(1)} %convolution_convert_fusion), channel_id=1, source_target_pairs={{128,0},{160,32},{192,64},{224,96},{256,128},{288,160},{320,192},{... | collective-permute-start | bytes 49160 | tf_op jit(solution)/shard_map/ppermute | solution.py:335
  150.8 45.1 %all-to-all-start.3 = ((bf16[128,16,128]{2,1,0:T(8,128)(2,1)}), bf16[128,16,128]{2,1,0:T(8,128)(2,1)S(1)}, u32[]{:S(2)}, u32[]{:S(2)}) async-start(bf16[128,16,128]{2,1,0:T(8,128)(2,1)} %get-tuple-element.32), calls=%async_computation.3 | async-start | bytes 1048576 | tf_op jit(solution)/shard_map/all_to_all | solution.py:330
  165.0 25.5 %collective-permute-start.9 = (bf16[4,8,1024]{2,1,0:T(8,128)(2,1)S(1)}, bf16[4,8,1024]{2,1,0:T(8,128)(2,1)S(1)}, u32[]{:S(2)}, u32[]{:S(2)}) collective-permute-start(bf16[4,8,1024]{2,1,0:T(8,128)(2,1)S(1)} %pad_maximum_fusion.3), channel_id=1, source_target_pairs={{480,0},{0,32},{32,64},{64,96},{96,128},{128,160},{160,192},{192,2... | collective-permute-start | bytes 196616 | tf_op jit(solution)/shard_map/ppermute | solution.py:335
  168.3 22.2 %collective-permute-start.8 = (bf16[4,8,1024]{2,1,0:T(8,128)(2,1)S(1)}, bf16[4,8,1024]{2,1,0:T(8,128)(2,1)S(1)}, u32[]{:S(2)}, u32[]{:S(2)}) collective-permute-start(bf16[4,8,1024]{2,1,0:T(8,128)(2,1)S(1)} %pad_maximum_fusion.3), channel_id=1, source_target_pairs={{64,0},{96,32},{128,64},{160,96},{192,128},{224,160},{256,192},{28... | collective-permute-start | bytes 196616 | tf_op jit(solution)/shard_map/ppermute | solution.py:335
  173.3 18.9 %collective-permute-start.7 = (bf16[4,8,1024]{2,1,0:T(8,128)(2,1)S(1)}, bf16[4,8,1024]{2,1,0:T(8,128)(2,1)S(1)}, u32[]{:S(2)}, u32[]{:S(2)}) collective-permute-start(bf16[4,8,1024]{2,1,0:T(8,128)(2,1)S(1)} %pad_maximum_fusion.3), channel_id=1, source_target_pairs={{32,0},{64,32},{96,64},{128,96},{160,128},{192,160},{224,192},{256... | collective-permute-start | bytes 196616 | tf_op jit(solution)/shard_map/ppermute | solution.py:335
  197.4 43.0 %all-to-all-start.4 = ((bf16[128,16,128]{2,1,0:T(8,128)(2,1)}), bf16[128,16,128]{2,1,0:T(8,128)(2,1)S(1)}, u32[]{:S(2)}, u32[]{:S(2)}) async-start(bf16[128,16,128]{2,1,0:T(8,128)(2,1)} %shard_map.61), calls=%async_computation.4 | async-start | bytes 1048576 | tf_op jit(solution)/shard_map/all_to_all | solution.py:330
  209.5 10.8 %collective-permute-start.12 = (bf16[4,4,8,1024]{3,2,1,0:T(8,128)(2,1)S(1)}, bf16[4,4,8,1024]{3,2,1,0:T(8,128)(2,1)S(1)}, u32[]{:S(2)}, u32[]{:S(2)}) collective-permute-start(bf16[4,4,8,1024]{3,2,1,0:T(8,128)(2,1)S(1)} %pad_maximum_fusion.2), channel_id=1, source_target_pairs={{24,0},{0,8},{8,16},{16,24},{25,1},{1,9},{9,17},{17,25},{26,2},{2,... | collective-permute-start | bytes 786440 | tf_op jit(solution)/shard_map/ppermute | solution.py:335
  212.8 17.4 %collective-permute-start.11 = (bf16[4,4,8,1024]{3,2,1,0:T(8,128)(2,1)S(1)}, bf16[4,4,8,1024]{3,2,1,0:T(8,128)(2,1)S(1)}, u32[]{:S(2)}, u32[]{:S(2)}) collective-permute-start(bf16[4,4,8,1024]{3,2,1,0:T(8,128)(2,1)S(1)} %pad_maximum_fusion.2), channel_id=1, source_target_pairs={{16,0},{24,8},{0,16},{8,24},{17,1},{25,9},{1,17},{9,25},{18,2},{26... | collective-permute-start | bytes 786440 | tf_op jit(solution)/shard_map/ppermute | solution.py:335
  217.2 14.6 %collective-permute-start.10 = (bf16[4,4,8,1024]{3,2,1,0:T(8,128)(2,1)S(1)}, bf16[4,4,8,1024]{3,2,1,0:T(8,128)(2,1)S(1)}, u32[]{:S(2)}, u32[]{:S(2)}) collective-permute-start(bf16[4,4,8,1024]{3,2,1,0:T(8,128)(2,1)S(1)} %pad_maximum_fusion.2), channel_id=1, source_target_pairs={{8,0},{16,8},{24,16},{0,24},{9,1},{17,9},{25,17},{1,25},{10,2},{18... | collective-permute-start | bytes 786440 | tf_op jit(solution)/shard_map/ppermute | solution.py:335
  231.9 5.4 %collective-permute-start.13 = (bf16[4,4,4,8,1024]{4,3,2,1,0:T(8,128)(2,1)S(1)}, bf16[4,4,4,8,1024]{4,3,2,1,0:T(8,128)(2,1)S(1)}, u32[]{:S(2)}, u32[]{:S(2)}) collective-permute-start(bf16[4,4,4,8,1024]{4,3,2,1,0:T(8,128)(2,1)S(1)} %get-tuple-element.41), channel_id=1, source_target_pairs={{4,0},{0,4},{5,1},{1,5},{6,2},{2,6},{7,3},{3,7},{12,8},{8,12},{13,... | collective-permute-start | bytes 3145736 | tf_op jit(solution)/shard_map/ppermute | solution.py:335

commit v5 on v4

--- a/solution.py
+++ b/solution.py
@@ -74,23 +74,27 @@
     return terms[0]
 
 
-def panel_sweep(groups, first):
+def panel_sweep(groups, starts):
     sub_ids = lax.broadcasted_iota(jnp.int32, (SUB, LANES), 0)
     lane_ids = lax.broadcasted_iota(jnp.int32, (SUB, LANES), 1)
+    tiles = range(len(starts))
+    from_start = [lane_ids - start for start in starts]
     for p in range(len(groups)):
-        tile, lane = divmod(first + p * SUB, LANES)
-        pivot_lanes = (lane_ids // SUB) == lane // SUB
-        spread = [lane_of(groups[p][tile], lane + j) for j in range(SUB)]
+        lane = p * SUB
+        places = [x - lane for x in from_start]
+        pivot_lanes = [(x >= 0) & (x < SUB) for x in places]
+        spread = [lane_of(groups[p][-1], lane + j) for j in range(SUB)]
         u = {(i, j): row_of(spread[j], i) for j in range(SUB) for i in range(j + 1)}
-        sources = []
-        for j in range(SUB):
-            line = [-row_of(x, j) for x in groups[p]]
-            line[tile] = jnp.where(
-                pivot_lanes, jnp.where(lane_ids == lane + j, 1.0, 0.0), line[tile]
-            )
-            sources.append(line)
+        sources = [
+            [
+                jnp.where(
+                    pivot_lanes[t], jnp.where(places[t] == j, 1.0, 0.0), -row_of(groups[p][t], j)
+                )
+                for t in tiles
+            ]
+            for j in range(SUB)
+        ]
         u = invert_small(u, SUB)
-        tiles = range(len(groups[p]))
         lines = [
             [
                 tree_sum([u[min(i, j), max(i, j)] * sources[j][t] for j in range(SUB)])
@@ -101,11 +105,9 @@
         for g in range(len(groups)):
             if g == p:
                 continue
-            factors = [lane_of(groups[g][tile], lane + j) for j in range(SUB)]
+            factors = [lane_of(groups[g][-1], lane + j) for j in range(SUB)]
             for t in tiles:
-                kept = groups[g][t]
-                if t == tile:
-                    kept = jnp.where(pivot_lanes, 0.0, kept)
+                kept = jnp.where(pivot_lanes[t], 0.0, groups[g][t])
                 groups[g][t] = kept - tree_sum([factors[j] * lines[j][t] for j in range(SUB)])
         for t in tiles:
             row = lines[0][t]
@@ -118,23 +120,29 @@
 def block_sweep(d_ref):
     wide = d_ref.shape[0]
     lane_ids = lax.broadcasted_iota(jnp.int32, (wide, wide), 1)
-    for first in range(0, wide, BASE):
-        old = d_ref[first : first + BASE, :]
+
+    @pl.loop(0, wide // BASE)
+    def _(q):
+        first = q * BASE
+        rows = pl.ds(pl.multiple_of(first, BASE), BASE)
+        old = d_ref[rows, :]
+        tile = pl.ds(pl.multiple_of(first // LANES * LANES, LANES), LANES)
+        start = lax.rem(first, LANES)
+        own = pltpu.roll(d_ref[rows, tile], lax.rem(LANES - start, LANES), 1)
         groups = [
-            [old[g : g + SUB, t : t + LANES] for t in range(0, wide, LANES)]
+            [old[g : g + SUB, t : t + LANES] for t in range(0, wide, LANES)] + [own[g : g + SUB]]
             for g in range(0, BASE, SUB)
         ]
-        groups = panel_sweep(groups, first)
-        new = jnp.concatenate([jnp.concatenate(g, axis=1) for g in groups], axis=0)
+        groups = panel_sweep(groups, [first - t for t in range(0, wide, LANES)] + [0])
+        new = jnp.concatenate([jnp.concatenate(g[:-1], axis=1) for g in groups], axis=0)
         update = lax.dot_general(
             stacked(old, LEFT, 0),
             stacked(new, RIGHT, 0),
             (((0,), (0,)), ((), ())),
             preferred_element_type=jnp.float32,
         )
-        kept = jnp.where(lane_ids // BASE == first // BASE, 0.0, d_ref[...])
-        d_ref[...] = kept - update
-        d_ref[first : first + BASE, :] = new
+        d_ref[...] = jnp.where(lane_ids // BASE == q, 0.0, d_ref[...]) - update
+        d_ref[rows, :] = new
 
 
 def invert_kernel(
@@ -184,45 +192,82 @@
             total = total + jnp.where(diagonal, m_ref[block(i), block(i)] + shift, 0.0)
         total = jnp.sum(jnp.sum(total, axis=0, keepdims=True), axis=1, keepdims=True)
         scale = n / total
-        for _, i, j in arrivals:
-            value = m_ref[block(i), block(j)]
-            if i == j:
-                m_ref[block(i), block(i)] = jnp.where(diagonal, value + shift, value) * scale
-            else:
-                value = value * scale
-                m_ref[block(i), block(j)] = value
-                m_ref[block(j), block(i)] = value.T
+        def part(i):
+            return pl.ds(pl.multiple_of(i * wide, wide), wide)
+
+        def settle(i, j):
+            value = m_ref[part(i), part(j)] * scale
+            m_ref[part(i), part(j)] = value
+            m_ref[part(j), part(i)] = value.T
+
+        @pl.loop(0, count)
+        def _(i):
+            value = m_ref[part(i), part(i)]
+            m_ref[part(i), part(i)] = jnp.where(diagonal, value + shift, value) * scale
+
+        @pl.loop(1, count)
+        def _(i):
+            settle(0, i)
+
+        @pl.loop(1, count)
+        def _(i):
+            settle(i, lax.rem(i, count - 1) + 1)
 
         @pl.loop(0, count)
         def _(k):
-            at = pl.ds(pl.multiple_of(k * wide, wide), wide)
+            at = part(k)
             d_ref[...] = m_ref[at, at]
             block_sweep(d_ref)
 
-            left_ref[...] = stacked(m_ref[:, at], LEFT, 1)
-            right_ref[...] = stacked(m_ref[at, :], RIGHT, 0)
-            rows = -dot(stacked(d_ref[...], LEFT, 1), right_ref[...])
-            m_ref[:, at] = jnp.zeros((n, wide), jnp.float32)
-            m_ref[at, :] = rows
+            @pl.loop(0, count)
+            def _(i):
+                left_ref[part(i), :] = stacked(m_ref[part(i), at], LEFT, 1)
+                right_ref[:, part(i)] = stacked(m_ref[at, part(i)], RIGHT, 0)
+
+            pivot_left = stacked(d_ref[...], LEFT, 1)
+
+            @pl.loop(0, count)
+            def _(j):
+                m_ref[at, part(j)] = -dot(pivot_left, right_ref[:, part(j)])
+
+            @pl.loop(0, count)
+            def _(i):
+                m_ref[part(i), at] = jnp.zeros((wide, wide), jnp.float32)
+
             m_ref[at, at] = d_ref[...]
-            right_ref[...] = stacked(m_ref[at, :], RIGHT, 0)
-            for i in range(count):
-
-                @pl.when(i != k)
-                def _():
-                    m_ref[block(i), :] = m_ref[block(i), :] - dot(left_ref[block(i), :], right_ref[...])
-
-        for j in range(count):
-            band = (m_ref[block(0), block(j)] * -scale).astype(jnp.bfloat16)
+
+            @pl.loop(0, count)
+            def _(j):
+                right_ref[:, part(j)] = stacked(m_ref[at, part(j)], RIGHT, 0)
+
+            @pl.loop(1, count)
+            def _(step):
+                i = part(lax.rem(k + step, count))
+
+                @pl.loop(0, count // 2)
+                def _(j):
+                    half = pl.ds(pl.multiple_of(j * 2 * wide, 2 * wide), 2 * wide)
+                    m_ref[i, half] = m_ref[i, half] - dot(left_ref[i, :], right_ref[:, half])
+
+        @pl.loop(0, count)
+        def _(j):
+            band = (m_ref[block(0), part(j)] * -scale).astype(jnp.bfloat16)
+            first = lax.rem(mp_index + j, count) * (wide // LANES)
             for r in range(wide // ROWS):
                 for c in range(wide // LANES):
-                    at = lax.rem(mp_index + j, count) * (wide // LANES) + r * (n // LANES) + c
-                    band_ref[at] = band[r * ROWS : (r + 1) * ROWS, c * LANES : (c + 1) * LANES]
+                    band_ref[first + r * (n // LANES) + c] = band[
+                        r * ROWS : (r + 1) * ROWS, c * LANES : (c + 1) * LANES
+                    ]
+
         sent = pltpu.make_async_copy(band_ref, band_hbm, out_sem)
         sent.start()
-        for j in range(count):
-            for i in range(count):
-                full_ref[place(i), place(j)] = (m_ref[block(i), block(j)] * -scale).astype(jnp.bfloat16)
+
+        @pl.loop(0, count)
+        def _(i):
+            @pl.loop(0, count)
+            def _(j):
+                full_ref[place(i), place(j)] = (m_ref[part(i), part(j)] * -scale).astype(jnp.bfloat16)
+
         sent.wait()
 
     @pl.when(scalar_ref[0] <= 0)
@@ -257,7 +302,7 @@
             pltpu.SemaphoreType.DMA((10,)),
             pltpu.SemaphoreType.DMA,
         ],
-        compiler_params=pltpu.CompilerParams(vmem_limit_bytes=24 * 1024 * 1024),
+        compiler_params=pltpu.CompilerParams(vmem_limit_bytes=56 * 1024 * 1024),
         cost_estimate=pl.CostEstimate(
             flops=36 * n * n * n, bytes_accessed=6 * n * n, transcendentals=0
         ),
@@ -393,10 +438,10 @@
         return jnp.stack([value] + [from_ahead(value, axis, step) for step in steps])
 
     held = jnp.dot(tile, inverse, preferred_element_type=jnp.float32).astype(jnp.bfloat16)
-    held = gather(held, "z", (4, 8, 12))
+    held = exchange(jnp.broadcast_to(held[None], (z_count,) + held.shape), "z")
     inverse_band, held = lax.optimization_barrier((inverse_band, held))
     spread = exchange(inverse_band, DP)
-    held = gather(held, "z", (1, 2, 15))
+    held = gather(gather(held, "x", (1, 2, 3)), "c", (1,))
     slot_range = jnp.arange(dp_count, dtype=jnp.int32)
     empty = jnp.min(jnp.where(old_flat >= 0, dp_count - 1, slot_range))
     source = jnp.where(new_flat >= 0, positions(old_flat, new_flat), empty)
@@ -404,16 +449,13 @@
     arrived = exchange(outgoing, DP)
     arrived = arrived.reshape(band // ROWS, width // LANES, ROWS, LANES)
     inverses = arrived.transpose(0, 2, 1, 3).reshape(1, 1, band, width)
-    held = gather(gather(held, "x", (1, 2, 3)), "c", (1,))
     held = held.reshape(dp_count, row_count, width)
     tile_range = jnp.arange(tile_count, dtype=jnp.int32)
     place = positions(old_flat, tile_range // a_span * layer_blocks + tile_range % a_span)
-    far_z = (place // (x_count * c_count) - z + z_count) % z_count
     far_x = (place // c_count - x + x_count) % x_count
     far_c = (place - c + c_count) % c_count
-    low = far_z % 4
-    high = (far_z + jnp.where(low == 3, 1, 0)) // 4 % 4
-    precond = take(held, ((far_c * x_count + far_x) * 4 + low) * 4 + high)
+    from_z = place // (x_count * c_count)
+    precond = take(held, (far_c * x_count + far_x) * z_count + from_z)
     return (inverses, precond)
 
 

time: 244 us -> 255 us (1.045)
  blocking collectives: 0 us -> 43.6 us
  starting transfers between devices: 121 us -> 84.1 us
  waiting for transfers between devices: 90.2 us -> 98.2 us
  local copies, waits for them, and re-layouts: 13.2 us -> 7.36 us
    all_to_all x0 -> x1, blocking collectives: none -> 43.6 us  [exchange(): return lax.all_to_all(pieces, axes, split_axis=0, concat_axis=0, tiled=True)]
    ppermute x14 -> x8, starting transfers between devices: 63.2 us -> 24.8 us  [from_ahead(): lax.ppermute(value, axis, [((i + step) % count, i) for i in range(count)])]
    all_to_all x5, waiting for transfers between devices: 54.4 us -> 85.9 us  [exchange(): return lax.all_to_all(pieces, axes, split_axis=0, concat_axis=0, tiled=True)]
    ppermute x14 -> x8, waiting for transfers between devices: 35.8 us -> 12.3 us  [from_ahead(): lax.ppermute(value, axis, [((i + step) % count, i) for i in range(count)])]
    unnamed x18 -> x10, local copies, waits for them, and re-layouts: 6.21 us -> 1.32 us
  transfers between devices with their start and end apart: 19 -> 13, of which waited for: 13 -> 9; matrix products, arithmetic and copies ran while one was open for 5% -> 5% of each run, Pallas kernels for 1% -> 1%
where the time goes in v5:
time: 255 us; the launch traced here: 253 us
  waiting for transfers between devices  98.2 us (39%)
  starting transfers between devices  84.1 us (33%)
  blocking collectives  43.6 us (17%)
  other arithmetic  8.53 us (3%)
  local copies, waits for them, and re-layouts  7.36 us (3%)
  Pallas kernels  5.33 us (2%)
  between operations  3.46 us (1%)
    all_to_all x5, waiting for transfers between devices, exchange(): return lax.all_to_all(pieces, axes, split_axis=0, concat_axis=0, tiled=True)  85.9 us
    all_to_all x5, starting transfers between devices, exchange(): return lax.all_to_all(pieces, axes, split_axis=0, concat_axis=0, tiled=True)  59.3 us
    all_to_all x1, blocking collectives, exchange(): return lax.all_to_all(pieces, axes, split_axis=0, concat_axis=0, tiled=True)  43.6 us
    ppermute x8, starting transfers between devices, from_ahead(): lax.ppermute(value, axis, [((i + step) % count, i) for i in range(count)])  24.8 us
    ppermute x8, waiting for transfers between devices, from_ahead(): lax.ppermute(value, axis, [((i + step) % count, i) for i in range(count)])  12.3 us
  transfers between devices with their start and end apart: 13, of which 9 were waited for; matrix products, arithmetic and copies ran while one was open for 5% of the time, Pallas kernels for 1%

profile of v5, /device:TPU:1, one launch (start us, length us, event | category | flops | bytes accessed | tf_op | source)
XLA Modules:
  0.0 252.6 jit_solution(14901992124769760778)
XLA Ops:
  0.6 0.0 copy-start
  0.6 0.0 copy-start.1
  0.7 1.3 copy-done.1
  2.0 0.8 shard_map.59
  2.7 10.4 %all-to-all-start = ((f32[32,1,128]{2,1,0:T(1,128)}), f32[32,1,128]{2,1,0:T(1,128)S(1)}, u32[]{:S(2)}, u32[]{:S(2)}) async-start(f32[32,1,128]{2,1,0:T(1,128)} %get-tuple-element.19), calls=%async_computation | async-start | bytes 32768 | tf_op jit(solution)/shard_map/all_to_all | solution.py:375
  13.1 0.7 compare_reduce_fusion
  13.8 0.7 remainder_reduce_fusion
  14.5 0.7 bitcast_select_fusion
  15.2 0.1 iota_compare_fusion
  15.3 0.1 ne.197
  15.4 0.1 rem.133
  15.6 0.1 div.61
  15.7 0.2 fusion.3
  15.9 4.1 %all-to-all-done = f32[32,1,128]{2,1,0:T(1,128)S(1)} async-done(((f32[32,1,128]{2,1,0:T(1,128)}), f32[32,1,128]{2,1,0:T(1,128)S(1)}, u32[]{:S(2)}, u32[]{:S(2)}) %all-to-all-start) | async-done | bytes 16416 | tf_op jit(solution)/shard_map/all_to_all | solution.py:375
  20.0 0.1 fusion.5
  20.1 0.0 copy-done
  20.1 1.6 gather_fusion.1
  21.7 2.5 %collective-permute-start = (bf16[64,8,1024]{2,1,0:T(8,128)(2,1)}, bf16[64,8,1024]{2,1,0:T(8,128)(2,1)}, u32[]{:S(2)}, u32[]{:S(2)}) collective-permute-start(bf16[64,8,1024]{2,1,0:T(8,128)(2,1)} %gather_fusion.1), channel_id=1, source_target_pairs={{4,0},{0,4},{5,1},{1,5},{6,2},{2,6},{7,3},{3,7},{12,8},{8,12},{13,... | collective-permute-start | bytes 3145736 | tf_op jit(solution)/shard_map/ppermute | solution.py:380
  24.3 2.8 %collective-permute-start.2 = (f32[256,512]{1,0:T(8,128)S(1)}, f32[256,512]{1,0:T(8,128)}, u32[]{:S(2)}, u32[]{:S(2)}) collective-permute-start(f32[256,512]{1,0:T(8,128)S(1)} %get-tuple-element.25), channel_id=1, source_target_pairs={{2,0},{3,1},{0,2},{1,3},{6,4},{7,5},{4,6},{5,7},{10,8},{11,9},{8,1... | collective-permute-start | bytes 1572872 | tf_op jit(solution)/shard_map/ppermute | solution.py:380
  27.2 3.7 %collective-permute-start.1 = (f32[256,512]{1,0:T(8,128)S(1)}, f32[256,512]{1,0:T(8,128)}, u32[]{:S(2)}, u32[]{:S(2)}) collective-permute-start(f32[256,512]{1,0:T(8,128)S(1)} %get-tuple-element.25), channel_id=1, source_target_pairs={{1,0},{2,1},{3,2},{0,3},{5,4},{6,5},{7,6},{4,7},{9,8},{10,9},{11,1... | collective-permute-start | bytes 1572872 | tf_op jit(solution)/shard_map/ppermute | solution.py:380
  30.8 0.6 broadcast_in_dim.78
  31.4 13.0 %all-to-all-start.1 = ((f32[16,1,128]{2,1,0:T(1,128)}), f32[16,1,128]{2,1,0:T(1,128)S(1)}, u32[]{:S(2)}, u32[]{:S(2)}) async-start(f32[16,1,128]{2,1,0:T(1,128)} %broadcast_in_dim.78), calls=%async_computation.1 | async-start | bytes 16384 | tf_op jit(solution)/shard_map/all_to_all | solution.py:375
  44.5 1.9 collective-permute-start.3
  46.4 0.6 gather_fusion
  47.0 0.0 copy-start.4
  47.0 0.0 collective-permute-done
  47.0 2.6 %add_convert_fusion = bf16[64,8,1024]{2,1,0:T(8,128)(2,1)} fusion(bf16[64,8,1024]{2,1,0:T(8,128)(2,1)} %collective-permute-done, bf16[64,8,1024]{2,1,0:T(8,128)(2,1)S(1)} %gather_fusion), kind=kLoop, calls=%fused_computation.4 | loop fusion | flops 2097152 | bytes 3145728 | tf_op jit(solution)/shard_map/convert_element_type | solution.py:427
  49.7 6.0 %all-to-all-done.1 = f32[16,1,128]{2,1,0:T(1,128)S(1)} async-done(((f32[16,1,128]{2,1,0:T(1,128)}), f32[16,1,128]{2,1,0:T(1,128)S(1)}, u32[]{:S(2)}, u32[]{:S(2)}) %all-to-all-start.1) | async-done | bytes 8224 | tf_op jit(solution)/shard_map/all_to_all | solution.py:375
  55.7 7.0 %all-to-all-start.2 = ((bf16[64,8,1024]{2,1,0:T(8,128)(2,1)}), bf16[64,8,1024]{2,1,0:T(8,128)(2,1)S(1)}, u32[]{:S(2)}, u32[]{:S(2)}) async-start(bf16[64,8,1024]{2,1,0:T(8,128)(2,1)} %add_convert_fusion), calls=%async_computation.2 | async-start | bytes 2097152 | tf_op jit(solution)/shard_map/all_to_all | solution.py:375
  62.7 0.0 copy-done.4
  62.7 0.6 fusion.18
  65.8 0.7 pad_add_fusion.scalar_ref
  66.5 0.0 collective-permute-done.3.three_hbm
  66.5 0.0 collective-permute-done.2.two_hbm
  66.5 0.0 collective-permute-done.1.one_hbm
  66.5 0.0 copy-done.2
  66.5 3.0 %shard_map.60 = (bf16[128,16,128]{2,1,0:T(8,128)(2,1)}, bf16[1024,1024]{1,0:T(8,128)(2,1)}) custom-call(s32[4]{0:T(128)} %pad_add_fusion.scalar_ref, f32[16,128]{1,0:T(8,128)} %bitcast.83, f32[256,1024]{1,0:T(8,128)} %bitcast.73, f32[256,512]{1,0:T(8,128)} %collective-permute-done.1.one_hbm, f32[256,512]{1,0:T(8,128)} %collective-permute-done.2.two_hbm, ...), custom_call_target="tpu_custom_call" | custom-call | flops 38654705664 | bytes 6291456 | tf_op jit(solution)/shard_map/pallas_call | solution.py:288
  69.6 44.0 %all-to-all-done.2 = bf16[64,8,1024]{2,1,0:T(8,128)(2,1)S(1)} async-done(((bf16[64,8,1024]{2,1,0:T(8,128)(2,1)}), bf16[64,8,1024]{2,1,0:T(8,128)(2,1)S(1)}, u32[]{:S(2)}, u32[]{:S(2)}) %all-to-all-start.2) | async-done | bytes 1048608 | tf_op jit(solution)/shard_map/all_to_all | solution.py:375
  113.5 0.2 reduce_sum.43
  113.7 2.0 convolution_convert_fusion
  115.7 43.6 %all_to_all.30 = bf16[16,8,1024]{2,1,0:T(8,128)(2,1)S(1)} all-to-all(bf16[16,8,1024]{2,1,0:T(8,128)(2,1)S(1)} %broadcast_in_dim.79), channel_id=1, replica_groups=mesh['z'=16,'x'=4,'c'=2,'mp'=4] {'z'}, dimensions={0} | all-to-all | bytes 524288 | tf_op jit(solution)/shard_map/all_to_all | solution.py:375
  159.3 15.6 %all-to-all-start.4 = ((bf16[128,16,128]{2,1,0:T(8,128)(2,1)}), bf16[128,16,128]{2,1,0:T(8,128)(2,1)S(1)}, u32[]{:S(2)}, u32[]{:S(2)}) async-start(bf16[128,16,128]{2,1,0:T(8,128)(2,1)} %get-tuple-element.32), calls=%async_computation.4 | async-start | bytes 1048576 | tf_op jit(solution)/shard_map/all_to_all | solution.py:375
  174.9 3.3 %collective-permute-start.6 = (bf16[16,8,1024]{2,1,0:T(8,128)(2,1)S(1)}, bf16[16,8,1024]{2,1,0:T(8,128)(2,1)S(1)}, u32[]{:S(2)}, u32[]{:S(2)}) collective-permute-start(bf16[16,8,1024]{2,1,0:T(8,128)(2,1)S(1)} %all_to_all.30), channel_id=1, source_target_pairs={{24,0},{0,8},{8,16},{16,24},{25,1},{1,9},{9,17},{17,25},{26,2},{2,... | collective-permute-start | bytes 786440 | tf_op jit(solution)/shard_map/ppermute | solution.py:380
  178.2 4.3 %collective-permute-start.5 = (bf16[16,8,1024]{2,1,0:T(8,128)(2,1)S(1)}, bf16[16,8,1024]{2,1,0:T(8,128)(2,1)S(1)}, u32[]{:S(2)}, u32[]{:S(2)}) collective-permute-start(bf16[16,8,1024]{2,1,0:T(8,128)(2,1)S(1)} %all_to_all.30), channel_id=1, source_target_pairs={{16,0},{24,8},{0,16},{8,24},{17,1},{25,9},{1,17},{9,25},{18,2},{26... | collective-permute-start | bytes 786440 | tf_op jit(solution)/shard_map/ppermute | solution.py:380
  182.5 3.1 %collective-permute-start.4 = (bf16[16,8,1024]{2,1,0:T(8,128)(2,1)S(1)}, bf16[16,8,1024]{2,1,0:T(8,128)(2,1)S(1)}, u32[]{:S(2)}, u32[]{:S(2)}) collective-permute-start(bf16[16,8,1024]{2,1,0:T(8,128)(2,1)S(1)} %all_to_all.30), channel_id=1, source_target_pairs={{8,0},{16,8},{24,16},{0,24},{9,1},{17,9},{25,17},{1,25},{10,2},{18... | collective-permute-start | bytes 786440 | tf_op jit(solution)/shard_map/ppermute | solution.py:380
  185.6 0.1 collective-permute-done.6
  185.7 9.9 %collective-permute-done.5 = bf16[16,8,1024]{2,1,0:T(8,128)(2,1)S(1)} collective-permute-done((bf16[16,8,1024]{2,1,0:T(8,128)(2,1)S(1)}, bf16[16,8,1024]{2,1,0:T(8,128)(2,1)S(1)}, u32[]{:S(2)}, u32[]{:S(2)}) %collective-permute-start.5) | collective-permute-done | bytes 262176 | tf_op jit(solution)/shard_map/ppermute | solution.py:380
  195.6 1.5 collective-permute-done.4
  197.1 0.2 fusion.17
  197.3 3.1 %collective-permute-start.7 = (bf16[4,16,8,1024]{3,2,1,0:T(8,128)(2,1)S(1)}, bf16[4,16,8,1024]{3,2,1,0:T(8,128)(2,1)S(1)}, u32[]{:S(2)}, u32[]{:S(2)}) collective-permute-start(bf16[4,16,8,1024]{3,2,1,0:T(8,128)(2,1)S(1)} %get-tuple-element.41), channel_id=1, source_target_pairs={{4,0},{0,4},{5,1},{1,5},{6,2},{2,6},{7,3},{3,7},{12,8},{8,12},{13,... | collective-permute-start | bytes 3145736 | tf_op jit(solution)/shard_map/ppermute | solution.py:380
  200.5 0.6 fusion.10
  201.1 0.0 copy-done.3
  201.1 0.2 select_reduce_fusion
  201.3 0.7 compare_select_fusion.9.index_ref
  201.9 0.8 collective-permute-done.7
  202.7 0.2 pad_maximum_fusion
  202.9 2.8 %all-to-all-done.4.src_ref = bf16[128,16,128]{2,1,0:T(8,128)(2,1)S(1)} async-done(((bf16[128,16,128]{2,1,0:T(8,128)(2,1)}), bf16[128,16,128]{2,1,0:T(8,128)(2,1)S(1)}, u32[]{:S(2)}, u32[]{:S(2)}) %all-to-all-start.4) | async-done | bytes 524320 | tf_op jit(solution)/shard_map/all_to_all | solution.py:375
  205.7 1.6 shard_map.61
  207.3 13.3 %all-to-all-start.5 = ((bf16[128,16,128]{2,1,0:T(8,128)(2,1)}), bf16[128,16,128]{2,1,0:T(8,128)(2,1)S(1)}, u32[]{:S(2)}, u32[]{:S(2)}) async-start(bf16[128,16,128]{2,1,0:T(8,128)(2,1)} %shard_map.61), calls=%async_computation.5 | async-start | bytes 1048576 | tf_op jit(solution)/shard_map/all_to_all | solution.py:375
  220.6 0.2 select_reduce_fusion.1
  220.9 1.6 gather_fusion.2
  222.4 29.0 %all-to-all-done.5 = bf16[128,16,128]{2,1,0:T(8,128)(2,1)S(1)} async-done(((bf16[128,16,128]{2,1,0:T(8,128)(2,1)}), bf16[128,16,128]{2,1,0:T(8,128)(2,1)S(1)}, u32[]{:S(2)}, u32[]{:S(2)}) %all-to-all-start.5) | async-done | bytes 524320 | tf_op jit(solution)/shard_map/all_to_all | solution.py:375
  251.5 0.1 copy.12
  251.6 1.0 reshape.319
  (10 shorter events, 0.1 us)
Async XLA Ops:
  0.6 19.5 %copy-start = (bf16[1,56,8,1024]{3,2,1,0:T(8,128)(2,1)S(1)}, bf16[1,56,8,1024]{3,2,1,0:T(8,128)(2,1)}, u32[]{:S(2)}) copy-start(bf16[1,56,8,1024]{3,2,1,0:T(8,128)(2,1)} %param.5) | copy-start | bytes 2752516
  0.6 1.3 copy-start.1
  2.7 17.3 %all-to-all-start = ((f32[32,1,128]{2,1,0:T(1,128)}), f32[32,1,128]{2,1,0:T(1,128)S(1)}, u32[]{:S(2)}, u32[]{:S(2)}) async-start(f32[32,1,128]{2,1,0:T(1,128)} %get-tuple-element.19), calls=%async_computation | async-start | bytes 32768 | tf_op jit(solution)/shard_map/all_to_all | solution.py:375
  21.7 25.3 %collective-permute-start = (bf16[64,8,1024]{2,1,0:T(8,128)(2,1)}, bf16[64,8,1024]{2,1,0:T(8,128)(2,1)}, u32[]{:S(2)}, u32[]{:S(2)}) collective-permute-start(bf16[64,8,1024]{2,1,0:T(8,128)(2,1)} %gather_fusion.1), channel_id=1, source_target_pairs={{4,0},{0,4},{5,1},{1,5},{6,2},{2,6},{7,3},{3,7},{12,8},{8,12},{13,... | collective-permute-start | bytes 3145736 | tf_op jit(solution)/shard_map/ppermute | solution.py:380
  24.3 42.2 %collective-permute-start.2 = (f32[256,512]{1,0:T(8,128)S(1)}, f32[256,512]{1,0:T(8,128)}, u32[]{:S(2)}, u32[]{:S(2)}) collective-permute-start(f32[256,512]{1,0:T(8,128)S(1)} %get-tuple-element.25), channel_id=1, source_target_pairs={{2,0},{3,1},{0,2},{1,3},{6,4},{7,5},{4,6},{5,7},{10,8},{11,9},{8,1... | collective-permute-start | bytes 1572872 | tf_op jit(solution)/shard_map/ppermute | solution.py:380
  27.2 39.3 %collective-permute-start.1 = (f32[256,512]{1,0:T(8,128)S(1)}, f32[256,512]{1,0:T(8,128)}, u32[]{:S(2)}, u32[]{:S(2)}) collective-permute-start(f32[256,512]{1,0:T(8,128)S(1)} %get-tuple-element.25), channel_id=1, source_target_pairs={{1,0},{2,1},{3,2},{0,3},{5,4},{6,5},{7,6},{4,7},{9,8},{10,9},{11,1... | collective-permute-start | bytes 1572872 | tf_op jit(solution)/shard_map/ppermute | solution.py:380
  31.4 24.3 %all-to-all-start.1 = ((f32[16,1,128]{2,1,0:T(1,128)}), f32[16,1,128]{2,1,0:T(1,128)S(1)}, u32[]{:S(2)}, u32[]{:S(2)}) async-start(f32[16,1,128]{2,1,0:T(1,128)} %broadcast_in_dim.78), calls=%async_computation.1 | async-start | bytes 16384 | tf_op jit(solution)/shard_map/all_to_all | solution.py:375
  44.5 22.0 %collective-permute-start.3 = (f32[256,512]{1,0:T(8,128)S(1)}, f32[256,512]{1,0:T(8,128)}, u32[]{:S(2)}, u32[]{:S(2)}) collective-permute-start(f32[256,512]{1,0:T(8,128)S(1)} %get-tuple-element.26), channel_id=1, source_target_pairs={{3,0},{0,1},{1,2},{2,3},{7,4},{4,5},{5,6},{6,7},{11,8},{8,9},{9,10... | collective-permute-start | bytes 1572872 | tf_op jit(solution)/shard_map/ppermute | solution.py:380
  47.0 15.7 %copy-start.4 = (s32[128,1]{0,1:T(1,128)S(1)}, s32[128,1]{0,1:T(1,128)}, u32[]{:S(2)}) copy-start(s32[128,1]{0,1:T(1,128)} %param.6) | copy-start | bytes 1540
  55.7 10.8 %copy-start.2 = (f32[16,1,128]{2,1,0:T(1,128)}, f32[16,1,128]{2,1,0:T(1,128)S(1)}, u32[]{:S(2)}) copy-start(f32[16,1,128]{2,1,0:T(1,128)S(1)} %all-to-all-done.1) | copy-start | bytes 24580
  55.7 57.8 %all-to-all-start.2 = ((bf16[64,8,1024]{2,1,0:T(8,128)(2,1)}), bf16[64,8,1024]{2,1,0:T(8,128)(2,1)S(1)}, u32[]{:S(2)}, u32[]{:S(2)}) async-start(bf16[64,8,1024]{2,1,0:T(8,128)(2,1)} %add_convert_fusion), calls=%async_computation.2 | async-start | bytes 2097152 | tf_op jit(solution)/shard_map/all_to_all | solution.py:375
  159.3 41.8 %copy-start.3 = (s32[128,1]{0,1:T(1,128)S(1)}, s32[128,1]{0,1:T(1,128)}, u32[]{:S(2)}) copy-start(s32[128,1]{0,1:T(1,128)} %param.7) | copy-start | bytes 1540
  159.3 46.5 %all-to-all-start.4 = ((bf16[128,16,128]{2,1,0:T(8,128)(2,1)}), bf16[128,16,128]{2,1,0:T(8,128)(2,1)S(1)}, u32[]{:S(2)}, u32[]{:S(2)}) async-start(bf16[128,16,128]{2,1,0:T(8,128)(2,1)} %get-tuple-element.32), calls=%async_computation.4 | async-start | bytes 1048576 | tf_op jit(solution)/shard_map/all_to_all | solution.py:375
  174.9 10.8 %collective-permute-start.6 = (bf16[16,8,1024]{2,1,0:T(8,128)(2,1)S(1)}, bf16[16,8,1024]{2,1,0:T(8,128)(2,1)S(1)}, u32[]{:S(2)}, u32[]{:S(2)}) collective-permute-start(bf16[16,8,1024]{2,1,0:T(8,128)(2,1)S(1)} %all_to_all.30), channel_id=1, source_target_pairs={{24,0},{0,8},{8,16},{16,24},{25,1},{1,9},{9,17},{17,25},{26,2},{2,... | collective-permute-start | bytes 786440 | tf_op jit(solution)/shard_map/ppermute | solution.py:380
  178.2 17.4 %collective-permute-start.5 = (bf16[16,8,1024]{2,1,0:T(8,128)(2,1)S(1)}, bf16[16,8,1024]{2,1,0:T(8,128)(2,1)S(1)}, u32[]{:S(2)}, u32[]{:S(2)}) collective-permute-start(bf16[16,8,1024]{2,1,0:T(8,128)(2,1)S(1)} %all_to_all.30), channel_id=1, source_target_pairs={{16,0},{24,8},{0,16},{8,24},{17,1},{25,9},{1,17},{9,25},{18,2},{26... | collective-permute-start | bytes 786440 | tf_op jit(solution)/shard_map/ppermute | solution.py:380
  182.5 14.6 %collective-permute-start.4 = (bf16[16,8,1024]{2,1,0:T(8,128)(2,1)S(1)}, bf16[16,8,1024]{2,1,0:T(8,128)(2,1)S(1)}, u32[]{:S(2)}, u32[]{:S(2)}) collective-permute-start(bf16[16,8,1024]{2,1,0:T(8,128)(2,1)S(1)} %all_to_all.30), channel_id=1, source_target_pairs={{8,0},{16,8},{24,16},{0,24},{9,1},{17,9},{25,17},{1,25},{10,2},{18... | collective-permute-start | bytes 786440 | tf_op jit(solution)/shard_map/ppermute | solution.py:380
  197.3 5.4 %collective-permute-start.7 = (bf16[4,16,8,1024]{3,2,1,0:T(8,128)(2,1)S(1)}, bf16[4,16,8,1024]{3,2,1,0:T(8,128)(2,1)S(1)}, u32[]{:S(2)}, u32[]{:S(2)}) collective-permute-start(bf16[4,16,8,1024]{3,2,1,0:T(8,128)(2,1)S(1)} %get-tuple-element.41), channel_id=1, source_target_pairs={{4,0},{0,4},{5,1},{1,5},{6,2},{2,6},{7,3},{3,7},{12,8},{8,12},{13,... | collective-permute-start | bytes 3145736 | tf_op jit(solution)/shard_map/ppermute | solution.py:380
  207.3 44.2 %all-to-all-start.5 = ((bf16[128,16,128]{2,1,0:T(8,128)(2,1)}), bf16[128,16,128]{2,1,0:T(8,128)(2,1)S(1)}, u32[]{:S(2)}, u32[]{:S(2)}) async-start(bf16[128,16,128]{2,1,0:T(8,128)(2,1)} %shard_map.61), calls=%async_computation.5 | async-start | bytes 1048576 | tf_op jit(solution)/shard_map/all_to_all | solution.py:375

commit v6 on v4

--- a/solution.py
+++ b/solution.py
@@ -45,27 +45,31 @@
     return jnp.dot(left, right, preferred_element_type=jnp.float32)
 
 
-def invert_small(u, size):
-    def at(i, j):
-        return u[min(i, j), max(i, j)]
-
-    for a in range(0, size, 2):
-        b = a + 1
-        aa, ab, bb = u[a, a], u[a, b], u[b, b]
-        scale = reciprocal(aa * bb - ab * ab)
-        others = [i for i in range(size) if i not in (a, b)]
-        row_a = {i: bb * at(a, i) - ab * at(b, i) for i in others}
-        row_b = {i: aa * at(b, i) - ab * at(a, i) for i in others}
-        new = {(a, a): -bb * scale, (a, b): ab * scale, (b, b): -aa * scale}
-        for i in others:
-            new[min(a, i), max(a, i)] = row_a[i] * scale
-            new[min(b, i), max(b, i)] = row_b[i] * scale
-            for j in others:
-                if i <= j:
-                    cross = at(a, i) * row_a[j] + at(b, i) * row_b[j]
-                    new[i, j] = u[i, j] - cross * scale
-        u = new
-    return u
+def solve_small(u, lines):
+    size = len(lines)
+    lower, inverse = {}, []
+    solved = []
+    scale = reciprocal(u[0, 0])
+    for j in range(size):
+        inverse.append(scale)
+        if j + 1 < size:
+            pivot = u[j + 1, j + 1] - (u[j, j + 1] * u[j, j + 1]) * scale
+        for i in range(j + 1, size):
+            lower[i, j] = u[j, i] * scale
+        if j + 1 < size:
+            scale = reciprocal(pivot)
+        for i in range(j + 1, size):
+            for m in range(i, size):
+                if m > j + 1:
+                    u[i, m] = u[i, m] - lower[i, j] * u[j, m]
+        solved.append(lines[j])
+        for i in range(j + 1, size):
+            lines[i] = [x - lower[i, j] * y for x, y in zip(lines[i], lines[j])]
+    for j in reversed(range(size)):
+        solved[j] = [x * inverse[j] for x in solved[j]]
+        for i in range(j + 1, size):
+            solved[j] = [x - lower[i, j] * y for x, y in zip(solved[j], solved[i])]
+    return solved
 
 
 def tree_sum(terms):
@@ -84,20 +88,13 @@
         u = {(i, j): row_of(spread[j], i) for j in range(SUB) for i in range(j + 1)}
         sources = []
         for j in range(SUB):
-            line = [-row_of(x, j) for x in groups[p]]
+            line = [row_of(x, j) for x in groups[p]]
             line[tile] = jnp.where(
-                pivot_lanes, jnp.where(lane_ids == lane + j, 1.0, 0.0), line[tile]
+                pivot_lanes, jnp.where(lane_ids == lane + j, -1.0, 0.0), line[tile]
             )
             sources.append(line)
-        u = invert_small(u, SUB)
         tiles = range(len(groups[p]))
-        lines = [
-            [
-                tree_sum([u[min(i, j), max(i, j)] * sources[j][t] for j in range(SUB)])
-                for t in tiles
-            ]
-            for i in range(SUB)
-        ]
+        lines = solve_small(u, sources)
         for g in range(len(groups)):
             if g == p:
                 continue
@@ -179,18 +176,11 @@
         for copy in copies:
             copy.wait()
 
-        total = jnp.zeros((wide, wide), jnp.float32)
-        for i in range(count):
-            total = total + jnp.where(diagonal, m_ref[block(i), block(i)] + shift, 0.0)
-        total = jnp.sum(jnp.sum(total, axis=0, keepdims=True), axis=1, keepdims=True)
-        scale = n / total
         for _, i, j in arrivals:
             value = m_ref[block(i), block(j)]
             if i == j:
-                m_ref[block(i), block(i)] = jnp.where(diagonal, value + shift, value) * scale
+                m_ref[block(i), block(i)] = jnp.where(diagonal, value + shift, value)
             else:
-                value = value * scale
-                m_ref[block(i), block(j)] = value
                 m_ref[block(j), block(i)] = value.T
 
         @pl.loop(0, count)
@@ -213,7 +203,7 @@
                     m_ref[block(i), :] = m_ref[block(i), :] - dot(left_ref[block(i), :], right_ref[...])
 
         for j in range(count):
-            band = (m_ref[block(0), block(j)] * -scale).astype(jnp.bfloat16)
+            band = (-m_ref[block(0), block(j)]).astype(jnp.bfloat16)
             for r in range(wide // ROWS):
                 for c in range(wide // LANES):
                     at = lax.rem(mp_index + j, count) * (wide // LANES) + r * (n // LANES) + c
@@ -222,7 +212,7 @@
         sent.start()
         for j in range(count):
             for i in range(count):
-                full_ref[place(i), place(j)] = (m_ref[block(i), block(j)] * -scale).astype(jnp.bfloat16)
+                full_ref[place(i), place(j)] = (-m_ref[block(i), block(j)]).astype(jnp.bfloat16)
         sent.wait()
 
     @pl.when(scalar_ref[0] <= 0)
@@ -257,7 +247,7 @@
             pltpu.SemaphoreType.DMA((10,)),
             pltpu.SemaphoreType.DMA,
         ],
-        compiler_params=pltpu.CompilerParams(vmem_limit_bytes=24 * 1024 * 1024),
+        compiler_params=pltpu.CompilerParams(vmem_limit_bytes=56 * 1024 * 1024),
         cost_estimate=pl.CostEstimate(
             flops=36 * n * n * n, bytes_accessed=6 * n * n, transcendentals=0
         ),
@@ -362,9 +352,10 @@
     plane_bin = jnp.where(plane >= 0, plane_bin, -1)
     lane_ids = lax.broadcasted_iota(jnp.int32, (1, 1, LANES), 2)
     binned = jnp.sum(jnp.where(lane_ids == plane_bin[:, None, None], trace, 0.0), axis=(0, 1))
-    binned, near, far, tiles = lax.optimization_barrier((binned, near, far, gradients[0]))
+    binned, tiles = lax.optimization_barrier((binned, gradients[0]))
     binned = jnp.broadcast_to(binned[None, None], (z_count, 1, LANES))
     traces = exchange(binned, "z").reshape(z_count, LANES)
+    traces, near, far = lax.optimization_barrier((traces, near, far))
 
     one = from_ahead(near, "mp", 1)
     two = from_ahead(near, "mp", 2)
@@ -393,10 +384,8 @@
         return jnp.stack([value] + [from_ahead(value, axis, step) for step in steps])
 
     held = jnp.dot(tile, inverse, preferred_element_type=jnp.float32).astype(jnp.bfloat16)
-    held = gather(held, "z", (4, 8, 12))
-    inverse_band, held = lax.optimization_barrier((inverse_band, held))
+    held = lax.all_gather(held, "z", axis=0, tiled=False)
     spread = exchange(inverse_band, DP)
-    held = gather(held, "z", (1, 2, 15))
     slot_range = jnp.arange(dp_count, dtype=jnp.int32)
     empty = jnp.min(jnp.where(old_flat >= 0, dp_count - 1, slot_range))
     source = jnp.where(new_flat >= 0, positions(old_flat, new_flat), empty)
@@ -408,12 +397,10 @@
     held = held.reshape(dp_count, row_count, width)
     tile_range = jnp.arange(tile_count, dtype=jnp.int32)
     place = positions(old_flat, tile_range // a_span * layer_blocks + tile_range % a_span)
-    far_z = (place // (x_count * c_count) - z + z_count) % z_count
     far_x = (place // c_count - x + x_count) % x_count
     far_c = (place - c + c_count) % c_count
-    low = far_z % 4
-    high = (far_z + jnp.where(low == 3, 1, 0)) // 4 % 4
-    precond = take(held, ((far_c * x_count + far_x) * 4 + low) * 4 + high)
+    from_z = place // (x_count * c_count)
+    precond = take(held, (far_c * x_count + far_x) * z_count + from_z)
     return (inverses, precond)
 
 

time: 244 us -> 244 us (level)
  blocking collectives: 0 us -> 40.7 us
  starting transfers between devices: 121 us -> 100 us
  waiting for transfers between devices: 90.2 us -> 73.9 us
  local copies, waits for them, and re-layouts: 13.2 us -> 7.34 us
    all_gather x0 -> x1, blocking collectives: none -> 40.7 us  [local(): held = lax.all_gather(held, 'z', axis=0, tiled=False)]
    ppermute x14 -> x8, starting transfers between devices: 63.2 us -> 24.9 us  [from_ahead(): lax.ppermute(value, axis, [((i + step) % count, i) for i in range(count)])]
    all_to_all x5, starting transfers between devices: 57.5 us -> 75.2 us  [exchange(): return lax.all_to_all(pieces, axes, split_axis=0, concat_axis=0, tiled=True)]
    ppermute x14 -> x8, waiting for transfers between devices: 35.8 us -> 22.6 us  [from_ahead(): lax.ppermute(value, axis, [((i + step) % count, i) for i in range(count)])]
    unnamed x18 -> x10, local copies, waits for them, and re-layouts: 6.21 us -> 1.32 us
    all_to_all x5, waiting for transfers between devices: 54.4 us -> 51.3 us  [exchange(): return lax.all_to_all(pieces, axes, split_axis=0, concat_axis=0, tiled=True)]
  transfers between devices with their start and end apart: 19 -> 13, of which waited for: 13 -> 9; matrix products, arithmetic and copies ran while one was open for 5% -> 6% of each run, Pallas kernels for 1% -> 1%
where the time goes in v6:
time: 244 us; the launch traced here: 242 us
  starting transfers between devices  100 us (41%)
  waiting for transfers between devices  73.9 us (30%)
  blocking collectives  40.7 us (17%)
  other arithmetic  8.54 us (3%)
  local copies, waits for them, and re-layouts  7.34 us (3%)
  Pallas kernels  5.51 us (2%)
  between operations  3.44 us (1%)
    all_to_all x5, starting transfers between devices, exchange(): return lax.all_to_all(pieces, axes, split_axis=0, concat_axis=0, tiled=True)  75.2 us
    all_to_all x5, waiting for transfers between devices, exchange(): return lax.all_to_all(pieces, axes, split_axis=0, concat_axis=0, tiled=True)  51.3 us
    all_gather x1, blocking collectives, local(): held = lax.all_gather(held, 'z', axis=0, tiled=False)  40.7 us
    ppermute x8, starting transfers between devices, from_ahead(): lax.ppermute(value, axis, [((i + step) % count, i) for i in range(count)])  24.9 us
    ppermute x8, waiting for transfers between devices, from_ahead(): lax.ppermute(value, axis, [((i + step) % count, i) for i in range(count)])  22.6 us
  transfers between devices with their start and end apart: 13, of which 9 were waited for; matrix products, arithmetic and copies ran while one was open for 6% of the time, Pallas kernels for 1%

profile of v6, /device:TPU:1, one launch (start us, length us, event | category | flops | bytes accessed | tf_op | source)
XLA Modules:
  0.0 241.6 jit_solution(12585163564928763517)
XLA Ops:
  0.6 0.0 copy-start
  0.6 0.0 copy-start.1
  0.7 1.3 copy-done.1
  2.0 0.8 shard_map.59
  2.7 10.4 %all-to-all-start = ((f32[32,1,128]{2,1,0:T(1,128)}), f32[32,1,128]{2,1,0:T(1,128)S(1)}, u32[]{:S(2)}, u32[]{:S(2)}) async-start(f32[32,1,128]{2,1,0:T(1,128)} %get-tuple-element.18), calls=%async_computation | async-start | bytes 32768 | tf_op jit(solution)/shard_map/all_to_all | solution.py:320
  13.1 0.7 compare_reduce_fusion
  13.8 0.7 remainder_reduce_fusion
  14.5 0.7 bitcast_select_fusion
  15.2 0.1 iota_compare_fusion
  15.3 0.1 ne.197
  15.4 0.1 rem.133
  15.6 0.1 div.61
  15.7 0.2 fusion.3
  15.9 4.1 %all-to-all-done = f32[32,1,128]{2,1,0:T(1,128)S(1)} async-done(((f32[32,1,128]{2,1,0:T(1,128)}), f32[32,1,128]{2,1,0:T(1,128)S(1)}, u32[]{:S(2)}, u32[]{:S(2)}) %all-to-all-start) | async-done | bytes 16416 | tf_op jit(solution)/shard_map/all_to_all | solution.py:320
  20.0 0.1 fusion.5
  20.1 0.0 copy-done
  20.1 1.6 gather_fusion.1
  21.7 2.5 %collective-permute-start = (bf16[64,8,1024]{2,1,0:T(8,128)(2,1)}, bf16[64,8,1024]{2,1,0:T(8,128)(2,1)}, u32[]{:S(2)}, u32[]{:S(2)}) collective-permute-start(bf16[64,8,1024]{2,1,0:T(8,128)(2,1)} %gather_fusion.1), channel_id=1, source_target_pairs={{4,0},{0,4},{5,1},{1,5},{6,2},{2,6},{7,3},{3,7},{12,8},{8,12},{13,... | collective-permute-start | bytes 3145736 | tf_op jit(solution)/shard_map/ppermute | solution.py:325
  24.3 0.6 broadcast_in_dim.72
  24.9 13.0 %all-to-all-start.1 = ((f32[16,1,128]{2,1,0:T(1,128)}), f32[16,1,128]{2,1,0:T(1,128)S(1)}, u32[]{:S(2)}, u32[]{:S(2)}) async-start(f32[16,1,128]{2,1,0:T(1,128)} %broadcast_in_dim.72), calls=%async_computation.1 | async-start | bytes 16384 | tf_op jit(solution)/shard_map/all_to_all | solution.py:320
  38.0 0.6 gather_fusion
  38.6 10.6 %all-to-all-done.1 = f32[16,1,128]{2,1,0:T(1,128)S(1)} async-done(((f32[16,1,128]{2,1,0:T(1,128)}), f32[16,1,128]{2,1,0:T(1,128)S(1)}, u32[]{:S(2)}, u32[]{:S(2)}) %all-to-all-start.1) | async-done | bytes 8224 | tf_op jit(solution)/shard_map/all_to_all | solution.py:320
  49.2 3.0 %collective-permute-start.2 = (f32[256,512]{1,0:T(8,128)S(1)}, f32[256,512]{1,0:T(8,128)}, u32[]{:S(2)}, u32[]{:S(2)}) collective-permute-start(f32[256,512]{1,0:T(8,128)S(1)} %get-tuple-element.25), channel_id=1, source_target_pairs={{2,0},{3,1},{0,2},{1,3},{6,4},{7,5},{4,6},{5,7},{10,8},{11,9},{8,1... | collective-permute-start | bytes 1572872 | tf_op jit(solution)/shard_map/ppermute | solution.py:325
  52.1 3.7 %collective-permute-start.1 = (f32[256,512]{1,0:T(8,128)S(1)}, f32[256,512]{1,0:T(8,128)}, u32[]{:S(2)}, u32[]{:S(2)}) collective-permute-start(f32[256,512]{1,0:T(8,128)S(1)} %get-tuple-element.25), channel_id=1, source_target_pairs={{1,0},{2,1},{3,2},{0,3},{5,4},{6,5},{7,6},{4,7},{9,8},{10,9},{11,1... | collective-permute-start | bytes 1572872 | tf_op jit(solution)/shard_map/ppermute | solution.py:325
  55.8 1.9 collective-permute-start.3
  57.7 0.0 collective-permute-done
  57.7 2.6 %add_convert_fusion = bf16[64,8,1024]{2,1,0:T(8,128)(2,1)} fusion(bf16[64,8,1024]{2,1,0:T(8,128)(2,1)} %collective-permute-done, bf16[64,8,1024]{2,1,0:T(8,128)(2,1)S(1)} %gather_fusion), kind=kLoop, calls=%fused_computation.4 | loop fusion | flops 2097152 | bytes 3145728 | tf_op jit(solution)/shard_map/convert_element_type | solution.py:373
  60.4 0.0 copy-done.2
  60.4 4.7 %all-to-all-start.2 = ((bf16[64,8,1024]{2,1,0:T(8,128)(2,1)}), bf16[64,8,1024]{2,1,0:T(8,128)(2,1)S(1)}, u32[]{:S(2)}, u32[]{:S(2)}) async-start(bf16[64,8,1024]{2,1,0:T(8,128)(2,1)} %add_convert_fusion), calls=%async_computation.2 | async-start | bytes 2097152 | tf_op jit(solution)/shard_map/all_to_all | solution.py:320
  65.0 0.0 copy-done.4
  65.0 0.6 fusion.18
  68.2 0.7 pad_add_fusion.scalar_ref
  68.8 9.1 %collective-permute-done.3.three_hbm = f32[256,512]{1,0:T(8,128)} collective-permute-done((f32[256,512]{1,0:T(8,128)S(1)}, f32[256,512]{1,0:T(8,128)}, u32[]{:S(2)}, u32[]{:S(2)}) %collective-permute-start.3) | collective-permute-done | bytes 524320 | tf_op jit(solution)/shard_map/ppermute | solution.py:325
  77.9 0.0 collective-permute-done.2.two_hbm
  77.9 0.0 collective-permute-done.1.one_hbm
  77.9 3.2 %shard_map.60 = (bf16[128,16,128]{2,1,0:T(8,128)(2,1)}, bf16[1024,1024]{1,0:T(8,128)(2,1)}) custom-call(s32[4]{0:T(128)} %pad_add_fusion.scalar_ref, f32[16,128]{1,0:T(8,128)} %bitcast.87, f32[256,1024]{1,0:T(8,128)} %bitcast.74, f32[256,512]{1,0:T(8,128)} %collective-permute-done.1.one_hbm, f32[256,512]{1,0:T(8,128)} %collective-permute-done.2.two_hbm, ...), custom_call_target="tpu_custom_call" | custom-call | flops 38654705664 | bytes 6291456 | tf_op jit(solution)/shard_map/pallas_call | solution.py:233
  81.1 0.0 copy-start.3
  81.1 35.4 %all-to-all-done.2 = bf16[64,8,1024]{2,1,0:T(8,128)(2,1)S(1)} async-done(((bf16[64,8,1024]{2,1,0:T(8,128)(2,1)}), bf16[64,8,1024]{2,1,0:T(8,128)(2,1)S(1)}, u32[]{:S(2)}, u32[]{:S(2)}) %all-to-all-start.2) | async-done | bytes 1048608 | tf_op jit(solution)/shard_map/all_to_all | solution.py:320
  116.5 0.2 reduce_sum.43
  116.7 27.2 %all-to-all-start.3 = ((bf16[128,16,128]{2,1,0:T(8,128)(2,1)}), bf16[128,16,128]{2,1,0:T(8,128)(2,1)S(1)}, u32[]{:S(2)}, u32[]{:S(2)}) async-start(bf16[128,16,128]{2,1,0:T(8,128)(2,1)} %get-tuple-element.29), calls=%async_computation.3 | async-start | bytes 1048576 | tf_op jit(solution)/shard_map/all_to_all | solution.py:320
  143.8 0.6 fusion.10
  144.5 0.0 copy-done.3
  144.5 0.2 select_reduce_fusion
  144.6 0.7 compare_select_fusion.9.index_ref
  145.3 2.0 convolution_convert_fusion
  147.3 40.7 %all-gather = bf16[128,1024]{1,0:T(8,128)(2,1)S(1)} all-gather(bf16[8,1024]{1,0:T(8,128)(2,1)S(1)} %convolution_convert_fusion), channel_id=2, replica_groups=mesh['z'=16,'x'=4,'c'=2,'mp'=4] {'z'}, dimensions={0}, use_global_device_ids=true | all-gather | bytes 278528 | tf_op jit(solution)/shard_map/all_gather | solution.py:387
  188.0 0.0 all-to-all-done.3.src_ref
  188.0 1.6 shard_map.61
  189.6 20.0 %all-to-all-start.4 = ((bf16[128,16,128]{2,1,0:T(8,128)(2,1)}), bf16[128,16,128]{2,1,0:T(8,128)(2,1)S(1)}, u32[]{:S(2)}, u32[]{:S(2)}) async-start(bf16[128,16,128]{2,1,0:T(8,128)(2,1)} %shard_map.61), calls=%async_computation.4 | async-start | bytes 1048576 | tf_op jit(solution)/shard_map/all_to_all | solution.py:320
  209.6 3.3 %collective-permute-start.6 = (bf16[16,8,1024]{2,1,0:T(8,128)(2,1)S(1)}, bf16[16,8,1024]{2,1,0:T(8,128)(2,1)S(1)}, u32[]{:S(2)}, u32[]{:S(2)}) collective-permute-start(bf16[16,8,1024]{2,1,0:T(8,128)(2,1)S(1)} %bitcast.78), channel_id=1, source_target_pairs={{24,0},{0,8},{8,16},{16,24},{25,1},{1,9},{9,17},{17,25},{26,2},{2,... | collective-permute-start | bytes 786440 | tf_op jit(solution)/shard_map/ppermute | solution.py:325
  212.9 4.3 %collective-permute-start.5 = (bf16[16,8,1024]{2,1,0:T(8,128)(2,1)S(1)}, bf16[16,8,1024]{2,1,0:T(8,128)(2,1)S(1)}, u32[]{:S(2)}, u32[]{:S(2)}) collective-permute-start(bf16[16,8,1024]{2,1,0:T(8,128)(2,1)S(1)} %bitcast.79), channel_id=1, source_target_pairs={{16,0},{24,8},{0,16},{8,24},{17,1},{25,9},{1,17},{9,25},{18,2},{26... | collective-permute-start | bytes 786440 | tf_op jit(solution)/shard_map/ppermute | solution.py:325
  217.2 3.1 %collective-permute-start.4 = (bf16[16,8,1024]{2,1,0:T(8,128)(2,1)S(1)}, bf16[16,8,1024]{2,1,0:T(8,128)(2,1)S(1)}, u32[]{:S(2)}, u32[]{:S(2)}) collective-permute-start(bf16[16,8,1024]{2,1,0:T(8,128)(2,1)S(1)} %bitcast.80), channel_id=1, source_target_pairs={{8,0},{16,8},{24,16},{0,24},{9,1},{17,9},{25,17},{1,25},{10,2},{18... | collective-permute-start | bytes 786440 | tf_op jit(solution)/shard_map/ppermute | solution.py:325
  220.3 0.1 collective-permute-done.6
  220.4 9.9 %collective-permute-done.5 = bf16[16,8,1024]{2,1,0:T(8,128)(2,1)S(1)} collective-permute-done((bf16[16,8,1024]{2,1,0:T(8,128)(2,1)S(1)}, bf16[16,8,1024]{2,1,0:T(8,128)(2,1)S(1)}, u32[]{:S(2)}, u32[]{:S(2)}) %collective-permute-start.5) | collective-permute-done | bytes 262176 | tf_op jit(solution)/shard_map/ppermute | solution.py:325
  230.2 1.5 collective-permute-done.4
  231.8 0.2 fusion.17
  232.0 3.1 %collective-permute-start.7 = (bf16[4,16,8,1024]{3,2,1,0:T(8,128)(2,1)S(1)}, bf16[4,16,8,1024]{3,2,1,0:T(8,128)(2,1)S(1)}, u32[]{:S(2)}, u32[]{:S(2)}) collective-permute-start(bf16[4,16,8,1024]{3,2,1,0:T(8,128)(2,1)S(1)} %get-tuple-element.39), channel_id=1, source_target_pairs={{4,0},{0,4},{5,1},{1,5},{6,2},{2,6},{7,3},{3,7},{12,8},{8,12},{13,... | collective-permute-start | bytes 3145736 | tf_op jit(solution)/shard_map/ppermute | solution.py:325
  235.1 0.2 select_reduce_fusion.1
  235.4 2.0 collective-permute-done.7
  237.4 0.2 pad_maximum_fusion
  237.6 1.6 gather_fusion.2
  239.1 1.3 all-to-all-done.4
  240.4 0.1 copy.12
  240.5 1.0 reshape.318
  (9 shorter events, 0.1 us)
Async XLA Ops:
  0.6 19.5 %copy-start = (bf16[1,56,8,1024]{3,2,1,0:T(8,128)(2,1)S(1)}, bf16[1,56,8,1024]{3,2,1,0:T(8,128)(2,1)}, u32[]{:S(2)}) copy-start(bf16[1,56,8,1024]{3,2,1,0:T(8,128)(2,1)} %param.5) | copy-start | bytes 2752516
  0.6 1.3 copy-start.1
  2.7 17.3 %all-to-all-start = ((f32[32,1,128]{2,1,0:T(1,128)}), f32[32,1,128]{2,1,0:T(1,128)S(1)}, u32[]{:S(2)}, u32[]{:S(2)}) async-start(f32[32,1,128]{2,1,0:T(1,128)} %get-tuple-element.18), calls=%async_computation | async-start | bytes 32768 | tf_op jit(solution)/shard_map/all_to_all | solution.py:320
  21.7 36.0 %collective-permute-start = (bf16[64,8,1024]{2,1,0:T(8,128)(2,1)}, bf16[64,8,1024]{2,1,0:T(8,128)(2,1)}, u32[]{:S(2)}, u32[]{:S(2)}) collective-permute-start(bf16[64,8,1024]{2,1,0:T(8,128)(2,1)} %gather_fusion.1), channel_id=1, source_target_pairs={{4,0},{0,4},{5,1},{1,5},{6,2},{2,6},{7,3},{3,7},{12,8},{8,12},{13,... | collective-permute-start | bytes 3145736 | tf_op jit(solution)/shard_map/ppermute | solution.py:325
  24.9 24.3 %all-to-all-start.1 = ((f32[16,1,128]{2,1,0:T(1,128)}), f32[16,1,128]{2,1,0:T(1,128)S(1)}, u32[]{:S(2)}, u32[]{:S(2)}) async-start(f32[16,1,128]{2,1,0:T(1,128)} %broadcast_in_dim.72), calls=%async_computation.1 | async-start | bytes 16384 | tf_op jit(solution)/shard_map/all_to_all | solution.py:320
  49.2 11.2 %copy-start.2 = (f32[16,1,128]{2,1,0:T(1,128)}, f32[16,1,128]{2,1,0:T(1,128)S(1)}, u32[]{:S(2)}) copy-start(f32[16,1,128]{2,1,0:T(1,128)S(1)} %all-to-all-done.1) | copy-start | bytes 24580
  49.2 15.9 %copy-start.4 = (s32[128,1]{0,1:T(1,128)S(1)}, s32[128,1]{0,1:T(1,128)}, u32[]{:S(2)}) copy-start(s32[128,1]{0,1:T(1,128)} %param.6) | copy-start | bytes 1540
  49.2 28.7 %collective-permute-start.2 = (f32[256,512]{1,0:T(8,128)S(1)}, f32[256,512]{1,0:T(8,128)}, u32[]{:S(2)}, u32[]{:S(2)}) collective-permute-start(f32[256,512]{1,0:T(8,128)S(1)} %get-tuple-element.25), channel_id=1, source_target_pairs={{2,0},{3,1},{0,2},{1,3},{6,4},{7,5},{4,6},{5,7},{10,8},{11,9},{8,1... | collective-permute-start | bytes 1572872 | tf_op jit(solution)/shard_map/ppermute | solution.py:325
  52.1 25.7 %collective-permute-start.1 = (f32[256,512]{1,0:T(8,128)S(1)}, f32[256,512]{1,0:T(8,128)}, u32[]{:S(2)}, u32[]{:S(2)}) collective-permute-start(f32[256,512]{1,0:T(8,128)S(1)} %get-tuple-element.25), channel_id=1, source_target_pairs={{1,0},{2,1},{3,2},{0,3},{5,4},{6,5},{7,6},{4,7},{9,8},{10,9},{11,1... | collective-permute-start | bytes 1572872 | tf_op jit(solution)/shard_map/ppermute | solution.py:325
  55.8 22.1 %collective-permute-start.3 = (f32[256,512]{1,0:T(8,128)S(1)}, f32[256,512]{1,0:T(8,128)}, u32[]{:S(2)}, u32[]{:S(2)}) collective-permute-start(f32[256,512]{1,0:T(8,128)S(1)} %get-tuple-element.26), channel_id=1, source_target_pairs={{3,0},{0,1},{1,2},{2,3},{7,4},{4,5},{5,6},{6,7},{11,8},{8,9},{9,10... | collective-permute-start | bytes 1572872 | tf_op jit(solution)/shard_map/ppermute | solution.py:325
  60.4 56.1 %all-to-all-start.2 = ((bf16[64,8,1024]{2,1,0:T(8,128)(2,1)}), bf16[64,8,1024]{2,1,0:T(8,128)(2,1)S(1)}, u32[]{:S(2)}, u32[]{:S(2)}) async-start(bf16[64,8,1024]{2,1,0:T(8,128)(2,1)} %add_convert_fusion), calls=%async_computation.2 | async-start | bytes 2097152 | tf_op jit(solution)/shard_map/all_to_all | solution.py:320
  81.1 63.4 %copy-start.3 = (s32[128,1]{0,1:T(1,128)S(1)}, s32[128,1]{0,1:T(1,128)}, u32[]{:S(2)}) copy-start(s32[128,1]{0,1:T(1,128)} %param.7) | copy-start | bytes 1540
  116.7 71.4 %all-to-all-start.3 = ((bf16[128,16,128]{2,1,0:T(8,128)(2,1)}), bf16[128,16,128]{2,1,0:T(8,128)(2,1)S(1)}, u32[]{:S(2)}, u32[]{:S(2)}) async-start(bf16[128,16,128]{2,1,0:T(8,128)(2,1)} %get-tuple-element.29), calls=%async_computation.3 | async-start | bytes 1048576 | tf_op jit(solution)/shard_map/all_to_all | solution.py:320
  189.6 50.8 %all-to-all-start.4 = ((bf16[128,16,128]{2,1,0:T(8,128)(2,1)}), bf16[128,16,128]{2,1,0:T(8,128)(2,1)S(1)}, u32[]{:S(2)}, u32[]{:S(2)}) async-start(bf16[128,16,128]{2,1,0:T(8,128)(2,1)} %shard_map.61), calls=%async_computation.4 | async-start | bytes 1048576 | tf_op jit(solution)/shard_map/all_to_all | solution.py:320
  209.6 10.8 %collective-permute-start.6 = (bf16[16,8,1024]{2,1,0:T(8,128)(2,1)S(1)}, bf16[16,8,1024]{2,1,0:T(8,128)(2,1)S(1)}, u32[]{:S(2)}, u32[]{:S(2)}) collective-permute-start(bf16[16,8,1024]{2,1,0:T(8,128)(2,1)S(1)} %bitcast.78), channel_id=1, source_target_pairs={{24,0},{0,8},{8,16},{16,24},{25,1},{1,9},{9,17},{17,25},{26,2},{2,... | collective-permute-start | bytes 786440 | tf_op jit(solution)/shard_map/ppermute | solution.py:325
  212.9 17.4 %collective-permute-start.5 = (bf16[16,8,1024]{2,1,0:T(8,128)(2,1)S(1)}, bf16[16,8,1024]{2,1,0:T(8,128)(2,1)S(1)}, u32[]{:S(2)}, u32[]{:S(2)}) collective-permute-start(bf16[16,8,1024]{2,1,0:T(8,128)(2,1)S(1)} %bitcast.79), channel_id=1, source_target_pairs={{16,0},{24,8},{0,16},{8,24},{17,1},{25,9},{1,17},{9,25},{18,2},{26... | collective-permute-start | bytes 786440 | tf_op jit(solution)/shard_map/ppermute | solution.py:325
  217.2 14.6 %collective-permute-start.4 = (bf16[16,8,1024]{2,1,0:T(8,128)(2,1)S(1)}, bf16[16,8,1024]{2,1,0:T(8,128)(2,1)S(1)}, u32[]{:S(2)}, u32[]{:S(2)}) collective-permute-start(bf16[16,8,1024]{2,1,0:T(8,128)(2,1)S(1)} %bitcast.80), channel_id=1, source_target_pairs={{8,0},{16,8},{24,16},{0,24},{9,1},{17,9},{25,17},{1,25},{10,2},{18... | collective-permute-start | bytes 786440 | tf_op jit(solution)/shard_map/ppermute | solution.py:325
  232.0 5.4 %collective-permute-start.7 = (bf16[4,16,8,1024]{3,2,1,0:T(8,128)(2,1)S(1)}, bf16[4,16,8,1024]{3,2,1,0:T(8,128)(2,1)S(1)}, u32[]{:S(2)}, u32[]{:S(2)}) collective-permute-start(bf16[4,16,8,1024]{3,2,1,0:T(8,128)(2,1)S(1)} %get-tuple-element.39), channel_id=1, source_target_pairs={{4,0},{0,4},{5,1},{1,5},{6,2},{2,6},{7,3},{3,7},{12,8},{8,12},{13,... | collective-permute-start | bytes 3145736 | tf_op jit(solution)/shard_map/ppermute | solution.py:325

commit v7 on v6

--- a/solution.py
+++ b/solution.py
@@ -43,39 +43,6 @@
 
 def dot(left, right):
     return jnp.dot(left, right, preferred_element_type=jnp.float32)
-
-
-def solve_small(u, lines):
-    size = len(lines)
-    lower, inverse = {}, []
-    solved = []
-    scale = reciprocal(u[0, 0])
-    for j in range(size):
-        inverse.append(scale)
-        if j + 1 < size:
-            pivot = u[j + 1, j + 1] - (u[j, j + 1] * u[j, j + 1]) * scale
-        for i in range(j + 1, size):
-            lower[i, j] = u[j, i] * scale
-        if j + 1 < size:
-            scale = reciprocal(pivot)
-        for i in range(j + 1, size):
-            for m in range(i, size):
-                if m > j + 1:
-                    u[i, m] = u[i, m] - lower[i, j] * u[j, m]
-        solved.append(lines[j])
-        for i in range(j + 1, size):
-            lines[i] = [x - lower[i, j] * y for x, y in zip(lines[i], lines[j])]
-    for j in reversed(range(size)):
-        solved[j] = [x * inverse[j] for x in solved[j]]
-        for i in range(j + 1, size):
-            solved[j] = [x - lower[i, j] * y for x, y in zip(solved[j], solved[i])]
-    return solved
-
-
-def tree_sum(terms):
-    while len(terms) > 1:
-        terms = [a + b for a, b in zip(terms[::2], terms[1::2])]
-    return terms[0]
 
 
 def panel_sweep(groups, first):
@@ -85,30 +52,41 @@
         tile, lane = divmod(first + p * SUB, LANES)
         pivot_lanes = (lane_ids // SUB) == lane // SUB
         spread = [lane_of(groups[p][tile], lane + j) for j in range(SUB)]
-        u = {(i, j): row_of(spread[j], i) for j in range(SUB) for i in range(j + 1)}
-        sources = []
+        rows = list(groups[p])
+        rows[tile] = jnp.where(
+            pivot_lanes, jnp.where(lane_ids == sub_ids + lane, 1.0, 0.0), rows[tile]
+        )
+        pivot = row_of(spread[0], 0)
         for j in range(SUB):
-            line = [row_of(x, j) for x in groups[p]]
-            line[tile] = jnp.where(
-                pivot_lanes, jnp.where(lane_ids == lane + j, -1.0, 0.0), line[tile]
-            )
-            sources.append(line)
-        tiles = range(len(groups[p]))
-        lines = solve_small(u, sources)
+            here = sub_ids == j
+            scale = reciprocal(pivot)
+            if j + 1 < SUB:
+                cross = row_of(spread[j], j + 1) * row_of(spread[j + 1], j)
+                pivot = row_of(spread[j + 1], j + 1) - cross * scale
+            column = jnp.where(here, -1.0, spread[j])
+
+            def eliminate(x):
+                line = row_of(x, j)
+                return jnp.where(here, 0.0, x) - (column * line) * scale
+
+            rows = [eliminate(x) for x in rows]
+            for i in range(j + 1, SUB):
+                spread[i] = eliminate(spread[i])
+        rows[tile] = jnp.where(pivot_lanes, -rows[tile], rows[tile])
+        lines = [[row_of(x, j) for x in rows] for j in range(SUB)]
         for g in range(len(groups)):
             if g == p:
                 continue
             factors = [lane_of(groups[g][tile], lane + j) for j in range(SUB)]
-            for t in tiles:
+            for t in range(len(rows)):
+                terms = [factors[j] * lines[j][t] for j in range(SUB)]
+                while len(terms) > 1:
+                    terms = [a + b for a, b in zip(terms[::2], terms[1::2])]
                 kept = groups[g][t]
                 if t == tile:
                     kept = jnp.where(pivot_lanes, 0.0, kept)
-                groups[g][t] = kept - tree_sum([factors[j] * lines[j][t] for j in range(SUB)])
-        for t in tiles:
-            row = lines[0][t]
-            for j in range(1, SUB):
-                row = jnp.where(sub_ids == j, lines[j][t], row)
-            groups[p][t] = row
+                groups[g][t] = kept - terms[0]
+        groups[p] = rows
     return groups
 
 
@@ -135,12 +113,16 @@
 
 
 def invert_kernel(
-    scalar_ref, traces_ref, rows_hbm, one_hbm, two_hbm, three_hbm,
+    slots_ref, traces_ref, rows_hbm, one_hbm, two_hbm, three_hbm,
     band_hbm, full_ref, m_ref, d_ref, left_ref, right_ref, band_ref, in_sems, out_sem,
 ):
     wide, n = rows_hbm.shape
     count = n // wide
-    mp_index = scalar_ref[1]
+    dp_index, mp_index = slots_ref[slots_ref.shape[0] - 2], slots_ref[slots_ref.shape[0] - 1]
+    own = slots_ref[dp_index]
+    a_span = FF // n
+    layer_blocks = a_span + D // n
+    layer = lax.div(own, layer_blocks)
 
     def block(i):
         return slice(i * wide, (i + 1) * wide)
@@ -148,7 +130,7 @@
     def place(i):
         return pl.ds(pl.multiple_of(lax.rem(mp_index + i, count) * wide, wide), wide)
 
-    @pl.when(scalar_ref[0] > 0)
+    @pl.when(own >= 0)
     def _():
         arrivals = [(rows_hbm.at[:, place(j)], 0, j) for j in range(count)]
         for i, source in enumerate((one_hbm, two_hbm, three_hbm)):
@@ -167,9 +149,9 @@
         def pick_lane(lane):
             return jnp.sum(jnp.where(lane_ids == lane, traces, 0.0), axis=1, keepdims=True)
 
-        lane = 2 * scalar_ref[2]
+        lane = 2 * layer
         ratio = jnp.sqrt(pick_lane(lane) / FF / (pick_lane(lane + 1) / D))
-        shift = jnp.where(scalar_ref[3] > 0, DAMPING_BASE * ratio, DAMPING_BASE / ratio)
+        shift = jnp.where(lax.rem(own, layer_blocks) < a_span, DAMPING_BASE * ratio, DAMPING_BASE / ratio)
         diagonal = lax.broadcasted_iota(jnp.int32, (wide, wide), 0) == lax.broadcasted_iota(
             jnp.int32, (wide, wide), 1
         )
@@ -215,7 +197,7 @@
                 full_ref[place(i), place(j)] = (-m_ref[block(i), block(j)]).astype(jnp.bfloat16)
         sent.wait()
 
-    @pl.when(scalar_ref[0] <= 0)
+    @pl.when(own < 0)
     def _():
         band_ref[...] = jnp.zeros(band_ref.shape, jnp.bfloat16)
         full_ref[...] = jnp.zeros(full_ref.shape, jnp.bfloat16)
@@ -224,7 +206,7 @@
         sent.wait()
 
 
-def invert(scalars, traces, rows, one, two, three):
+def invert(slots, traces, rows, one, two, three):
     wide, n = rows.shape
     in_smem = pl.BlockSpec(memory_space=pltpu.SMEM)
     in_vmem = pl.BlockSpec(memory_space=pltpu.VMEM)
@@ -251,7 +233,7 @@
         cost_estimate=pl.CostEstimate(
             flops=36 * n * n * n, bytes_accessed=6 * n * n, transcendentals=0
         ),
-    )(scalars, traces, rows, one, two, three)
+    )(slots, traces, rows, one, two, three)
 
 
 def prepare_kernel(mp_ref, rows_ref, near_ref, far_ref, trace_ref):
@@ -336,13 +318,8 @@
     tile_count, row_count = gradients.shape[1:3]
     a_span = FF // width
     layer_blocks = a_span + D // width
-    layers = tile_count // a_span
     old_flat = old_slots.reshape(dp_count)
     new_flat = new_slots.reshape(dp_count)
-    own = lax.dynamic_index_in_dim(old_flat, dp_index, keepdims=False)
-    own_block = jnp.maximum(own, 0)
-    own_layer = own_block // layer_blocks
-    own_input = own_block % layer_blocks < a_span
 
     rows = old_factors[0, 0]
     near, far, trace = prepare(mp_index, rows, x_count * c_count * mp_count)
@@ -352,10 +329,9 @@
     plane_bin = jnp.where(plane >= 0, plane_bin, -1)
     lane_ids = lax.broadcasted_iota(jnp.int32, (1, 1, LANES), 2)
     binned = jnp.sum(jnp.where(lane_ids == plane_bin[:, None, None], trace, 0.0), axis=(0, 1))
-    binned, tiles = lax.optimization_barrier((binned, gradients[0]))
+    binned, near, far, tiles = lax.optimization_barrier((binned, near, far, gradients[0]))
     binned = jnp.broadcast_to(binned[None, None], (z_count, 1, LANES))
     traces = exchange(binned, "z").reshape(z_count, LANES)
-    traces, near, far = lax.optimization_barrier((traces, near, far))
 
     one = from_ahead(near, "mp", 1)
     two = from_ahead(near, "mp", 2)
@@ -374,10 +350,9 @@
     partial = exchange(partial, ("z", "x"))
     tile = jnp.sum(partial.astype(jnp.float32), axis=0).astype(jnp.bfloat16)
 
-    scalars = jnp.stack(
-        [v.astype(jnp.int32) for v in (own >= 0, mp_index, own_layer, own_input)]
-    )
-    inverse_band, inverse = invert(scalars, traces, rows, one, two, three)
+    places = jnp.stack([dp_index.astype(jnp.int32), mp_index.astype(jnp.int32)])
+    slots = jnp.concatenate([old_flat, places])
+    inverse_band, inverse = invert(slots, traces, rows, one, two, three)
     inverse_band, tile = lax.optimization_barrier((inverse_band, tile))
 
     def gather(value, axis, steps):

time: 244 us -> 232 us (0.951)
  starting transfers between devices: 100 us -> 93.3 us
  between operations: 3.44 us -> 0.93 us
    ppermute x8, waiting for transfers between devices: 22.6 us -> 13.5 us  [from_ahead(): lax.ppermute(value, axis, [((i + step) % count, i) for i in range(count)])]
    all_to_all x5, waiting for transfers between devices: 51.3 us -> 58.5 us  [exchange(): return lax.all_to_all(pieces, axes, split_axis=0, concat_axis=0, tiled=True)]
    all_to_all x5, starting transfers between devices: 75.2 us -> 68.6 us  [exchange(): return lax.all_to_all(pieces, axes, split_axis=0, concat_axis=0, tiled=True)]
  transfers between devices with their start and end apart: 13 -> 13, of which waited for: 9 -> 8; matrix products, arithmetic and copies ran while one was open for 6% -> 6% of each run, Pallas kernels for 1% -> 1%
where the time goes in v7:
time: 232 us; the launch traced here: 230 us
  starting transfers between devices  93.3 us (40%)
  waiting for transfers between devices  72 us (31%)
  blocking collectives  40.8 us (18%)
  other arithmetic  7.92 us (3%)
  local copies, waits for them, and re-layouts  7.34 us (3%)
  Pallas kernels  5.34 us (2%)
    all_to_all x5, starting transfers between devices, exchange(): return lax.all_to_all(pieces, axes, split_axis=0, concat_axis=0, tiled=True)  68.6 us
    all_to_all x5, waiting for transfers between devices, exchange(): return lax.all_to_all(pieces, axes, split_axis=0, concat_axis=0, tiled=True)  58.5 us
    all_gather x1, blocking collectives, local(): held = lax.all_gather(held, 'z', axis=0, tiled=False)  40.8 us
    ppermute x8, starting transfers between devices, from_ahead(): lax.ppermute(value, axis, [((i + step) % count, i) for i in range(count)])  24.8 us
    ppermute x8, waiting for transfers between devices, from_ahead(): lax.ppermute(value, axis, [((i + step) % count, i) for i in range(count)])  13.5 us
  transfers between devices with their start and end apart: 13, of which 8 were waited for; matrix products, arithmetic and copies ran while one was open for 6% of the time, Pallas kernels for 1%

profile of v7, /device:TPU:1, one launch (start us, length us, event | category | flops | bytes accessed | tf_op | source)
XLA Modules:
  0.0 229.6 jit_solution(10834619332404442993)
XLA Ops:
  0.6 0.0 copy-start
  0.6 0.0 copy-start.1
  0.7 1.3 copy-done.1
  2.0 0.8 shard_map.59
  2.7 10.4 %all-to-all-start = ((f32[32,1,128]{2,1,0:T(1,128)}), f32[32,1,128]{2,1,0:T(1,128)S(1)}, u32[]{:S(2)}, u32[]{:S(2)}) async-start(f32[32,1,128]{2,1,0:T(1,128)} %get-tuple-element.17), calls=%async_computation | async-start | bytes 32768 | tf_op jit(solution)/shard_map/all_to_all | solution.py:302
  13.1 0.7 compare_reduce_fusion
  13.8 0.7 remainder_reduce_fusion
  14.5 0.7 bitcast_select_fusion
  15.2 0.1 iota_compare_fusion
  15.3 0.1 ne.179
  15.4 0.1 rem.122
  15.6 0.1 div.52
  15.7 0.2 fusion.3
  15.9 4.1 %all-to-all-done = f32[32,1,128]{2,1,0:T(1,128)S(1)} async-done(((f32[32,1,128]{2,1,0:T(1,128)}), f32[32,1,128]{2,1,0:T(1,128)S(1)}, u32[]{:S(2)}, u32[]{:S(2)}) %all-to-all-start) | async-done | bytes 16416 | tf_op jit(solution)/shard_map/all_to_all | solution.py:302
  20.0 0.1 fusion.5
  20.1 0.0 copy-done
  20.1 1.6 gather_fusion.1
  21.7 2.5 %collective-permute-start = (bf16[64,8,1024]{2,1,0:T(8,128)(2,1)}, bf16[64,8,1024]{2,1,0:T(8,128)(2,1)}, u32[]{:S(2)}, u32[]{:S(2)}) collective-permute-start(bf16[64,8,1024]{2,1,0:T(8,128)(2,1)} %gather_fusion.1), channel_id=1, source_target_pairs={{4,0},{0,4},{5,1},{1,5},{6,2},{2,6},{7,3},{3,7},{12,8},{8,12},{13,... | collective-permute-start | bytes 3145736 | tf_op jit(solution)/shard_map/ppermute | solution.py:307
  24.3 2.8 %collective-permute-start.2 = (f32[256,512]{1,0:T(8,128)S(1)}, f32[256,512]{1,0:T(8,128)}, u32[]{:S(2)}, u32[]{:S(2)}) collective-permute-start(f32[256,512]{1,0:T(8,128)S(1)} %get-tuple-element.23), channel_id=1, source_target_pairs={{2,0},{3,1},{0,2},{1,3},{6,4},{7,5},{4,6},{5,7},{10,8},{11,9},{8,1... | collective-permute-start | bytes 1572872 | tf_op jit(solution)/shard_map/ppermute | solution.py:307
  27.2 3.7 %collective-permute-start.1 = (f32[256,512]{1,0:T(8,128)S(1)}, f32[256,512]{1,0:T(8,128)}, u32[]{:S(2)}, u32[]{:S(2)}) collective-permute-start(f32[256,512]{1,0:T(8,128)S(1)} %get-tuple-element.23), channel_id=1, source_target_pairs={{1,0},{2,1},{3,2},{0,3},{5,4},{6,5},{7,6},{4,7},{9,8},{10,9},{11,1... | collective-permute-start | bytes 1572872 | tf_op jit(solution)/shard_map/ppermute | solution.py:307
  30.8 0.6 broadcast_in_dim.72
  31.4 13.0 %all-to-all-start.1 = ((f32[16,1,128]{2,1,0:T(1,128)}), f32[16,1,128]{2,1,0:T(1,128)S(1)}, u32[]{:S(2)}, u32[]{:S(2)}) async-start(f32[16,1,128]{2,1,0:T(1,128)} %broadcast_in_dim.72), calls=%async_computation.1 | async-start | bytes 16384 | tf_op jit(solution)/shard_map/all_to_all | solution.py:302
  44.5 1.9 collective-permute-start.3
  46.4 0.6 gather_fusion
  47.0 0.0 copy-start.3
  47.0 0.0 collective-permute-done
  47.0 2.6 %add_convert_fusion = bf16[64,8,1024]{2,1,0:T(8,128)(2,1)} fusion(bf16[64,8,1024]{2,1,0:T(8,128)(2,1)} %collective-permute-done, bf16[64,8,1024]{2,1,0:T(8,128)(2,1)S(1)} %gather_fusion), kind=kLoop, calls=%fused_computation.4 | loop fusion | flops 2097152 | bytes 3145728 | tf_op jit(solution)/shard_map/convert_element_type | solution.py:349
  49.7 6.0 %all-to-all-done.1 = f32[16,1,128]{2,1,0:T(1,128)S(1)} async-done(((f32[16,1,128]{2,1,0:T(1,128)}), f32[16,1,128]{2,1,0:T(1,128)S(1)}, u32[]{:S(2)}, u32[]{:S(2)}) %all-to-all-start.1) | async-done | bytes 8224 | tf_op jit(solution)/shard_map/all_to_all | solution.py:302
  55.7 7.0 %all-to-all-start.2 = ((bf16[64,8,1024]{2,1,0:T(8,128)(2,1)}), bf16[64,8,1024]{2,1,0:T(8,128)(2,1)S(1)}, u32[]{:S(2)}, u32[]{:S(2)}) async-start(bf16[64,8,1024]{2,1,0:T(8,128)(2,1)} %add_convert_fusion), calls=%async_computation.2 | async-start | bytes 2097152 | tf_op jit(solution)/shard_map/all_to_all | solution.py:302
  62.7 0.0 copy-done.3
  62.7 0.6 pad_add_fusion.slots_ref
  63.4 0.0 collective-permute-done.3.three_hbm
  63.4 0.0 collective-permute-done.2.two_hbm
  63.4 0.0 collective-permute-done.1.one_hbm
  63.4 0.0 copy-done.2
  63.4 3.0 %shard_map.60 = (bf16[128,16,128]{2,1,0:T(8,128)(2,1)}, bf16[1024,1024]{1,0:T(8,128)(2,1)}) custom-call(s32[130]{0:T(256)} %pad_add_fusion.slots_ref, f32[16,128]{1,0:T(8,128)} %bitcast.82, f32[256,1024]{1,0:T(8,128)} %bitcast.69, f32[256,512]{1,0:T(8,128)} %collective-permute-done.1.one_hbm, f32[256,512]{1,0:T(8,128)} %collective-permute-done.2.two_hbm, ...), custom_call_target="tpu_custom_call" | custom-call | flops 38654705664 | bytes 6291456 | tf_op jit(solution)/shard_map/pallas_call | solution.py:215
  66.4 0.0 copy-start.4
  66.4 47.1 %all-to-all-done.2 = bf16[64,8,1024]{2,1,0:T(8,128)(2,1)S(1)} async-done(((bf16[64,8,1024]{2,1,0:T(8,128)(2,1)}), bf16[64,8,1024]{2,1,0:T(8,128)(2,1)S(1)}, u32[]{:S(2)}, u32[]{:S(2)}) %all-to-all-start.2) | async-done | bytes 1048608 | tf_op jit(solution)/shard_map/all_to_all | solution.py:302
  113.5 0.2 reduce_sum.43
  113.7 18.2 %all-to-all-start.3 = ((bf16[128,16,128]{2,1,0:T(8,128)(2,1)}), bf16[128,16,128]{2,1,0:T(8,128)(2,1)S(1)}, u32[]{:S(2)}, u32[]{:S(2)}) async-start(bf16[128,16,128]{2,1,0:T(8,128)(2,1)} %get-tuple-element.27), calls=%async_computation.3 | async-start | bytes 1048576 | tf_op jit(solution)/shard_map/all_to_all | solution.py:302
  131.9 0.6 fusion.10
  132.5 0.0 copy-done.4
  132.5 0.2 select_reduce_fusion
  132.7 0.7 compare_select_fusion.9.index_ref
  133.4 2.0 convolution_convert_fusion
  135.3 40.8 %all-gather = bf16[128,1024]{1,0:T(8,128)(2,1)S(1)} all-gather(bf16[8,1024]{1,0:T(8,128)(2,1)S(1)} %convolution_convert_fusion), channel_id=2, replica_groups=mesh['z'=16,'x'=4,'c'=2,'mp'=4] {'z'}, dimensions={0}, use_global_device_ids=true | all-gather | bytes 278528 | tf_op jit(solution)/shard_map/all_gather | solution.py:362
  176.1 0.0 all-to-all-done.3.src_ref
  176.1 1.6 shard_map.61
  177.7 20.0 %all-to-all-start.4 = ((bf16[128,16,128]{2,1,0:T(8,128)(2,1)}), bf16[128,16,128]{2,1,0:T(8,128)(2,1)S(1)}, u32[]{:S(2)}, u32[]{:S(2)}) async-start(bf16[128,16,128]{2,1,0:T(8,128)(2,1)} %shard_map.61), calls=%async_computation.4 | async-start | bytes 1048576 | tf_op jit(solution)/shard_map/all_to_all | solution.py:302
  197.7 3.3 %collective-permute-start.6 = (bf16[16,8,1024]{2,1,0:T(8,128)(2,1)S(1)}, bf16[16,8,1024]{2,1,0:T(8,128)(2,1)S(1)}, u32[]{:S(2)}, u32[]{:S(2)}) collective-permute-start(bf16[16,8,1024]{2,1,0:T(8,128)(2,1)S(1)} %bitcast.73), channel_id=1, source_target_pairs={{24,0},{0,8},{8,16},{16,24},{25,1},{1,9},{9,17},{17,25},{26,2},{2,... | collective-permute-start | bytes 786440 | tf_op jit(solution)/shard_map/ppermute | solution.py:307
  201.0 4.3 %collective-permute-start.5 = (bf16[16,8,1024]{2,1,0:T(8,128)(2,1)S(1)}, bf16[16,8,1024]{2,1,0:T(8,128)(2,1)S(1)}, u32[]{:S(2)}, u32[]{:S(2)}) collective-permute-start(bf16[16,8,1024]{2,1,0:T(8,128)(2,1)S(1)} %bitcast.74), channel_id=1, source_target_pairs={{16,0},{24,8},{0,16},{8,24},{17,1},{25,9},{1,17},{9,25},{18,2},{26... | collective-permute-start | bytes 786440 | tf_op jit(solution)/shard_map/ppermute | solution.py:307
  205.3 3.1 %collective-permute-start.4 = (bf16[16,8,1024]{2,1,0:T(8,128)(2,1)S(1)}, bf16[16,8,1024]{2,1,0:T(8,128)(2,1)S(1)}, u32[]{:S(2)}, u32[]{:S(2)}) collective-permute-start(bf16[16,8,1024]{2,1,0:T(8,128)(2,1)S(1)} %bitcast.75), channel_id=1, source_target_pairs={{8,0},{16,8},{24,16},{0,24},{9,1},{17,9},{25,17},{1,25},{10,2},{18... | collective-permute-start | bytes 786440 | tf_op jit(solution)/shard_map/ppermute | solution.py:307
  208.4 0.1 collective-permute-done.6
  208.4 9.9 %collective-permute-done.5 = bf16[16,8,1024]{2,1,0:T(8,128)(2,1)S(1)} collective-permute-done((bf16[16,8,1024]{2,1,0:T(8,128)(2,1)S(1)}, bf16[16,8,1024]{2,1,0:T(8,128)(2,1)S(1)}, u32[]{:S(2)}, u32[]{:S(2)}) %collective-permute-start.5) | collective-permute-done | bytes 262176 | tf_op jit(solution)/shard_map/ppermute | solution.py:307
  218.3 1.5 collective-permute-done.4
  219.9 0.2 fusion.17
  220.0 3.1 %collective-permute-start.7 = (bf16[4,16,8,1024]{3,2,1,0:T(8,128)(2,1)S(1)}, bf16[4,16,8,1024]{3,2,1,0:T(8,128)(2,1)S(1)}, u32[]{:S(2)}, u32[]{:S(2)}) collective-permute-start(bf16[4,16,8,1024]{3,2,1,0:T(8,128)(2,1)S(1)} %get-tuple-element.37), channel_id=1, source_target_pairs={{4,0},{0,4},{5,1},{1,5},{6,2},{2,6},{7,3},{3,7},{12,8},{8,12},{13,... | collective-permute-start | bytes 3145736 | tf_op jit(solution)/shard_map/ppermute | solution.py:307
  223.2 0.2 select_reduce_fusion.1
  223.4 2.0 collective-permute-done.7
  225.4 0.2 pad_maximum_fusion
  225.6 1.6 gather_fusion.2
  227.2 1.3 all-to-all-done.4
  228.5 0.1 copy.12
  228.6 1.0 reshape.303
  (8 shorter events, 0.1 us)
Async XLA Ops:
  0.6 19.5 %copy-start = (bf16[1,56,8,1024]{3,2,1,0:T(8,128)(2,1)S(1)}, bf16[1,56,8,1024]{3,2,1,0:T(8,128)(2,1)}, u32[]{:S(2)}) copy-start(bf16[1,56,8,1024]{3,2,1,0:T(8,128)(2,1)} %param.5) | copy-start | bytes 2752516
  0.6 1.3 copy-start.1
  2.7 17.3 %all-to-all-start = ((f32[32,1,128]{2,1,0:T(1,128)}), f32[32,1,128]{2,1,0:T(1,128)S(1)}, u32[]{:S(2)}, u32[]{:S(2)}) async-start(f32[32,1,128]{2,1,0:T(1,128)} %get-tuple-element.17), calls=%async_computation | async-start | bytes 32768 | tf_op jit(solution)/shard_map/all_to_all | solution.py:302
  21.7 25.3 %collective-permute-start = (bf16[64,8,1024]{2,1,0:T(8,128)(2,1)}, bf16[64,8,1024]{2,1,0:T(8,128)(2,1)}, u32[]{:S(2)}, u32[]{:S(2)}) collective-permute-start(bf16[64,8,1024]{2,1,0:T(8,128)(2,1)} %gather_fusion.1), channel_id=1, source_target_pairs={{4,0},{0,4},{5,1},{1,5},{6,2},{2,6},{7,3},{3,7},{12,8},{8,12},{13,... | collective-permute-start | bytes 3145736 | tf_op jit(solution)/shard_map/ppermute | solution.py:307
  24.3 39.1 %collective-permute-start.2 = (f32[256,512]{1,0:T(8,128)S(1)}, f32[256,512]{1,0:T(8,128)}, u32[]{:S(2)}, u32[]{:S(2)}) collective-permute-start(f32[256,512]{1,0:T(8,128)S(1)} %get-tuple-element.23), channel_id=1, source_target_pairs={{2,0},{3,1},{0,2},{1,3},{6,4},{7,5},{4,6},{5,7},{10,8},{11,9},{8,1... | collective-permute-start | bytes 1572872 | tf_op jit(solution)/shard_map/ppermute | solution.py:307
  27.2 36.2 %collective-permute-start.1 = (f32[256,512]{1,0:T(8,128)S(1)}, f32[256,512]{1,0:T(8,128)}, u32[]{:S(2)}, u32[]{:S(2)}) collective-permute-start(f32[256,512]{1,0:T(8,128)S(1)} %get-tuple-element.23), channel_id=1, source_target_pairs={{1,0},{2,1},{3,2},{0,3},{5,4},{6,5},{7,6},{4,7},{9,8},{10,9},{11,1... | collective-permute-start | bytes 1572872 | tf_op jit(solution)/shard_map/ppermute | solution.py:307
  31.4 24.3 %all-to-all-start.1 = ((f32[16,1,128]{2,1,0:T(1,128)}), f32[16,1,128]{2,1,0:T(1,128)S(1)}, u32[]{:S(2)}, u32[]{:S(2)}) async-start(f32[16,1,128]{2,1,0:T(1,128)} %broadcast_in_dim.72), calls=%async_computation.1 | async-start | bytes 16384 | tf_op jit(solution)/shard_map/all_to_all | solution.py:302
  44.5 18.9 %collective-permute-start.3 = (f32[256,512]{1,0:T(8,128)S(1)}, f32[256,512]{1,0:T(8,128)}, u32[]{:S(2)}, u32[]{:S(2)}) collective-permute-start(f32[256,512]{1,0:T(8,128)S(1)} %get-tuple-element.24), channel_id=1, source_target_pairs={{3,0},{0,1},{1,2},{2,3},{7,4},{4,5},{5,6},{6,7},{11,8},{8,9},{9,10... | collective-permute-start | bytes 1572872 | tf_op jit(solution)/shard_map/ppermute | solution.py:307
  47.0 15.7 %copy-start.3 = (s32[128,1]{0,1:T(1,128)S(1)}, s32[128,1]{0,1:T(1,128)}, u32[]{:S(2)}) copy-start(s32[128,1]{0,1:T(1,128)} %param.6) | copy-start | bytes 1540
  55.7 7.7 %copy-start.2 = (f32[16,1,128]{2,1,0:T(1,128)}, f32[16,1,128]{2,1,0:T(1,128)S(1)}, u32[]{:S(2)}) copy-start(f32[16,1,128]{2,1,0:T(1,128)S(1)} %all-to-all-done.1) | copy-start | bytes 24580
  55.7 57.8 %all-to-all-start.2 = ((bf16[64,8,1024]{2,1,0:T(8,128)(2,1)}), bf16[64,8,1024]{2,1,0:T(8,128)(2,1)S(1)}, u32[]{:S(2)}, u32[]{:S(2)}) async-start(bf16[64,8,1024]{2,1,0:T(8,128)(2,1)} %add_convert_fusion), calls=%async_computation.2 | async-start | bytes 2097152 | tf_op jit(solution)/shard_map/all_to_all | solution.py:302
  66.4 66.1 %copy-start.4 = (s32[128,1]{0,1:T(1,128)S(1)}, s32[128,1]{0,1:T(1,128)}, u32[]{:S(2)}) copy-start(s32[128,1]{0,1:T(1,128)} %param.7) | copy-start | bytes 1540
  113.7 62.4 %all-to-all-start.3 = ((bf16[128,16,128]{2,1,0:T(8,128)(2,1)}), bf16[128,16,128]{2,1,0:T(8,128)(2,1)S(1)}, u32[]{:S(2)}, u32[]{:S(2)}) async-start(bf16[128,16,128]{2,1,0:T(8,128)(2,1)} %get-tuple-element.27), calls=%async_computation.3 | async-start | bytes 1048576 | tf_op jit(solution)/shard_map/all_to_all | solution.py:302
  177.7 50.8 %all-to-all-start.4 = ((bf16[128,16,128]{2,1,0:T(8,128)(2,1)}), bf16[128,16,128]{2,1,0:T(8,128)(2,1)S(1)}, u32[]{:S(2)}, u32[]{:S(2)}) async-start(bf16[128,16,128]{2,1,0:T(8,128)(2,1)} %shard_map.61), calls=%async_computation.4 | async-start | bytes 1048576 | tf_op jit(solution)/shard_map/all_to_all | solution.py:302
  197.7 10.8 %collective-permute-start.6 = (bf16[16,8,1024]{2,1,0:T(8,128)(2,1)S(1)}, bf16[16,8,1024]{2,1,0:T(8,128)(2,1)S(1)}, u32[]{:S(2)}, u32[]{:S(2)}) collective-permute-start(bf16[16,8,1024]{2,1,0:T(8,128)(2,1)S(1)} %bitcast.73), channel_id=1, source_target_pairs={{24,0},{0,8},{8,16},{16,24},{25,1},{1,9},{9,17},{17,25},{26,2},{2,... | collective-permute-start | bytes 786440 | tf_op jit(solution)/shard_map/ppermute | solution.py:307
  201.0 17.4 %collective-permute-start.5 = (bf16[16,8,1024]{2,1,0:T(8,128)(2,1)S(1)}, bf16[16,8,1024]{2,1,0:T(8,128)(2,1)S(1)}, u32[]{:S(2)}, u32[]{:S(2)}) collective-permute-start(bf16[16,8,1024]{2,1,0:T(8,128)(2,1)S(1)} %bitcast.74), channel_id=1, source_target_pairs={{16,0},{24,8},{0,16},{8,24},{17,1},{25,9},{1,17},{9,25},{18,2},{26... | collective-permute-start | bytes 786440 | tf_op jit(solution)/shard_map/ppermute | solution.py:307
  205.3 14.6 %collective-permute-start.4 = (bf16[16,8,1024]{2,1,0:T(8,128)(2,1)S(1)}, bf16[16,8,1024]{2,1,0:T(8,128)(2,1)S(1)}, u32[]{:S(2)}, u32[]{:S(2)}) collective-permute-start(bf16[16,8,1024]{2,1,0:T(8,128)(2,1)S(1)} %bitcast.75), channel_id=1, source_target_pairs={{8,0},{16,8},{24,16},{0,24},{9,1},{17,9},{25,17},{1,25},{10,2},{18... | collective-permute-start | bytes 786440 | tf_op jit(solution)/shard_map/ppermute | solution.py:307
  220.0 5.4 %collective-permute-start.7 = (bf16[4,16,8,1024]{3,2,1,0:T(8,128)(2,1)S(1)}, bf16[4,16,8,1024]{3,2,1,0:T(8,128)(2,1)S(1)}, u32[]{:S(2)}, u32[]{:S(2)}) collective-permute-start(bf16[4,16,8,1024]{3,2,1,0:T(8,128)(2,1)S(1)} %get-tuple-element.37), channel_id=1, source_target_pairs={{4,0},{0,4},{5,1},{1,5},{6,2},{2,6},{7,3},{3,7},{12,8},{8,12},{13,... | collective-permute-start | bytes 3145736 | tf_op jit(solution)/shard_map/ppermute | solution.py:307

commit v8 on v7

--- a/solution.py
+++ b/solution.py
@@ -178,11 +178,9 @@
             m_ref[at, :] = rows
             m_ref[at, at] = d_ref[...]
             right_ref[...] = stacked(m_ref[at, :], RIGHT, 0)
-            for i in range(count):
-
-                @pl.when(i != k)
-                def _():
-                    m_ref[block(i), :] = m_ref[block(i), :] - dot(left_ref[block(i), :], right_ref[...])
+            left_ref[at, :] = jnp.zeros((wide, 3 * wide), jnp.bfloat16)
+            for j in range(count):
+                m_ref[:, block(j)] = m_ref[:, block(j)] - dot(left_ref[...], right_ref[:, block(j)])
 
         for j in range(count):
             band = (-m_ref[block(0), block(j)]).astype(jnp.bfloat16)

time: 232 us -> 232 us (level)
  Pallas kernels: 5.34 us -> 54.2 us
  waiting for transfers between devices: 72 us -> 24.9 us
  starting transfers between devices: 93.3 us -> 90.9 us
    pallas_call x1, Pallas kernels: 3.03 us -> 51.9 us  [invert(): pl.pallas_call(invert_kernel, out_shape=(jax.ShapeDtypeStruct(pieces, jnp...]
    all_to_all x5, waiting for transfers between devices: 58.5 us -> 11.4 us  [exchange(): return lax.all_to_all(pieces, axes, split_axis=0, concat_axis=0, tiled=True)]
    all_to_all x5, starting transfers between devices: 68.6 us -> 66.1 us  [exchange(): return lax.all_to_all(pieces, axes, split_axis=0, concat_axis=0, tiled=True)]
  transfers between devices with their start and end apart: 13 -> 13, of which waited for: 8 -> 7; matrix products, arithmetic and copies ran while one was open for 6% -> 6% of each run, Pallas kernels for 1% -> 23%
where the time goes in v8:
time: 232 us; the launch traced here: 229 us
  starting transfers between devices  90.9 us (39%)
  Pallas kernels  54.2 us (23%)
  blocking collectives  40.8 us (18%)
  waiting for transfers between devices  24.9 us (11%)
  other arithmetic  7.92 us (3%)
  local copies, waits for them, and re-layouts  7.34 us (3%)
    all_to_all x5, starting transfers between devices, exchange(): return lax.all_to_all(pieces, axes, split_axis=0, concat_axis=0, tiled=True)  66.1 us
    pallas_call x1, Pallas kernels, invert(): pl.pallas_call(invert_kernel, out_shape=(jax.ShapeDtypeStruct(pieces, jnp...  51.9 us
    all_gather x1, blocking collectives, local(): held = lax.all_gather(held, 'z', axis=0, tiled=False)  40.8 us
    ppermute x8, starting transfers between devices, from_ahead(): lax.ppermute(value, axis, [((i + step) % count, i) for i in range(count)])  24.8 us
    ppermute x8, waiting for transfers between devices, from_ahead(): lax.ppermute(value, axis, [((i + step) % count, i) for i in range(count)])  13.5 us
    all_to_all x5, waiting for transfers between devices, exchange(): return lax.all_to_all(pieces, axes, split_axis=0, concat_axis=0, tiled=True)  11.4 us
  transfers between devices with their start and end apart: 13, of which 7 were waited for; matrix products, arithmetic and copies ran while one was open for 6% of the time, Pallas kernels for 23%

profile of v8, /device:TPU:1, one launch (start us, length us, event | category | flops | bytes accessed | tf_op | source)
XLA Modules:
  0.0 228.9 jit_solution(8830689308081105086)
XLA Ops:
  0.6 0.0 copy-start
  0.6 0.0 copy-start.1
  0.7 1.3 copy-done.1
  2.0 0.8 shard_map.59
  2.7 10.4 %all-to-all-start = ((f32[32,1,128]{2,1,0:T(1,128)}), f32[32,1,128]{2,1,0:T(1,128)S(1)}, u32[]{:S(2)}, u32[]{:S(2)}) async-start(f32[32,1,128]{2,1,0:T(1,128)} %get-tuple-element.17), calls=%async_computation | async-start | bytes 32768 | tf_op jit(solution)/shard_map/all_to_all | solution.py:300
  13.1 0.7 compare_reduce_fusion
  13.8 0.7 remainder_reduce_fusion
  14.5 0.7 bitcast_select_fusion
  15.2 0.1 iota_compare_fusion
  15.3 0.1 ne.179
  15.4 0.1 rem.122
  15.6 0.1 div.52
  15.7 0.2 fusion.3
  15.9 4.1 %all-to-all-done = f32[32,1,128]{2,1,0:T(1,128)S(1)} async-done(((f32[32,1,128]{2,1,0:T(1,128)}), f32[32,1,128]{2,1,0:T(1,128)S(1)}, u32[]{:S(2)}, u32[]{:S(2)}) %all-to-all-start) | async-done | bytes 16416 | tf_op jit(solution)/shard_map/all_to_all | solution.py:300
  20.0 0.1 fusion.5
  20.1 0.0 copy-done
  20.1 1.6 gather_fusion.1
  21.7 2.5 %collective-permute-start = (bf16[64,8,1024]{2,1,0:T(8,128)(2,1)}, bf16[64,8,1024]{2,1,0:T(8,128)(2,1)}, u32[]{:S(2)}, u32[]{:S(2)}) collective-permute-start(bf16[64,8,1024]{2,1,0:T(8,128)(2,1)} %gather_fusion.1), channel_id=1, source_target_pairs={{4,0},{0,4},{5,1},{1,5},{6,2},{2,6},{7,3},{3,7},{12,8},{8,12},{13,... | collective-permute-start | bytes 3145736 | tf_op jit(solution)/shard_map/ppermute | solution.py:305
  24.3 2.8 %collective-permute-start.2 = (f32[256,512]{1,0:T(8,128)S(1)}, f32[256,512]{1,0:T(8,128)}, u32[]{:S(2)}, u32[]{:S(2)}) collective-permute-start(f32[256,512]{1,0:T(8,128)S(1)} %get-tuple-element.23), channel_id=1, source_target_pairs={{2,0},{3,1},{0,2},{1,3},{6,4},{7,5},{4,6},{5,7},{10,8},{11,9},{8,1... | collective-permute-start | bytes 1572872 | tf_op jit(solution)/shard_map/ppermute | solution.py:305
  27.2 3.7 %collective-permute-start.1 = (f32[256,512]{1,0:T(8,128)S(1)}, f32[256,512]{1,0:T(8,128)}, u32[]{:S(2)}, u32[]{:S(2)}) collective-permute-start(f32[256,512]{1,0:T(8,128)S(1)} %get-tuple-element.23), channel_id=1, source_target_pairs={{1,0},{2,1},{3,2},{0,3},{5,4},{6,5},{7,6},{4,7},{9,8},{10,9},{11,1... | collective-permute-start | bytes 1572872 | tf_op jit(solution)/shard_map/ppermute | solution.py:305
  30.8 0.6 broadcast_in_dim.72
  31.4 13.0 %all-to-all-start.1 = ((f32[16,1,128]{2,1,0:T(1,128)}), f32[16,1,128]{2,1,0:T(1,128)S(1)}, u32[]{:S(2)}, u32[]{:S(2)}) async-start(f32[16,1,128]{2,1,0:T(1,128)} %broadcast_in_dim.72), calls=%async_computation.1 | async-start | bytes 16384 | tf_op jit(solution)/shard_map/all_to_all | solution.py:300
  44.5 1.9 collective-permute-start.3
  46.4 0.6 gather_fusion
  47.0 0.0 copy-start.3
  47.0 0.0 collective-permute-done
  47.0 2.6 %add_convert_fusion = bf16[64,8,1024]{2,1,0:T(8,128)(2,1)} fusion(bf16[64,8,1024]{2,1,0:T(8,128)(2,1)} %collective-permute-done, bf16[64,8,1024]{2,1,0:T(8,128)(2,1)S(1)} %gather_fusion), kind=kLoop, calls=%fused_computation.4 | loop fusion | flops 2097152 | bytes 3145728 | tf_op jit(solution)/shard_map/convert_element_type | solution.py:347
  49.7 6.0 %all-to-all-done.1 = f32[16,1,128]{2,1,0:T(1,128)S(1)} async-done(((f32[16,1,128]{2,1,0:T(1,128)}), f32[16,1,128]{2,1,0:T(1,128)S(1)}, u32[]{:S(2)}, u32[]{:S(2)}) %all-to-all-start.1) | async-done | bytes 8224 | tf_op jit(solution)/shard_map/all_to_all | solution.py:300
  55.7 7.0 %all-to-all-start.2 = ((bf16[64,8,1024]{2,1,0:T(8,128)(2,1)}), bf16[64,8,1024]{2,1,0:T(8,128)(2,1)S(1)}, u32[]{:S(2)}, u32[]{:S(2)}) async-start(bf16[64,8,1024]{2,1,0:T(8,128)(2,1)} %add_convert_fusion), calls=%async_computation.2 | async-start | bytes 2097152 | tf_op jit(solution)/shard_map/all_to_all | solution.py:300
  62.7 0.0 copy-done.3
  62.7 0.6 pad_add_fusion.slots_ref
  63.4 0.0 collective-permute-done.3.three_hbm
  63.4 0.0 collective-permute-done.2.two_hbm
  63.4 0.0 collective-permute-done.1.one_hbm
  63.4 0.0 copy-done.2
  63.4 51.9 %shard_map.60 = (bf16[128,16,128]{2,1,0:T(8,128)(2,1)}, bf16[1024,1024]{1,0:T(8,128)(2,1)}) custom-call(s32[130]{0:T(256)} %pad_add_fusion.slots_ref, f32[16,128]{1,0:T(8,128)} %bitcast.82, f32[256,1024]{1,0:T(8,128)} %bitcast.69, f32[256,512]{1,0:T(8,128)} %collective-permute-done.1.one_hbm, f32[256,512]{1,0:T(8,128)} %collective-permute-done.2.two_hbm, ...), custom_call_target="tpu_custom_call" | custom-call | flops 38654705664 | bytes 6291456 | tf_op jit(solution)/shard_map/pallas_call | solution.py:213
  115.2 0.0 copy-start.4
  115.2 0.0 all-to-all-done.2
  115.3 0.2 reduce_sum.43
  115.4 15.7 %all-to-all-start.3 = ((bf16[128,16,128]{2,1,0:T(8,128)(2,1)}), bf16[128,16,128]{2,1,0:T(8,128)(2,1)S(1)}, u32[]{:S(2)}, u32[]{:S(2)}) async-start(bf16[128,16,128]{2,1,0:T(8,128)(2,1)} %get-tuple-element.27), calls=%async_computation.3 | async-start | bytes 1048576 | tf_op jit(solution)/shard_map/all_to_all | solution.py:300
  131.1 0.6 fusion.10
  131.8 0.0 copy-done.4
  131.8 0.2 select_reduce_fusion
  131.9 0.7 compare_select_fusion.9.index_ref
  132.6 2.0 convolution_convert_fusion
  134.6 40.8 %all-gather = bf16[128,1024]{1,0:T(8,128)(2,1)S(1)} all-gather(bf16[8,1024]{1,0:T(8,128)(2,1)S(1)} %convolution_convert_fusion), channel_id=2, replica_groups=mesh['z'=16,'x'=4,'c'=2,'mp'=4] {'z'}, dimensions={0}, use_global_device_ids=true | all-gather | bytes 278528 | tf_op jit(solution)/shard_map/all_gather | solution.py:360
  175.3 0.0 all-to-all-done.3.src_ref
  175.3 1.6 shard_map.61
  176.9 20.0 %all-to-all-start.4 = ((bf16[128,16,128]{2,1,0:T(8,128)(2,1)}), bf16[128,16,128]{2,1,0:T(8,128)(2,1)S(1)}, u32[]{:S(2)}, u32[]{:S(2)}) async-start(bf16[128,16,128]{2,1,0:T(8,128)(2,1)} %shard_map.61), calls=%async_computation.4 | async-start | bytes 1048576 | tf_op jit(solution)/shard_map/all_to_all | solution.py:300
  196.9 3.3 %collective-permute-start.6 = (bf16[16,8,1024]{2,1,0:T(8,128)(2,1)S(1)}, bf16[16,8,1024]{2,1,0:T(8,128)(2,1)S(1)}, u32[]{:S(2)}, u32[]{:S(2)}) collective-permute-start(bf16[16,8,1024]{2,1,0:T(8,128)(2,1)S(1)} %bitcast.73), channel_id=1, source_target_pairs={{24,0},{0,8},{8,16},{16,24},{25,1},{1,9},{9,17},{17,25},{26,2},{2,... | collective-permute-start | bytes 786440 | tf_op jit(solution)/shard_map/ppermute | solution.py:305
  200.2 4.3 %collective-permute-start.5 = (bf16[16,8,1024]{2,1,0:T(8,128)(2,1)S(1)}, bf16[16,8,1024]{2,1,0:T(8,128)(2,1)S(1)}, u32[]{:S(2)}, u32[]{:S(2)}) collective-permute-start(bf16[16,8,1024]{2,1,0:T(8,128)(2,1)S(1)} %bitcast.74), channel_id=1, source_target_pairs={{16,0},{24,8},{0,16},{8,24},{17,1},{25,9},{1,17},{9,25},{18,2},{26... | collective-permute-start | bytes 786440 | tf_op jit(solution)/shard_map/ppermute | solution.py:305
  204.5 3.1 %collective-permute-start.4 = (bf16[16,8,1024]{2,1,0:T(8,128)(2,1)S(1)}, bf16[16,8,1024]{2,1,0:T(8,128)(2,1)S(1)}, u32[]{:S(2)}, u32[]{:S(2)}) collective-permute-start(bf16[16,8,1024]{2,1,0:T(8,128)(2,1)S(1)} %bitcast.75), channel_id=1, source_target_pairs={{8,0},{16,8},{24,16},{0,24},{9,1},{17,9},{25,17},{1,25},{10,2},{18... | collective-permute-start | bytes 786440 | tf_op jit(solution)/shard_map/ppermute | solution.py:305
  207.6 0.1 collective-permute-done.6
  207.7 9.9 %collective-permute-done.5 = bf16[16,8,1024]{2,1,0:T(8,128)(2,1)S(1)} collective-permute-done((bf16[16,8,1024]{2,1,0:T(8,128)(2,1)S(1)}, bf16[16,8,1024]{2,1,0:T(8,128)(2,1)S(1)}, u32[]{:S(2)}, u32[]{:S(2)}) %collective-permute-start.5) | collective-permute-done | bytes 262176 | tf_op jit(solution)/shard_map/ppermute | solution.py:305
  217.5 1.5 collective-permute-done.4
  219.1 0.2 fusion.17
  219.3 3.1 %collective-permute-start.7 = (bf16[4,16,8,1024]{3,2,1,0:T(8,128)(2,1)S(1)}, bf16[4,16,8,1024]{3,2,1,0:T(8,128)(2,1)S(1)}, u32[]{:S(2)}, u32[]{:S(2)}) collective-permute-start(bf16[4,16,8,1024]{3,2,1,0:T(8,128)(2,1)S(1)} %get-tuple-element.37), channel_id=1, source_target_pairs={{4,0},{0,4},{5,1},{1,5},{6,2},{2,6},{7,3},{3,7},{12,8},{8,12},{13,... | collective-permute-start | bytes 3145736 | tf_op jit(solution)/shard_map/ppermute | solution.py:305
  222.4 0.2 select_reduce_fusion.1
  222.7 2.0 collective-permute-done.7
  224.7 0.2 pad_maximum_fusion
  224.9 1.6 gather_fusion.2
  226.5 1.3 all-to-all-done.4
  227.7 0.1 copy.12
  227.9 1.0 reshape.303
  (8 shorter events, 0.1 us)
Async XLA Ops:
  0.6 19.5 %copy-start = (bf16[1,56,8,1024]{3,2,1,0:T(8,128)(2,1)S(1)}, bf16[1,56,8,1024]{3,2,1,0:T(8,128)(2,1)}, u32[]{:S(2)}) copy-start(bf16[1,56,8,1024]{3,2,1,0:T(8,128)(2,1)} %param.5) | copy-start | bytes 2752516
  0.6 1.3 copy-start.1
  2.7 17.3 %all-to-all-start = ((f32[32,1,128]{2,1,0:T(1,128)}), f32[32,1,128]{2,1,0:T(1,128)S(1)}, u32[]{:S(2)}, u32[]{:S(2)}) async-start(f32[32,1,128]{2,1,0:T(1,128)} %get-tuple-element.17), calls=%async_computation | async-start | bytes 32768 | tf_op jit(solution)/shard_map/all_to_all | solution.py:300
  21.7 25.3 %collective-permute-start = (bf16[64,8,1024]{2,1,0:T(8,128)(2,1)}, bf16[64,8,1024]{2,1,0:T(8,128)(2,1)}, u32[]{:S(2)}, u32[]{:S(2)}) collective-permute-start(bf16[64,8,1024]{2,1,0:T(8,128)(2,1)} %gather_fusion.1), channel_id=1, source_target_pairs={{4,0},{0,4},{5,1},{1,5},{6,2},{2,6},{7,3},{3,7},{12,8},{8,12},{13,... | collective-permute-start | bytes 3145736 | tf_op jit(solution)/shard_map/ppermute | solution.py:305
  24.3 39.1 %collective-permute-start.2 = (f32[256,512]{1,0:T(8,128)S(1)}, f32[256,512]{1,0:T(8,128)}, u32[]{:S(2)}, u32[]{:S(2)}) collective-permute-start(f32[256,512]{1,0:T(8,128)S(1)} %get-tuple-element.23), channel_id=1, source_target_pairs={{2,0},{3,1},{0,2},{1,3},{6,4},{7,5},{4,6},{5,7},{10,8},{11,9},{8,1... | collective-permute-start | bytes 1572872 | tf_op jit(solution)/shard_map/ppermute | solution.py:305
  27.2 36.2 %collective-permute-start.1 = (f32[256,512]{1,0:T(8,128)S(1)}, f32[256,512]{1,0:T(8,128)}, u32[]{:S(2)}, u32[]{:S(2)}) collective-permute-start(f32[256,512]{1,0:T(8,128)S(1)} %get-tuple-element.23), channel_id=1, source_target_pairs={{1,0},{2,1},{3,2},{0,3},{5,4},{6,5},{7,6},{4,7},{9,8},{10,9},{11,1... | collective-permute-start | bytes 1572872 | tf_op jit(solution)/shard_map/ppermute | solution.py:305
  31.4 24.3 %all-to-all-start.1 = ((f32[16,1,128]{2,1,0:T(1,128)}), f32[16,1,128]{2,1,0:T(1,128)S(1)}, u32[]{:S(2)}, u32[]{:S(2)}) async-start(f32[16,1,128]{2,1,0:T(1,128)} %broadcast_in_dim.72), calls=%async_computation.1 | async-start | bytes 16384 | tf_op jit(solution)/shard_map/all_to_all | solution.py:300
  44.5 18.9 %collective-permute-start.3 = (f32[256,512]{1,0:T(8,128)S(1)}, f32[256,512]{1,0:T(8,128)}, u32[]{:S(2)}, u32[]{:S(2)}) collective-permute-start(f32[256,512]{1,0:T(8,128)S(1)} %get-tuple-element.24), channel_id=1, source_target_pairs={{3,0},{0,1},{1,2},{2,3},{7,4},{4,5},{5,6},{6,7},{11,8},{8,9},{9,10... | collective-permute-start | bytes 1572872 | tf_op jit(solution)/shard_map/ppermute | solution.py:305
  47.0 15.7 %copy-start.3 = (s32[128,1]{0,1:T(1,128)S(1)}, s32[128,1]{0,1:T(1,128)}, u32[]{:S(2)}) copy-start(s32[128,1]{0,1:T(1,128)} %param.6) | copy-start | bytes 1540
  55.7 7.7 %copy-start.2 = (f32[16,1,128]{2,1,0:T(1,128)}, f32[16,1,128]{2,1,0:T(1,128)S(1)}, u32[]{:S(2)}) copy-start(f32[16,1,128]{2,1,0:T(1,128)S(1)} %all-to-all-done.1) | copy-start | bytes 24580
  55.7 59.5 %all-to-all-start.2 = ((bf16[64,8,1024]{2,1,0:T(8,128)(2,1)}), bf16[64,8,1024]{2,1,0:T(8,128)(2,1)S(1)}, u32[]{:S(2)}, u32[]{:S(2)}) async-start(bf16[64,8,1024]{2,1,0:T(8,128)(2,1)} %add_convert_fusion), calls=%async_computation.2 | async-start | bytes 2097152 | tf_op jit(solution)/shard_map/all_to_all | solution.py:300
  115.2 16.5 %copy-start.4 = (s32[128,1]{0,1:T(1,128)S(1)}, s32[128,1]{0,1:T(1,128)}, u32[]{:S(2)}) copy-start(s32[128,1]{0,1:T(1,128)} %param.7) | copy-start | bytes 1540
  115.4 59.9 %all-to-all-start.3 = ((bf16[128,16,128]{2,1,0:T(8,128)(2,1)}), bf16[128,16,128]{2,1,0:T(8,128)(2,1)S(1)}, u32[]{:S(2)}, u32[]{:S(2)}) async-start(bf16[128,16,128]{2,1,0:T(8,128)(2,1)} %get-tuple-element.27), calls=%async_computation.3 | async-start | bytes 1048576 | tf_op jit(solution)/shard_map/all_to_all | solution.py:300
  176.9 50.8 %all-to-all-start.4 = ((bf16[128,16,128]{2,1,0:T(8,128)(2,1)}), bf16[128,16,128]{2,1,0:T(8,128)(2,1)S(1)}, u32[]{:S(2)}, u32[]{:S(2)}) async-start(bf16[128,16,128]{2,1,0:T(8,128)(2,1)} %shard_map.61), calls=%async_computation.4 | async-start | bytes 1048576 | tf_op jit(solution)/shard_map/all_to_all | solution.py:300
  196.9 10.8 %collective-permute-start.6 = (bf16[16,8,1024]{2,1,0:T(8,128)(2,1)S(1)}, bf16[16,8,1024]{2,1,0:T(8,128)(2,1)S(1)}, u32[]{:S(2)}, u32[]{:S(2)}) collective-permute-start(bf16[16,8,1024]{2,1,0:T(8,128)(2,1)S(1)} %bitcast.73), channel_id=1, source_target_pairs={{24,0},{0,8},{8,16},{16,24},{25,1},{1,9},{9,17},{17,25},{26,2},{2,... | collective-permute-start | bytes 786440 | tf_op jit(solution)/shard_map/ppermute | solution.py:305
  200.2 17.4 %collective-permute-start.5 = (bf16[16,8,1024]{2,1,0:T(8,128)(2,1)S(1)}, bf16[16,8,1024]{2,1,0:T(8,128)(2,1)S(1)}, u32[]{:S(2)}, u32[]{:S(2)}) collective-permute-start(bf16[16,8,1024]{2,1,0:T(8,128)(2,1)S(1)} %bitcast.74), channel_id=1, source_target_pairs={{16,0},{24,8},{0,16},{8,24},{17,1},{25,9},{1,17},{9,25},{18,2},{26... | collective-permute-start | bytes 786440 | tf_op jit(solution)/shard_map/ppermute | solution.py:305
  204.5 14.6 %collective-permute-start.4 = (bf16[16,8,1024]{2,1,0:T(8,128)(2,1)S(1)}, bf16[16,8,1024]{2,1,0:T(8,128)(2,1)S(1)}, u32[]{:S(2)}, u32[]{:S(2)}) collective-permute-start(bf16[16,8,1024]{2,1,0:T(8,128)(2,1)S(1)} %bitcast.75), channel_id=1, source_target_pairs={{8,0},{16,8},{24,16},{0,24},{9,1},{17,9},{25,17},{1,25},{10,2},{18... | collective-permute-start | bytes 786440 | tf_op jit(solution)/shard_map/ppermute | solution.py:305
  219.3 5.4 %collective-permute-start.7 = (bf16[4,16,8,1024]{3,2,1,0:T(8,128)(2,1)S(1)}, bf16[4,16,8,1024]{3,2,1,0:T(8,128)(2,1)S(1)}, u32[]{:S(2)}, u32[]{:S(2)}) collective-permute-start(bf16[4,16,8,1024]{3,2,1,0:T(8,128)(2,1)S(1)} %get-tuple-element.37), channel_id=1, source_target_pairs={{4,0},{0,4},{5,1},{1,5},{6,2},{2,6},{7,3},{3,7},{12,8},{8,12},{13,... | collective-permute-start | bytes 3145736 | tf_op jit(solution)/shard_map/ppermute | solution.py:305

commit v9 on v8

--- a/solution.py
+++ b/solution.py
@@ -11,7 +11,7 @@
 X_COUNT, CORES = 4, 2
 DP = ("z", "x", "c")
 
-BASE = 32
+BASE = 64
 SUB = 8
 ROWS, LANES = 16, 128
 

time: 232 us -> 238 us (1.026)
  Pallas kernels: 54.2 us -> 5.52 us
  waiting for transfers between devices: 24.9 us -> 71.8 us
  starting transfers between devices: 90.9 us -> 98.7 us
    pallas_call x1, Pallas kernels: 51.9 us -> 3.21 us  [invert(): pl.pallas_call(invert_kernel, out_shape=(jax.ShapeDtypeStruct(pieces, jnp...]
    all_to_all x5, waiting for transfers between devices: 11.4 us -> 58.3 us  [exchange(): return lax.all_to_all(pieces, axes, split_axis=0, concat_axis=0, tiled=True)]
    all_to_all x5, starting transfers between devices: 66.1 us -> 73.9 us  [exchange(): return lax.all_to_all(pieces, axes, split_axis=0, concat_axis=0, tiled=True)]
  transfers between devices with their start and end apart: 13 -> 13, of which waited for: 7 -> 8; matrix products, arithmetic and copies ran while one was open for 6% -> 5% of each run, Pallas kernels for 23% -> 1%
where the time goes in v9:
time: 238 us; the launch traced here: 235 us
  starting transfers between devices  98.7 us (41%)
  waiting for transfers between devices  71.8 us (30%)
  blocking collectives  40.8 us (17%)
  other arithmetic  7.92 us (3%)
  local copies, waits for them, and re-layouts  7.34 us (3%)
  Pallas kernels  5.52 us (2%)
    all_to_all x5, starting transfers between devices, exchange(): return lax.all_to_all(pieces, axes, split_axis=0, concat_axis=0, tiled=True)  73.9 us
    all_to_all x5, waiting for transfers between devices, exchange(): return lax.all_to_all(pieces, axes, split_axis=0, concat_axis=0, tiled=True)  58.3 us
    all_gather x1, blocking collectives, local(): held = lax.all_gather(held, 'z', axis=0, tiled=False)  40.8 us
    ppermute x8, starting transfers between devices, from_ahead(): lax.ppermute(value, axis, [((i + step) % count, i) for i in range(count)])  24.8 us
    ppermute x8, waiting for transfers between devices, from_ahead(): lax.ppermute(value, axis, [((i + step) % count, i) for i in range(count)])  13.5 us
  transfers between devices with their start and end apart: 13, of which 8 were waited for; matrix products, arithmetic and copies ran while one was open for 5% of the time, Pallas kernels for 1%

profile of v9, /device:TPU:1, one launch (start us, length us, event | category | flops | bytes accessed | tf_op | source)
XLA Modules:
  0.0 235.0 jit_solution(7193068930774512909)
XLA Ops:
  0.6 0.0 copy-start
  0.6 0.0 copy-start.1
  0.7 1.3 copy-done.1
  2.0 0.8 shard_map.59
  2.7 10.4 %all-to-all-start = ((f32[32,1,128]{2,1,0:T(1,128)}), f32[32,1,128]{2,1,0:T(1,128)S(1)}, u32[]{:S(2)}, u32[]{:S(2)}) async-start(f32[32,1,128]{2,1,0:T(1,128)} %get-tuple-element.17), calls=%async_computation | async-start | bytes 32768 | tf_op jit(solution)/shard_map/all_to_all | solution.py:300
  13.1 0.7 compare_reduce_fusion
  13.8 0.7 remainder_reduce_fusion
  14.5 0.7 bitcast_select_fusion
  15.2 0.1 iota_compare_fusion
  15.3 0.1 ne.179
  15.4 0.1 rem.122
  15.6 0.1 div.52
  15.7 0.2 fusion.3
  15.9 4.1 %all-to-all-done = f32[32,1,128]{2,1,0:T(1,128)S(1)} async-done(((f32[32,1,128]{2,1,0:T(1,128)}), f32[32,1,128]{2,1,0:T(1,128)S(1)}, u32[]{:S(2)}, u32[]{:S(2)}) %all-to-all-start) | async-done | bytes 16416 | tf_op jit(solution)/shard_map/all_to_all | solution.py:300
  20.0 0.1 fusion.5
  20.1 0.0 copy-done
  20.1 1.6 gather_fusion.1
  21.7 2.5 %collective-permute-start = (bf16[64,8,1024]{2,1,0:T(8,128)(2,1)}, bf16[64,8,1024]{2,1,0:T(8,128)(2,1)}, u32[]{:S(2)}, u32[]{:S(2)}) collective-permute-start(bf16[64,8,1024]{2,1,0:T(8,128)(2,1)} %gather_fusion.1), channel_id=1, source_target_pairs={{4,0},{0,4},{5,1},{1,5},{6,2},{2,6},{7,3},{3,7},{12,8},{8,12},{13,... | collective-permute-start | bytes 3145736 | tf_op jit(solution)/shard_map/ppermute | solution.py:305
  24.3 2.8 %collective-permute-start.2 = (f32[256,512]{1,0:T(8,128)S(1)}, f32[256,512]{1,0:T(8,128)}, u32[]{:S(2)}, u32[]{:S(2)}) collective-permute-start(f32[256,512]{1,0:T(8,128)S(1)} %get-tuple-element.23), channel_id=1, source_target_pairs={{2,0},{3,1},{0,2},{1,3},{6,4},{7,5},{4,6},{5,7},{10,8},{11,9},{8,1... | collective-permute-start | bytes 1572872 | tf_op jit(solution)/shard_map/ppermute | solution.py:305
  27.2 3.7 %collective-permute-start.1 = (f32[256,512]{1,0:T(8,128)S(1)}, f32[256,512]{1,0:T(8,128)}, u32[]{:S(2)}, u32[]{:S(2)}) collective-permute-start(f32[256,512]{1,0:T(8,128)S(1)} %get-tuple-element.23), channel_id=1, source_target_pairs={{1,0},{2,1},{3,2},{0,3},{5,4},{6,5},{7,6},{4,7},{9,8},{10,9},{11,1... | collective-permute-start | bytes 1572872 | tf_op jit(solution)/shard_map/ppermute | solution.py:305
  30.8 0.6 broadcast_in_dim.72
  31.4 13.0 %all-to-all-start.1 = ((f32[16,1,128]{2,1,0:T(1,128)}), f32[16,1,128]{2,1,0:T(1,128)S(1)}, u32[]{:S(2)}, u32[]{:S(2)}) async-start(f32[16,1,128]{2,1,0:T(1,128)} %broadcast_in_dim.72), calls=%async_computation.1 | async-start | bytes 16384 | tf_op jit(solution)/shard_map/all_to_all | solution.py:300
  44.5 1.9 collective-permute-start.3
  46.4 0.6 gather_fusion
  47.0 0.0 copy-start.3
  47.0 0.0 collective-permute-done
  47.0 2.6 %add_convert_fusion = bf16[64,8,1024]{2,1,0:T(8,128)(2,1)} fusion(bf16[64,8,1024]{2,1,0:T(8,128)(2,1)} %collective-permute-done, bf16[64,8,1024]{2,1,0:T(8,128)(2,1)S(1)} %gather_fusion), kind=kLoop, calls=%fused_computation.4 | loop fusion | flops 2097152 | bytes 3145728 | tf_op jit(solution)/shard_map/convert_element_type | solution.py:347
  49.7 6.0 %all-to-all-done.1 = f32[16,1,128]{2,1,0:T(1,128)S(1)} async-done(((f32[16,1,128]{2,1,0:T(1,128)}), f32[16,1,128]{2,1,0:T(1,128)S(1)}, u32[]{:S(2)}, u32[]{:S(2)}) %all-to-all-start.1) | async-done | bytes 8224 | tf_op jit(solution)/shard_map/all_to_all | solution.py:300
  55.7 7.0 %all-to-all-start.2 = ((bf16[64,8,1024]{2,1,0:T(8,128)(2,1)}), bf16[64,8,1024]{2,1,0:T(8,128)(2,1)S(1)}, u32[]{:S(2)}, u32[]{:S(2)}) async-start(bf16[64,8,1024]{2,1,0:T(8,128)(2,1)} %add_convert_fusion), calls=%async_computation.2 | async-start | bytes 2097152 | tf_op jit(solution)/shard_map/all_to_all | solution.py:300
  62.7 0.0 copy-done.3
  62.7 0.6 pad_add_fusion.slots_ref
  63.4 0.0 collective-permute-done.3.three_hbm
  63.4 0.0 collective-permute-done.2.two_hbm
  63.4 0.0 collective-permute-done.1.one_hbm
  63.4 0.0 copy-done.2
  63.4 3.2 %shard_map.60 = (bf16[128,16,128]{2,1,0:T(8,128)(2,1)}, bf16[1024,1024]{1,0:T(8,128)(2,1)}) custom-call(s32[130]{0:T(256)} %pad_add_fusion.slots_ref, f32[16,128]{1,0:T(8,128)} %bitcast.82, f32[256,1024]{1,0:T(8,128)} %bitcast.69, f32[256,512]{1,0:T(8,128)} %collective-permute-done.1.one_hbm, f32[256,512]{1,0:T(8,128)} %collective-permute-done.2.two_hbm, ...), custom_call_target="tpu_custom_call" | custom-call | flops 38654705664 | bytes 6291456 | tf_op jit(solution)/shard_map/pallas_call | solution.py:213
  66.6 0.0 copy-start.4
  66.6 46.9 %all-to-all-done.2 = bf16[64,8,1024]{2,1,0:T(8,128)(2,1)S(1)} async-done(((bf16[64,8,1024]{2,1,0:T(8,128)(2,1)}), bf16[64,8,1024]{2,1,0:T(8,128)(2,1)S(1)}, u32[]{:S(2)}, u32[]{:S(2)}) %all-to-all-start.2) | async-done | bytes 1048608 | tf_op jit(solution)/shard_map/all_to_all | solution.py:300
  113.5 0.2 reduce_sum.43
  113.7 23.3 %all-to-all-start.3 = ((bf16[128,16,128]{2,1,0:T(8,128)(2,1)}), bf16[128,16,128]{2,1,0:T(8,128)(2,1)S(1)}, u32[]{:S(2)}, u32[]{:S(2)}) async-start(bf16[128,16,128]{2,1,0:T(8,128)(2,1)} %get-tuple-element.27), calls=%async_computation.3 | async-start | bytes 1048576 | tf_op jit(solution)/shard_map/all_to_all | solution.py:300
  137.0 0.6 fusion.10
  137.7 0.0 copy-done.4
  137.7 0.2 select_reduce_fusion
  137.8 0.7 compare_select_fusion.9.index_ref
  138.5 2.0 convolution_convert_fusion
  140.5 40.8 %all-gather = bf16[128,1024]{1,0:T(8,128)(2,1)S(1)} all-gather(bf16[8,1024]{1,0:T(8,128)(2,1)S(1)} %convolution_convert_fusion), channel_id=2, replica_groups=mesh['z'=16,'x'=4,'c'=2,'mp'=4] {'z'}, dimensions={0}, use_global_device_ids=true | all-gather | bytes 278528 | tf_op jit(solution)/shard_map/all_gather | solution.py:360
  181.2 0.0 all-to-all-done.3.src_ref
  181.2 1.6 shard_map.61
  182.8 20.2 %all-to-all-start.4 = ((bf16[128,16,128]{2,1,0:T(8,128)(2,1)}), bf16[128,16,128]{2,1,0:T(8,128)(2,1)S(1)}, u32[]{:S(2)}, u32[]{:S(2)}) async-start(bf16[128,16,128]{2,1,0:T(8,128)(2,1)} %shard_map.61), calls=%async_computation.4 | async-start | bytes 1048576 | tf_op jit(solution)/shard_map/all_to_all | solution.py:300
  203.0 3.3 %collective-permute-start.6 = (bf16[16,8,1024]{2,1,0:T(8,128)(2,1)S(1)}, bf16[16,8,1024]{2,1,0:T(8,128)(2,1)S(1)}, u32[]{:S(2)}, u32[]{:S(2)}) collective-permute-start(bf16[16,8,1024]{2,1,0:T(8,128)(2,1)S(1)} %bitcast.73), channel_id=1, source_target_pairs={{24,0},{0,8},{8,16},{16,24},{25,1},{1,9},{9,17},{17,25},{26,2},{2,... | collective-permute-start | bytes 786440 | tf_op jit(solution)/shard_map/ppermute | solution.py:305
  206.3 4.3 %collective-permute-start.5 = (bf16[16,8,1024]{2,1,0:T(8,128)(2,1)S(1)}, bf16[16,8,1024]{2,1,0:T(8,128)(2,1)S(1)}, u32[]{:S(2)}, u32[]{:S(2)}) collective-permute-start(bf16[16,8,1024]{2,1,0:T(8,128)(2,1)S(1)} %bitcast.74), channel_id=1, source_target_pairs={{16,0},{24,8},{0,16},{8,24},{17,1},{25,9},{1,17},{9,25},{18,2},{26... | collective-permute-start | bytes 786440 | tf_op jit(solution)/shard_map/ppermute | solution.py:305
  210.6 3.1 %collective-permute-start.4 = (bf16[16,8,1024]{2,1,0:T(8,128)(2,1)S(1)}, bf16[16,8,1024]{2,1,0:T(8,128)(2,1)S(1)}, u32[]{:S(2)}, u32[]{:S(2)}) collective-permute-start(bf16[16,8,1024]{2,1,0:T(8,128)(2,1)S(1)} %bitcast.75), channel_id=1, source_target_pairs={{8,0},{16,8},{24,16},{0,24},{9,1},{17,9},{25,17},{1,25},{10,2},{18... | collective-permute-start | bytes 786440 | tf_op jit(solution)/shard_map/ppermute | solution.py:305
  213.7 0.1 collective-permute-done.6
  213.8 9.9 %collective-permute-done.5 = bf16[16,8,1024]{2,1,0:T(8,128)(2,1)S(1)} collective-permute-done((bf16[16,8,1024]{2,1,0:T(8,128)(2,1)S(1)}, bf16[16,8,1024]{2,1,0:T(8,128)(2,1)S(1)}, u32[]{:S(2)}, u32[]{:S(2)}) %collective-permute-start.5) | collective-permute-done | bytes 262176 | tf_op jit(solution)/shard_map/ppermute | solution.py:305
  223.7 1.5 collective-permute-done.4
  225.2 0.2 fusion.17
  225.4 3.1 %collective-permute-start.7 = (bf16[4,16,8,1024]{3,2,1,0:T(8,128)(2,1)S(1)}, bf16[4,16,8,1024]{3,2,1,0:T(8,128)(2,1)S(1)}, u32[]{:S(2)}, u32[]{:S(2)}) collective-permute-start(bf16[4,16,8,1024]{3,2,1,0:T(8,128)(2,1)S(1)} %get-tuple-element.37), channel_id=1, source_target_pairs={{4,0},{0,4},{5,1},{1,5},{6,2},{2,6},{7,3},{3,7},{12,8},{8,12},{13,... | collective-permute-start | bytes 3145736 | tf_op jit(solution)/shard_map/ppermute | solution.py:305
  228.6 0.2 select_reduce_fusion.1
  228.8 2.0 collective-permute-done.7
  230.8 0.2 pad_maximum_fusion
  231.0 1.6 gather_fusion.2
  232.6 1.3 all-to-all-done.4
  233.8 0.1 copy.12
  234.0 1.0 reshape.303
  (8 shorter events, 0.1 us)
Async XLA Ops:
  0.6 19.5 %copy-start = (bf16[1,56,8,1024]{3,2,1,0:T(8,128)(2,1)S(1)}, bf16[1,56,8,1024]{3,2,1,0:T(8,128)(2,1)}, u32[]{:S(2)}) copy-start(bf16[1,56,8,1024]{3,2,1,0:T(8,128)(2,1)} %param.5) | copy-start | bytes 2752516
  0.6 1.3 copy-start.1
  2.7 17.3 %all-to-all-start = ((f32[32,1,128]{2,1,0:T(1,128)}), f32[32,1,128]{2,1,0:T(1,128)S(1)}, u32[]{:S(2)}, u32[]{:S(2)}) async-start(f32[32,1,128]{2,1,0:T(1,128)} %get-tuple-element.17), calls=%async_computation | async-start | bytes 32768 | tf_op jit(solution)/shard_map/all_to_all | solution.py:300
  21.7 25.3 %collective-permute-start = (bf16[64,8,1024]{2,1,0:T(8,128)(2,1)}, bf16[64,8,1024]{2,1,0:T(8,128)(2,1)}, u32[]{:S(2)}, u32[]{:S(2)}) collective-permute-start(bf16[64,8,1024]{2,1,0:T(8,128)(2,1)} %gather_fusion.1), channel_id=1, source_target_pairs={{4,0},{0,4},{5,1},{1,5},{6,2},{2,6},{7,3},{3,7},{12,8},{8,12},{13,... | collective-permute-start | bytes 3145736 | tf_op jit(solution)/shard_map/ppermute | solution.py:305
  24.3 39.1 %collective-permute-start.2 = (f32[256,512]{1,0:T(8,128)S(1)}, f32[256,512]{1,0:T(8,128)}, u32[]{:S(2)}, u32[]{:S(2)}) collective-permute-start(f32[256,512]{1,0:T(8,128)S(1)} %get-tuple-element.23), channel_id=1, source_target_pairs={{2,0},{3,1},{0,2},{1,3},{6,4},{7,5},{4,6},{5,7},{10,8},{11,9},{8,1... | collective-permute-start | bytes 1572872 | tf_op jit(solution)/shard_map/ppermute | solution.py:305
  27.2 36.2 %collective-permute-start.1 = (f32[256,512]{1,0:T(8,128)S(1)}, f32[256,512]{1,0:T(8,128)}, u32[]{:S(2)}, u32[]{:S(2)}) collective-permute-start(f32[256,512]{1,0:T(8,128)S(1)} %get-tuple-element.23), channel_id=1, source_target_pairs={{1,0},{2,1},{3,2},{0,3},{5,4},{6,5},{7,6},{4,7},{9,8},{10,9},{11,1... | collective-permute-start | bytes 1572872 | tf_op jit(solution)/shard_map/ppermute | solution.py:305
  31.4 24.3 %all-to-all-start.1 = ((f32[16,1,128]{2,1,0:T(1,128)}), f32[16,1,128]{2,1,0:T(1,128)S(1)}, u32[]{:S(2)}, u32[]{:S(2)}) async-start(f32[16,1,128]{2,1,0:T(1,128)} %broadcast_in_dim.72), calls=%async_computation.1 | async-start | bytes 16384 | tf_op jit(solution)/shard_map/all_to_all | solution.py:300
  44.5 18.9 %collective-permute-start.3 = (f32[256,512]{1,0:T(8,128)S(1)}, f32[256,512]{1,0:T(8,128)}, u32[]{:S(2)}, u32[]{:S(2)}) collective-permute-start(f32[256,512]{1,0:T(8,128)S(1)} %get-tuple-element.24), channel_id=1, source_target_pairs={{3,0},{0,1},{1,2},{2,3},{7,4},{4,5},{5,6},{6,7},{11,8},{8,9},{9,10... | collective-permute-start | bytes 1572872 | tf_op jit(solution)/shard_map/ppermute | solution.py:305
  47.0 15.7 %copy-start.3 = (s32[128,1]{0,1:T(1,128)S(1)}, s32[128,1]{0,1:T(1,128)}, u32[]{:S(2)}) copy-start(s32[128,1]{0,1:T(1,128)} %param.6) | copy-start | bytes 1540
  55.7 7.7 %copy-start.2 = (f32[16,1,128]{2,1,0:T(1,128)}, f32[16,1,128]{2,1,0:T(1,128)S(1)}, u32[]{:S(2)}) copy-start(f32[16,1,128]{2,1,0:T(1,128)S(1)} %all-to-all-done.1) | copy-start | bytes 24580
  55.7 57.8 %all-to-all-start.2 = ((bf16[64,8,1024]{2,1,0:T(8,128)(2,1)}), bf16[64,8,1024]{2,1,0:T(8,128)(2,1)S(1)}, u32[]{:S(2)}, u32[]{:S(2)}) async-start(bf16[64,8,1024]{2,1,0:T(8,128)(2,1)} %add_convert_fusion), calls=%async_computation.2 | async-start | bytes 2097152 | tf_op jit(solution)/shard_map/all_to_all | solution.py:300
  66.6 71.1 %copy-start.4 = (s32[128,1]{0,1:T(1,128)S(1)}, s32[128,1]{0,1:T(1,128)}, u32[]{:S(2)}) copy-start(s32[128,1]{0,1:T(1,128)} %param.7) | copy-start | bytes 1540
  113.7 67.5 %all-to-all-start.3 = ((bf16[128,16,128]{2,1,0:T(8,128)(2,1)}), bf16[128,16,128]{2,1,0:T(8,128)(2,1)S(1)}, u32[]{:S(2)}, u32[]{:S(2)}) async-start(bf16[128,16,128]{2,1,0:T(8,128)(2,1)} %get-tuple-element.27), calls=%async_computation.3 | async-start | bytes 1048576 | tf_op jit(solution)/shard_map/all_to_all | solution.py:300
  182.8 51.0 %all-to-all-start.4 = ((bf16[128,16,128]{2,1,0:T(8,128)(2,1)}), bf16[128,16,128]{2,1,0:T(8,128)(2,1)S(1)}, u32[]{:S(2)}, u32[]{:S(2)}) async-start(bf16[128,16,128]{2,1,0:T(8,128)(2,1)} %shard_map.61), calls=%async_computation.4 | async-start | bytes 1048576 | tf_op jit(solution)/shard_map/all_to_all | solution.py:300
  203.0 10.8 %collective-permute-start.6 = (bf16[16,8,1024]{2,1,0:T(8,128)(2,1)S(1)}, bf16[16,8,1024]{2,1,0:T(8,128)(2,1)S(1)}, u32[]{:S(2)}, u32[]{:S(2)}) collective-permute-start(bf16[16,8,1024]{2,1,0:T(8,128)(2,1)S(1)} %bitcast.73), channel_id=1, source_target_pairs={{24,0},{0,8},{8,16},{16,24},{25,1},{1,9},{9,17},{17,25},{26,2},{2,... | collective-permute-start | bytes 786440 | tf_op jit(solution)/shard_map/ppermute | solution.py:305
  206.3 17.4 %collective-permute-start.5 = (bf16[16,8,1024]{2,1,0:T(8,128)(2,1)S(1)}, bf16[16,8,1024]{2,1,0:T(8,128)(2,1)S(1)}, u32[]{:S(2)}, u32[]{:S(2)}) collective-permute-start(bf16[16,8,1024]{2,1,0:T(8,128)(2,1)S(1)} %bitcast.74), channel_id=1, source_target_pairs={{16,0},{24,8},{0,16},{8,24},{17,1},{25,9},{1,17},{9,25},{18,2},{26... | collective-permute-start | bytes 786440 | tf_op jit(solution)/shard_map/ppermute | solution.py:305
  210.6 14.6 %collective-permute-start.4 = (bf16[16,8,1024]{2,1,0:T(8,128)(2,1)S(1)}, bf16[16,8,1024]{2,1,0:T(8,128)(2,1)S(1)}, u32[]{:S(2)}, u32[]{:S(2)}) collective-permute-start(bf16[16,8,1024]{2,1,0:T(8,128)(2,1)S(1)} %bitcast.75), channel_id=1, source_target_pairs={{8,0},{16,8},{24,16},{0,24},{9,1},{17,9},{25,17},{1,25},{10,2},{18... | collective-permute-start | bytes 786440 | tf_op jit(solution)/shard_map/ppermute | solution.py:305
  225.4 5.4 %collective-permute-start.7 = (bf16[4,16,8,1024]{3,2,1,0:T(8,128)(2,1)S(1)}, bf16[4,16,8,1024]{3,2,1,0:T(8,128)(2,1)S(1)}, u32[]{:S(2)}, u32[]{:S(2)}) collective-permute-start(bf16[4,16,8,1024]{3,2,1,0:T(8,128)(2,1)S(1)} %get-tuple-element.37), channel_id=1, source_target_pairs={{4,0},{0,4},{5,1},{1,5},{6,2},{2,6},{7,3},{3,7},{12,8},{8,12},{13,... | collective-permute-start | bytes 3145736 | tf_op jit(solution)/shard_map/ppermute | solution.py:305

commit v10 on v8

--- a/solution.py
+++ b/solution.py
@@ -327,7 +327,8 @@
     plane_bin = jnp.where(plane >= 0, plane_bin, -1)
     lane_ids = lax.broadcasted_iota(jnp.int32, (1, 1, LANES), 2)
     binned = jnp.sum(jnp.where(lane_ids == plane_bin[:, None, None], trace, 0.0), axis=(0, 1))
-    binned, near, far, tiles = lax.optimization_barrier((binned, near, far, gradients[0]))
+    binned, near, far = lax.optimization_barrier((binned, near, far))
+    tiles = gradients[0]
     binned = jnp.broadcast_to(binned[None, None], (z_count, 1, LANES))
     traces = exchange(binned, "z").reshape(z_count, LANES)
 

time: 232 us -> 233 us (level)
  waiting for transfers between devices: 24.9 us -> 74.2 us
  Pallas kernels: 54.2 us -> 5.3 us
  starting transfers between devices: 90.9 us -> 93.4 us
    all_to_all x5, waiting for transfers between devices: 11.4 us -> 60.7 us  [exchange(): return lax.all_to_all(pieces, axes, split_axis=0, concat_axis=0, tiled=True)]
    pallas_call x1, Pallas kernels: 51.9 us -> 2.99 us  [invert(): pl.pallas_call(invert_kernel, out_shape=(jax.ShapeDtypeStruct(pieces, jnp...]
    ppermute x8, starting transfers between devices: 24.8 us -> 31 us  [from_ahead(): lax.ppermute(value, axis, [((i + step) % count, i) for i in range(count)])]
    all_to_all x5, starting transfers between devices: 66.1 us -> 62.4 us  [exchange(): return lax.all_to_all(pieces, axes, split_axis=0, concat_axis=0, tiled=True)]
  transfers between devices with their start and end apart: 13 -> 13, of which waited for: 7 -> 8; matrix products, arithmetic and copies ran while one was open for 6% -> 4% of each run, Pallas kernels for 23% -> 2%
where the time goes in v10:
time: 233 us; the launch traced here: 230 us
  starting transfers between devices  93.4 us (40%)
  waiting for transfers between devices  74.2 us (32%)
  blocking collectives  40.8 us (18%)
  other arithmetic  7.41 us (3%)
  local copies, waits for them, and re-layouts  6 us (3%)
  Pallas kernels  5.3 us (2%)
    all_to_all x5, starting transfers between devices, exchange(): return lax.all_to_all(pieces, axes, split_axis=0, concat_axis=0, tiled=True)  62.4 us
    all_to_all x5, waiting for transfers between devices, exchange(): return lax.all_to_all(pieces, axes, split_axis=0, concat_axis=0, tiled=True)  60.7 us
    all_gather x1, blocking collectives, local(): held = lax.all_gather(held, 'z', axis=0, tiled=False)  40.8 us
    ppermute x8, starting transfers between devices, from_ahead(): lax.ppermute(value, axis, [((i + step) % count, i) for i in range(count)])  31 us
    ppermute x8, waiting for transfers between devices, from_ahead(): lax.ppermute(value, axis, [((i + step) % count, i) for i in range(count)])  13.5 us
  transfers between devices with their start and end apart: 13, of which 8 were waited for; matrix products, arithmetic and copies ran while one was open for 4% of the time, Pallas kernels for 2%

profile of v10, /device:TPU:1, one launch (start us, length us, event | category | flops | bytes accessed | tf_op | source)
XLA Modules:
  0.0 230.0 jit_solution(5689279122817667692)
XLA Ops:
  0.6 0.0 copy-start
  0.6 0.0 copy-start.3
  0.7 0.0 copy-start.1
  0.7 0.8 compare_reduce_fusion
  1.5 0.7 remainder_reduce_fusion
  2.2 0.1 ne.174
  2.3 0.1 rem.118
  2.5 0.1 div.50
  2.6 0.2 fusion.3
  2.8 0.0 copy-done
  2.8 1.6 gather_fusion.1
  4.4 8.8 %collective-permute-start = (bf16[64,8,1024]{2,1,0:T(8,128)(2,1)}, bf16[64,8,1024]{2,1,0:T(8,128)(2,1)}, u32[]{:S(2)}, u32[]{:S(2)}) collective-permute-start(bf16[64,8,1024]{2,1,0:T(8,128)(2,1)} %gather_fusion.1), channel_id=1, source_target_pairs={{4,0},{0,4},{5,1},{1,5},{6,2},{2,6},{7,3},{3,7},{12,8},{8,12},{13,... | collective-permute-start | bytes 3145736 | tf_op jit(solution)/shard_map/ppermute | solution.py:305
  13.2 0.0 copy-done.1
  13.2 0.8 shard_map.59
  14.0 3.6 %all-to-all-start = ((f32[32,1,128]{2,1,0:T(1,128)}), f32[32,1,128]{2,1,0:T(1,128)S(1)}, u32[]{:S(2)}, u32[]{:S(2)}) async-start(f32[32,1,128]{2,1,0:T(1,128)} %get-tuple-element.16), calls=%async_computation | async-start | bytes 32768 | tf_op jit(solution)/shard_map/all_to_all | solution.py:300
  17.6 0.0 copy-done.3
  17.6 0.1 bitcast_select_fusion
  17.7 0.1 iota_compare_fusion
  17.8 0.6 gather_fusion
  18.4 6.0 %all-to-all-done = f32[32,1,128]{2,1,0:T(1,128)S(1)} async-done(((f32[32,1,128]{2,1,0:T(1,128)}), f32[32,1,128]{2,1,0:T(1,128)S(1)}, u32[]{:S(2)}, u32[]{:S(2)}) %all-to-all-start) | async-done | bytes 16416 | tf_op jit(solution)/shard_map/all_to_all | solution.py:300
  24.5 0.1 fusion.5
  24.5 2.7 %collective-permute-start.2 = (f32[256,512]{1,0:T(8,128)S(1)}, f32[256,512]{1,0:T(8,128)}, u32[]{:S(2)}, u32[]{:S(2)}) collective-permute-start(f32[256,512]{1,0:T(8,128)S(1)} %get-tuple-element.21), channel_id=1, source_target_pairs={{2,0},{3,1},{0,2},{1,3},{6,4},{7,5},{4,6},{5,7},{10,8},{11,9},{8,1... | collective-permute-start | bytes 1572872 | tf_op jit(solution)/shard_map/ppermute | solution.py:305
  27.3 3.8 %collective-permute-start.1 = (f32[256,512]{1,0:T(8,128)S(1)}, f32[256,512]{1,0:T(8,128)}, u32[]{:S(2)}, u32[]{:S(2)}) collective-permute-start(f32[256,512]{1,0:T(8,128)S(1)} %get-tuple-element.21), channel_id=1, source_target_pairs={{1,0},{2,1},{3,2},{0,3},{5,4},{6,5},{7,6},{4,7},{9,8},{10,9},{11,1... | collective-permute-start | bytes 1572872 | tf_op jit(solution)/shard_map/ppermute | solution.py:305
  31.0 0.6 broadcast_in_dim.72
  31.6 13.1 %all-to-all-start.1 = ((f32[16,1,128]{2,1,0:T(1,128)}), f32[16,1,128]{2,1,0:T(1,128)S(1)}, u32[]{:S(2)}, u32[]{:S(2)}) async-start(f32[16,1,128]{2,1,0:T(1,128)} %broadcast_in_dim.72), calls=%async_computation.1 | async-start | bytes 16384 | tf_op jit(solution)/shard_map/all_to_all | solution.py:300
  44.8 1.9 collective-permute-start.3
  46.7 0.0 collective-permute-done
  46.7 2.6 %add_convert_fusion = bf16[64,8,1024]{2,1,0:T(8,128)(2,1)} fusion(bf16[64,8,1024]{2,1,0:T(8,128)(2,1)} %collective-permute-done, bf16[64,8,1024]{2,1,0:T(8,128)(2,1)S(1)} %gather_fusion), kind=kLoop, calls=%fused_computation.4 | loop fusion | flops 2097152 | bytes 3145728 | tf_op jit(solution)/shard_map/convert_element_type | solution.py:348
  49.3 6.7 %all-to-all-done.1 = f32[16,1,128]{2,1,0:T(1,128)S(1)} async-done(((f32[16,1,128]{2,1,0:T(1,128)}), f32[16,1,128]{2,1,0:T(1,128)S(1)}, u32[]{:S(2)}, u32[]{:S(2)}) %all-to-all-start.1) | async-done | bytes 8224 | tf_op jit(solution)/shard_map/all_to_all | solution.py:300
  56.0 6.4 %all-to-all-start.2 = ((bf16[64,8,1024]{2,1,0:T(8,128)(2,1)}), bf16[64,8,1024]{2,1,0:T(8,128)(2,1)S(1)}, u32[]{:S(2)}, u32[]{:S(2)}) async-start(bf16[64,8,1024]{2,1,0:T(8,128)(2,1)} %add_convert_fusion), calls=%async_computation.2 | async-start | bytes 2097152 | tf_op jit(solution)/shard_map/all_to_all | solution.py:300
  62.4 0.6 pad_add_fusion.slots_ref
  63.0 0.0 collective-permute-done.3.three_hbm
  63.0 0.0 collective-permute-done.2.two_hbm
  63.0 0.0 collective-permute-done.1.one_hbm
  63.0 0.0 copy-done.2
  63.0 3.0 %shard_map.60 = (bf16[128,16,128]{2,1,0:T(8,128)(2,1)}, bf16[1024,1024]{1,0:T(8,128)(2,1)}) custom-call(s32[130]{0:T(256)} %pad_add_fusion.slots_ref, f32[16,128]{1,0:T(8,128)} %bitcast.82, f32[256,1024]{1,0:T(8,128)} %bitcast.69, f32[256,512]{1,0:T(8,128)} %collective-permute-done.1.one_hbm, f32[256,512]{1,0:T(8,128)} %collective-permute-done.2.two_hbm, ...), custom_call_target="tpu_custom_call" | custom-call | flops 38654705664 | bytes 6291456 | tf_op jit(solution)/shard_map/pallas_call | solution.py:213
  66.0 0.0 copy-start.4
  66.1 46.7 %all-to-all-done.2 = bf16[64,8,1024]{2,1,0:T(8,128)(2,1)S(1)} async-done(((bf16[64,8,1024]{2,1,0:T(8,128)(2,1)}), bf16[64,8,1024]{2,1,0:T(8,128)(2,1)S(1)}, u32[]{:S(2)}, u32[]{:S(2)}) %all-to-all-start.2) | async-done | bytes 1048608 | tf_op jit(solution)/shard_map/all_to_all | solution.py:300
  112.8 0.2 reduce_sum.43
  113.0 19.3 %all-to-all-start.3 = ((bf16[128,16,128]{2,1,0:T(8,128)(2,1)}), bf16[128,16,128]{2,1,0:T(8,128)(2,1)S(1)}, u32[]{:S(2)}, u32[]{:S(2)}) async-start(bf16[128,16,128]{2,1,0:T(8,128)(2,1)} %get-tuple-element.25), calls=%async_computation.3 | async-start | bytes 1048576 | tf_op jit(solution)/shard_map/all_to_all | solution.py:300
  132.2 0.6 fusion.10
  132.9 0.0 copy-done.4
  132.9 0.2 select_reduce_fusion
  133.1 0.7 compare_select_fusion.9.index_ref
  133.7 2.0 convolution_convert_fusion
  135.7 40.8 %all-gather = bf16[128,1024]{1,0:T(8,128)(2,1)S(1)} all-gather(bf16[8,1024]{1,0:T(8,128)(2,1)S(1)} %convolution_convert_fusion), channel_id=2, replica_groups=mesh['z'=16,'x'=4,'c'=2,'mp'=4] {'z'}, dimensions={0}, use_global_device_ids=true | all-gather | bytes 278528 | tf_op jit(solution)/shard_map/all_gather | solution.py:361
  176.5 0.0 all-to-all-done.3.src_ref
  176.5 1.6 shard_map.61
  178.0 20.0 %all-to-all-start.4 = ((bf16[128,16,128]{2,1,0:T(8,128)(2,1)}), bf16[128,16,128]{2,1,0:T(8,128)(2,1)S(1)}, u32[]{:S(2)}, u32[]{:S(2)}) async-start(bf16[128,16,128]{2,1,0:T(8,128)(2,1)} %shard_map.61), calls=%async_computation.4 | async-start | bytes 1048576 | tf_op jit(solution)/shard_map/all_to_all | solution.py:300
  198.0 3.3 %collective-permute-start.6 = (bf16[16,8,1024]{2,1,0:T(8,128)(2,1)S(1)}, bf16[16,8,1024]{2,1,0:T(8,128)(2,1)S(1)}, u32[]{:S(2)}, u32[]{:S(2)}) collective-permute-start(bf16[16,8,1024]{2,1,0:T(8,128)(2,1)S(1)} %bitcast.73), channel_id=1, source_target_pairs={{24,0},{0,8},{8,16},{16,24},{25,1},{1,9},{9,17},{17,25},{26,2},{2,... | collective-permute-start | bytes 786440 | tf_op jit(solution)/shard_map/ppermute | solution.py:305
  201.3 4.3 %collective-permute-start.5 = (bf16[16,8,1024]{2,1,0:T(8,128)(2,1)S(1)}, bf16[16,8,1024]{2,1,0:T(8,128)(2,1)S(1)}, u32[]{:S(2)}, u32[]{:S(2)}) collective-permute-start(bf16[16,8,1024]{2,1,0:T(8,128)(2,1)S(1)} %bitcast.74), channel_id=1, source_target_pairs={{16,0},{24,8},{0,16},{8,24},{17,1},{25,9},{1,17},{9,25},{18,2},{26... | collective-permute-start | bytes 786440 | tf_op jit(solution)/shard_map/ppermute | solution.py:305
  205.6 3.1 %collective-permute-start.4 = (bf16[16,8,1024]{2,1,0:T(8,128)(2,1)S(1)}, bf16[16,8,1024]{2,1,0:T(8,128)(2,1)S(1)}, u32[]{:S(2)}, u32[]{:S(2)}) collective-permute-start(bf16[16,8,1024]{2,1,0:T(8,128)(2,1)S(1)} %bitcast.75), channel_id=1, source_target_pairs={{8,0},{16,8},{24,16},{0,24},{9,1},{17,9},{25,17},{1,25},{10,2},{18... | collective-permute-start | bytes 786440 | tf_op jit(solution)/shard_map/ppermute | solution.py:305
  208.7 0.1 collective-permute-done.6
  208.8 9.9 %collective-permute-done.5 = bf16[16,8,1024]{2,1,0:T(8,128)(2,1)S(1)} collective-permute-done((bf16[16,8,1024]{2,1,0:T(8,128)(2,1)S(1)}, bf16[16,8,1024]{2,1,0:T(8,128)(2,1)S(1)}, u32[]{:S(2)}, u32[]{:S(2)}) %collective-permute-start.5) | collective-permute-done | bytes 262176 | tf_op jit(solution)/shard_map/ppermute | solution.py:305
  218.7 1.5 collective-permute-done.4
  220.2 0.2 fusion.17
  220.4 3.1 %collective-permute-start.7 = (bf16[4,16,8,1024]{3,2,1,0:T(8,128)(2,1)S(1)}, bf16[4,16,8,1024]{3,2,1,0:T(8,128)(2,1)S(1)}, u32[]{:S(2)}, u32[]{:S(2)}) collective-permute-start(bf16[4,16,8,1024]{3,2,1,0:T(8,128)(2,1)S(1)} %get-tuple-element.35), channel_id=1, source_target_pairs={{4,0},{0,4},{5,1},{1,5},{6,2},{2,6},{7,3},{3,7},{12,8},{8,12},{13,... | collective-permute-start | bytes 3145736 | tf_op jit(solution)/shard_map/ppermute | solution.py:305
  223.6 0.2 select_reduce_fusion.1
  223.8 2.0 collective-permute-done.7
  225.8 0.2 pad_maximum_fusion
  226.0 1.6 gather_fusion.2
  227.6 1.3 all-to-all-done.4
  228.8 0.1 copy.12
  229.0 1.0 reshape.303
  (8 shorter events, 0.1 us)
Async XLA Ops:
  0.6 2.2 copy-start
  0.6 17.0 %copy-start.3 = (s32[128,1]{0,1:T(1,128)S(1)}, s32[128,1]{0,1:T(1,128)}, u32[]{:S(2)}) copy-start(s32[128,1]{0,1:T(1,128)} %param.6) | copy-start | bytes 1540
  0.7 12.6 %copy-start.1 = (f32[1,1,256,1024]{3,2,1,0:T(8,128)S(1)}, f32[1,1,256,1024]{3,2,1,0:T(8,128)}, u32[]{:S(2)}) copy-start(f32[1,1,256,1024]{3,2,1,0:T(8,128)} %param.4) | copy-start | bytes 3145732
  4.4 42.3 %collective-permute-start = (bf16[64,8,1024]{2,1,0:T(8,128)(2,1)}, bf16[64,8,1024]{2,1,0:T(8,128)(2,1)}, u32[]{:S(2)}, u32[]{:S(2)}) collective-permute-start(bf16[64,8,1024]{2,1,0:T(8,128)(2,1)} %gather_fusion.1), channel_id=1, source_target_pairs={{4,0},{0,4},{5,1},{1,5},{6,2},{2,6},{7,3},{3,7},{12,8},{8,12},{13,... | collective-permute-start | bytes 3145736 | tf_op jit(solution)/shard_map/ppermute | solution.py:305
  14.0 10.5 %all-to-all-start = ((f32[32,1,128]{2,1,0:T(1,128)}), f32[32,1,128]{2,1,0:T(1,128)S(1)}, u32[]{:S(2)}, u32[]{:S(2)}) async-start(f32[32,1,128]{2,1,0:T(1,128)} %get-tuple-element.16), calls=%async_computation | async-start | bytes 32768 | tf_op jit(solution)/shard_map/all_to_all | solution.py:300
  24.5 38.5 %collective-permute-start.2 = (f32[256,512]{1,0:T(8,128)S(1)}, f32[256,512]{1,0:T(8,128)}, u32[]{:S(2)}, u32[]{:S(2)}) collective-permute-start(f32[256,512]{1,0:T(8,128)S(1)} %get-tuple-element.21), channel_id=1, source_target_pairs={{2,0},{3,1},{0,2},{1,3},{6,4},{7,5},{4,6},{5,7},{10,8},{11,9},{8,1... | collective-permute-start | bytes 1572872 | tf_op jit(solution)/shard_map/ppermute | solution.py:305
  27.3 35.8 %collective-permute-start.1 = (f32[256,512]{1,0:T(8,128)S(1)}, f32[256,512]{1,0:T(8,128)}, u32[]{:S(2)}, u32[]{:S(2)}) collective-permute-start(f32[256,512]{1,0:T(8,128)S(1)} %get-tuple-element.21), channel_id=1, source_target_pairs={{1,0},{2,1},{3,2},{0,3},{5,4},{6,5},{7,6},{4,7},{9,8},{10,9},{11,1... | collective-permute-start | bytes 1572872 | tf_op jit(solution)/shard_map/ppermute | solution.py:305
  31.6 24.4 %all-to-all-start.1 = ((f32[16,1,128]{2,1,0:T(1,128)}), f32[16,1,128]{2,1,0:T(1,128)S(1)}, u32[]{:S(2)}, u32[]{:S(2)}) async-start(f32[16,1,128]{2,1,0:T(1,128)} %broadcast_in_dim.72), calls=%async_computation.1 | async-start | bytes 16384 | tf_op jit(solution)/shard_map/all_to_all | solution.py:300
  44.8 18.3 %collective-permute-start.3 = (f32[256,512]{1,0:T(8,128)S(1)}, f32[256,512]{1,0:T(8,128)}, u32[]{:S(2)}, u32[]{:S(2)}) collective-permute-start(f32[256,512]{1,0:T(8,128)S(1)} %get-tuple-element.22), channel_id=1, source_target_pairs={{3,0},{0,1},{1,2},{2,3},{7,4},{4,5},{5,6},{6,7},{11,8},{8,9},{9,10... | collective-permute-start | bytes 1572872 | tf_op jit(solution)/shard_map/ppermute | solution.py:305
  56.0 7.0 %copy-start.2 = (f32[16,1,128]{2,1,0:T(1,128)}, f32[16,1,128]{2,1,0:T(1,128)S(1)}, u32[]{:S(2)}) copy-start(f32[16,1,128]{2,1,0:T(1,128)S(1)} %all-to-all-done.1) | copy-start | bytes 24580
  56.0 56.8 %all-to-all-start.2 = ((bf16[64,8,1024]{2,1,0:T(8,128)(2,1)}), bf16[64,8,1024]{2,1,0:T(8,128)(2,1)S(1)}, u32[]{:S(2)}, u32[]{:S(2)}) async-start(bf16[64,8,1024]{2,1,0:T(8,128)(2,1)} %add_convert_fusion), calls=%async_computation.2 | async-start | bytes 2097152 | tf_op jit(solution)/shard_map/all_to_all | solution.py:300
  66.0 66.8 %copy-start.4 = (s32[128,1]{0,1:T(1,128)S(1)}, s32[128,1]{0,1:T(1,128)}, u32[]{:S(2)}) copy-start(s32[128,1]{0,1:T(1,128)} %param.7) | copy-start | bytes 1540
  113.0 63.5 %all-to-all-start.3 = ((bf16[128,16,128]{2,1,0:T(8,128)(2,1)}), bf16[128,16,128]{2,1,0:T(8,128)(2,1)S(1)}, u32[]{:S(2)}, u32[]{:S(2)}) async-start(bf16[128,16,128]{2,1,0:T(8,128)(2,1)} %get-tuple-element.25), calls=%async_computation.3 | async-start | bytes 1048576 | tf_op jit(solution)/shard_map/all_to_all | solution.py:300
  178.0 50.8 %all-to-all-start.4 = ((bf16[128,16,128]{2,1,0:T(8,128)(2,1)}), bf16[128,16,128]{2,1,0:T(8,128)(2,1)S(1)}, u32[]{:S(2)}, u32[]{:S(2)}) async-start(bf16[128,16,128]{2,1,0:T(8,128)(2,1)} %shard_map.61), calls=%async_computation.4 | async-start | bytes 1048576 | tf_op jit(solution)/shard_map/all_to_all | solution.py:300
  198.0 10.8 %collective-permute-start.6 = (bf16[16,8,1024]{2,1,0:T(8,128)(2,1)S(1)}, bf16[16,8,1024]{2,1,0:T(8,128)(2,1)S(1)}, u32[]{:S(2)}, u32[]{:S(2)}) collective-permute-start(bf16[16,8,1024]{2,1,0:T(8,128)(2,1)S(1)} %bitcast.73), channel_id=1, source_target_pairs={{24,0},{0,8},{8,16},{16,24},{25,1},{1,9},{9,17},{17,25},{26,2},{2,... | collective-permute-start | bytes 786440 | tf_op jit(solution)/shard_map/ppermute | solution.py:305
  201.3 17.4 %collective-permute-start.5 = (bf16[16,8,1024]{2,1,0:T(8,128)(2,1)S(1)}, bf16[16,8,1024]{2,1,0:T(8,128)(2,1)S(1)}, u32[]{:S(2)}, u32[]{:S(2)}) collective-permute-start(bf16[16,8,1024]{2,1,0:T(8,128)(2,1)S(1)} %bitcast.74), channel_id=1, source_target_pairs={{16,0},{24,8},{0,16},{8,24},{17,1},{25,9},{1,17},{9,25},{18,2},{26... | collective-permute-start | bytes 786440 | tf_op jit(solution)/shard_map/ppermute | solution.py:305
  205.6 14.6 %collective-permute-start.4 = (bf16[16,8,1024]{2,1,0:T(8,128)(2,1)S(1)}, bf16[16,8,1024]{2,1,0:T(8,128)(2,1)S(1)}, u32[]{:S(2)}, u32[]{:S(2)}) collective-permute-start(bf16[16,8,1024]{2,1,0:T(8,128)(2,1)S(1)} %bitcast.75), channel_id=1, source_target_pairs={{8,0},{16,8},{24,16},{0,24},{9,1},{17,9},{25,17},{1,25},{10,2},{18... | collective-permute-start | bytes 786440 | tf_op jit(solution)/shard_map/ppermute | solution.py:305
  220.4 5.4 %collective-permute-start.7 = (bf16[4,16,8,1024]{3,2,1,0:T(8,128)(2,1)S(1)}, bf16[4,16,8,1024]{3,2,1,0:T(8,128)(2,1)S(1)}, u32[]{:S(2)}, u32[]{:S(2)}) collective-permute-start(bf16[4,16,8,1024]{3,2,1,0:T(8,128)(2,1)S(1)} %get-tuple-element.35), channel_id=1, source_target_pairs={{4,0},{0,4},{5,1},{1,5},{6,2},{2,6},{7,3},{3,7},{12,8},{8,12},{13,... | collective-permute-start | bytes 3145736 | tf_op jit(solution)/shard_map/ppermute | solution.py:305
